TPU v7x, 1024 devices: a whole 8x8x8 slice. The times are simulated.
1024 devices in a mesh: expert: 16 (over y_lo, z), dp: 64 (over y_hi, x, core).
Axes of the slice: x: 8, y: 8 (y_hi: 4, y_lo: 2; y = y_hi * 2 + y_lo), z: 8, core: 2. Of those that a mesh axis runs over, the one named last changes fastest.
Arguments:
- tokens: bfloat16 [8192, 4096], P('dp'), may hold values from -6 to 6
- first_expert: int32 [8192], P('dp'), may hold values from 0 to 1, as said below
- first_slot: int32 [8192], P('dp'), may hold values from -1 to 3, as said below
- second_expert: int32 [8192], P('dp'), may hold values from 0 to 1, as said below
- second_slot: int32 [8192], P('dp'), may hold values from -1 to 1, as said below
- first_gate: float32 [8192], P('dp'), may hold values from 0.3 to 1
- second_gate: float32 [8192], P('dp'), may hold values from 0.3 to 1
- w_gate: bfloat16 [8192, 16384], P('expert', 'dp'), may hold values from -0.09375 to 0.09375
- w_up: bfloat16 [8192, 16384], P('expert', 'dp'), may hold values from -0.09375 to 0.09375
- w_down: bfloat16 [16384, 8192], P('dp', 'expert'), may hold values from -0.046875 to 0.046875
- norm_gain: float32 [4096], replicated, may hold values from 0.25 to 1.75
- w_query: bfloat16 [4096, 8192], P('dp', 'expert'), may hold values from -0.09375 to 0.09375
Outputs:
- mixed: bfloat16 [8192, 4096], P('dp')
- query: bfloat16 [8192, 8192], P('dp', 'expert')
Inputs may be any that keep to these rules, and one draw needn't show every extreme that they name: `first_expert`: in every dp row each expert is the first expert of exactly 64 tokens. `first_slot`: in every dp row and for every expert, the slots 0 to 3 are each taken by exactly one token of that expert; the rest of its tokens have -1. second_expert = 1 - first_expert for every token. `second_slot`: only tokens with first_slot = -1 have a second slot; in every dp row and for every expert, the slots 0 to 1 are each taken by exactly one token.
All inputs are finite; a program needn't handle non-finite values.
Results may differ from a plain program's by a relative error of at most 0.0051.
Values may be sent and summed in bfloat16 or wider, within the bound.
No kernel may reach another device: no remote copies, remote signals or barrier semaphores. Data moves between devices by JAX's collectives and lax.ppermute only.
A program may use at most 32 MiB of HBM per device.

v0:
```python
import jax
import jax.numpy as jnp
from jax import lax
from jax.sharding import PartitionSpec as P

CAP1 = 4
CAP2 = 2


def partner(block, axis, distance):
    count = lax.axis_size(axis)
    route = []
    for low in range(count):
        high = low | 1 << distance
        if high != low and high < count:
            route += [(low, high), (high, low)]
    return lax.ppermute(block, axis, route)


def local(
    tokens,
    first_expert,
    first_slot,
    second_expert,
    second_slot,
    first_gate,
    second_gate,
    w_gate,
    w_up,
    w_down,
    norm_gain,
    w_query,
):
    n_expert = lax.axis_size("expert")
    group_size = min(8, n_expert // 2)
    experts = n_expert // group_size
    tok_count, width = tokens.shape
    block_width = width // group_size
    hidden_units = w_gate.shape[1]
    position = lax.axis_index("expert")
    own_expert = position // group_size
    own_block = position % group_size
    token_block = lax.dynamic_slice_in_dim(tokens, own_block * block_width, block_width, 1)

    def expert_pass(routes, capacity):
        placement = jnp.full((tok_count,), -1, jnp.int32)
        for expert_ids, slot_ids, slot_offset in routes:
            matched = (expert_ids == own_expert) & (slot_ids >= 0)
            placement = jnp.where(matched, slot_ids + slot_offset, placement)
        slot_hot = (jnp.arange(capacity, dtype=jnp.int32)[:, None] == placement[None, :]).astype(
            jnp.bfloat16
        )
        slot_rows = jnp.dot(slot_hot, token_block, preferred_element_type=jnp.float32).astype(
            jnp.bfloat16
        )
        shard_piece = lax.all_gather(slot_rows, "dp", axis=0, tiled=True)
        gate_part = jnp.dot(shard_piece, w_gate, preferred_element_type=jnp.float32)
        up_part = jnp.dot(shard_piece, w_up, preferred_element_type=jnp.float32)
        partial_value = jnp.concatenate([gate_part, up_part], axis=1)
        for bit_number in range(group_size.bit_length() - 1):
            partial_value = partial_value + partner(
                partial_value.astype(jnp.bfloat16), "expert", bit_number
            ).astype(partial_value.dtype)
        hidden = (
            jax.nn.silu(partial_value[:, :hidden_units]) * partial_value[:, hidden_units:]
        ).astype(jnp.bfloat16)
        expert_out = lax.psum_scatter(
            jnp.dot(hidden, w_down, preferred_element_type=jnp.float32),
            "dp",
            scatter_dimension=0,
            tiled=True,
        ).astype(jnp.bfloat16)
        gathered = lax.all_gather(expert_out, "expert", axis=0, tiled=True)
        expert_table = jnp.transpose(
            gathered.reshape(experts, group_size, capacity, block_width), (0, 2, 1, 3)
        )
        return expert_table.reshape(experts * capacity, width)

    def pick_rows(expert_table, expert_ids, slot_ids, slot_offset, capacity):
        table_column = jnp.where(slot_ids >= 0, expert_ids * capacity + slot_ids + slot_offset, -1)
        pick_hot = (
            table_column[:, None] == jnp.arange(experts * capacity, dtype=jnp.int32)[None, :]
        ).astype(jnp.bfloat16)
        return jnp.dot(pick_hot, expert_table, preferred_element_type=jnp.float32)

    first_table = expert_pass(((first_expert, first_slot, 0),), CAP1)
    first_out = pick_rows(first_table, first_expert, first_slot, 0, CAP1)
    second_table = expert_pass(((second_expert, second_slot, 0),), CAP2)
    second_out = pick_rows(second_table, second_expert, second_slot, 0, CAP2)
    mixed_float = (
        tokens.astype(jnp.float32)
        + first_gate[:, None] * first_out
        + second_gate[:, None] * second_out
    )
    mixed = mixed_float.astype(jnp.bfloat16)
    values = mixed.astype(jnp.float32)
    scale = lax.rsqrt(jnp.mean(values * values, axis=-1, keepdims=True) + 1e-05)
    normed = (values * scale * norm_gain[None, :]).astype(jnp.bfloat16)
    query_float = jnp.dot(
        normed,
        lax.all_gather(w_query, "dp", axis=0, tiled=True),
        preferred_element_type=jnp.float32,
    )
    return (mixed, query_float.astype(jnp.bfloat16))


def solution(mesh):
    in_specs = (
        P("dp", None),
        P("dp"),
        P("dp"),
        P("dp"),
        P("dp"),
        P("dp"),
        P("dp"),
        P("expert", "dp"),
        P("expert", "dp"),
        P("dp", "expert"),
        P(),
        P("dp", "expert"),
    )
    out_specs = (P("dp", None), P("dp", "expert"))
    return jax.shard_map(local, mesh=mesh, in_specs=in_specs, out_specs=out_specs, check_vma=False)
```

profile of v0, /device:TPU:16, one launch (start us, length us, event | category | flops | bytes accessed | tf_op | source)
XLA Modules:
  0.0 594.3 jit_solution(4036163035203625832)
XLA Ops:
  7.2 0.0 copy-start
  7.2 0.0 copy-start.1
  7.2 0.0 copy-start.2
  7.2 0.0 copy-start.3
  7.2 0.0 all-gather.6.cloned.1.call-start
  7.3 0.7 all-gather.6.cloned.1.call-update
  8.0 0.7 compare_select_fusion
  8.7 1.0 fusion.7
  9.7 82.9 %all-gather.2 = bf16[64,2,512]{2,1,0:T(2,128)(2,1)S(1)} all-gather(bf16[1,2,512]{2,1,0:T(2,128)(2,1)S(1)} %fusion.7), channel_id=1, replica_groups=mesh['expert'=16,'dp'=64] {'dp'}, dimensions={0}, use_global_device_ids=true | all-gather | bytes 133120 | tf_op jit(solution)/shard_map/all_gather | solution.py:56
  92.6 0.1 reshape.40
  92.7 1.2 fusion.41
  93.8 1.1 fusion.42
  95.0 5.2 collective-permute-start.3
  100.3 0.1 fusion.6
  100.4 76.9 %all-gather = bf16[64,4,512]{2,1,0:T(4,128)(2,1)S(1)} all-gather(bf16[1,4,512]{2,1,0:T(4,128)(2,1)S(1)} %fusion.6), channel_id=1, replica_groups=mesh['expert'=16,'dp'=64] {'dp'}, dimensions={0}, use_global_device_ids=true | all-gather | bytes 266240 | tf_op jit(solution)/shard_map/all_gather | solution.py:56
  177.3 0.1 reshape.36
  177.4 0.3 fusion.39
  177.7 0.3 fusion.40
  178.0 2.2 collective-permute-start
  180.2 0.0 collective-permute-done.3
  180.2 7.8 %collective-permute-start.4 = (bf16[128,512]{1,0:T(8,128)(2,1)S(1)}, bf16[128,512]{1,0:T(8,128)(2,1)S(1)}, u32[]{:S(2)}, u32[]{:S(2)}) collective-permute-start(bf16[128,512]{1,0:T(8,128)(2,1)S(1)} %fusion.28), channel_id=1, source_target_pairs={{0,128},{128,0},{64,192},{192,64},{256,384},{384,256},{320,448},{4... | collective-permute-start | bytes 393224 | tf_op jit(solution)/shard_map/ppermute | solution.py:17
  188.1 0.4 collective-permute-done
  188.4 0.1 fusion.27
  188.5 8.4 %collective-permute-start.1 = (bf16[256,512]{0,1:T(8,128)(2,1)S(1)}, bf16[256,512]{0,1:T(8,128)(2,1)S(1)}, u32[]{:S(2)}, u32[]{:S(2)}) collective-permute-start(bf16[256,512]{0,1:T(8,128)(2,1)S(1)} %fusion.27), channel_id=1, source_target_pairs={{0,128},{128,0},{64,192},{192,64},{256,384},{384,256},{320,448},{4... | collective-permute-start | bytes 786440 | tf_op jit(solution)/shard_map/ppermute | solution.py:17
  196.9 1.3 dynamic-slice
  199.4 0.0 collective-permute-done.4
  199.5 12.2 %collective-permute-start.5 = (bf16[128,512]{1,0:T(8,128)(2,1)S(1)}, bf16[128,512]{1,0:T(8,128)(2,1)S(1)}, u32[]{:S(2)}, u32[]{:S(2)}) collective-permute-start(bf16[128,512]{1,0:T(8,128)(2,1)S(1)} %fusion.15), channel_id=1, source_target_pairs={{0,256},{256,0},{64,320},{320,64},{128,384},{384,128},{192,448},{4... | collective-permute-start | bytes 393224 | tf_op jit(solution)/shard_map/ppermute | solution.py:17
  211.7 0.0 collective-permute-done.1
  211.7 0.1 fusion.12
  211.8 13.9 %collective-permute-start.2 = (bf16[256,512]{0,1:T(8,128)(2,1)S(1)}, bf16[256,512]{0,1:T(8,128)(2,1)S(1)}, u32[]{:S(2)}, u32[]{:S(2)}) collective-permute-start(bf16[256,512]{0,1:T(8,128)(2,1)S(1)} %fusion.12), channel_id=1, source_target_pairs={{0,256},{256,0},{64,320},{320,64},{128,384},{384,128},{192,448},{4... | collective-permute-start | bytes 786440 | tf_op jit(solution)/shard_map/ppermute | solution.py:17
  225.8 0.0 collective-permute-done.5
  225.8 0.1 convert_add_fusion.3
  225.9 0.2 fusion.22
  226.1 0.0 copy-start.5
  226.1 11.8 %collective-permute-done.2 = bf16[256,512]{0,1:T(8,128)(2,1)S(1)} collective-permute-done((bf16[256,512]{0,1:T(8,128)(2,1)S(1)}, bf16[256,512]{0,1:T(8,128)(2,1)S(1)}, u32[]{:S(2)}, u32[]{:S(2)}) %collective-permute-start.2) | collective-permute-done | bytes 262176 | tf_op jit(solution)/shard_map/ppermute | solution.py:17
  237.9 0.1 convert_add_fusion
  238.0 0.3 fusion.16
  238.3 0.0 copy-start.6
  238.3 282.3 %all-reduce.4 = (bf16[256,512]{1,0:T(8,128)(2,1)S(1)}, bf16[128,512]{1,0:T(8,128)(2,1)S(1)}) all-reduce(f32[256,512]{1,0:T(8,128)S(1)} %fusion.16, f32[128,512]{1,0:T(8,128)S(1)} %fusion.22), channel_id=2, replica_groups=mesh['expert'=16,'dp'=64] {'dp'}, use_global_device_ids=true, to_apply=%region_0.1.clone | all-reduce | flops 196608 | bytes 1179648
  520.6 31.3 %all-gather.1 = bf16[16,4,512]{2,1,0:T(4,128)(2,1)S(1)} all-gather(bf16[1,4,512]{2,1,0:T(4,128)(2,1)S(1)} %fusion.29), channel_id=1, replica_groups=mesh['expert'=16,'dp'=64] {'expert'}, dimensions={0}, use_global_device_ids=true | all-gather | bytes 69632 | tf_op jit(solution)/shard_map/all_gather | solution.py:73
  552.0 30.2 %all-gather.3 = bf16[16,2,512]{2,1,0:T(2,128)(2,1)S(1)} all-gather(bf16[1,2,512]{2,1,0:T(2,128)(2,1)S(1)} %fusion.30), channel_id=1, replica_groups=mesh['expert'=16,'dp'=64] {'expert'}, dimensions={0}, use_global_device_ids=true | all-gather | bytes 34816 | tf_op jit(solution)/shard_map/all_gather | solution.py:73
  582.3 0.5 fusion.1
  582.8 0.0 copy-start.7
  582.8 0.6 fusion.3
  583.4 0.0 copy-start.4
  583.4 0.0 all-gather.6.cloned.1.call-done
  583.4 0.0 copy-done.7
  583.5 3.9 convolution_convert_fusion
  (18 shorter events, 0.2 us)
Async XLA Ops:
  7.2 218.7 %copy-start = (bf16[256,512]{1,0:T(8,128)(2,1)S(1)}, bf16[256,512]{1,0:T(8,128)(2,1)}, u32[]{:S(2)}) copy-start(bf16[256,512]{1,0:T(8,128)(2,1)} %param.21) | copy-start | bytes 786436
  7.2 93.1 %copy-start.1 = (bf16[128,4096]{1,0:T(8,128)(2,1)S(1)}, bf16[128,4096]{1,0:T(8,128)(2,1)}, u32[]{:S(2)}) copy-start(bf16[128,4096]{1,0:T(8,128)(2,1)} %param.12) | copy-start | bytes 3145732
  7.2 170.2 %copy-start.2 = (bf16[512,256]{1,0:T(8,128)(2,1)S(1)}, bf16[512,256]{1,0:T(8,128)(2,1)}, u32[]{:S(2)}) copy-start(bf16[512,256]{1,0:T(8,128)(2,1)} %param.19) | copy-start | bytes 786436
  7.2 170.5 %copy-start.3 = (bf16[512,256]{1,0:T(8,128)(2,1)S(1)}, bf16[512,256]{1,0:T(8,128)(2,1)}, u32[]{:S(2)}) copy-start(bf16[512,256]{1,0:T(8,128)(2,1)} %param.20) | copy-start | bytes 786436
  7.2 576.2 %all-gather.6.cloned.1.call-start = ((), (), s32[]{:S(2)}) async-start(), calls=%async_computation | async-start | bytes 4259840 | tf_op jit(solution)/shard_map/all_gather | solution.py:101
  95.0 85.2 %collective-permute-start.3 = (bf16[128,512]{1,0:T(8,128)(2,1)S(1)}, bf16[128,512]{1,0:T(8,128)(2,1)S(1)}, u32[]{:S(2)}, u32[]{:S(2)}) collective-permute-start(bf16[128,512]{1,0:T(8,128)(2,1)S(1)} %fusion.14), channel_id=1, source_target_pairs={{0,64},{64,0},{128,192},{192,128},{256,320},{320,256},{384,448},{4... | collective-permute-start | bytes 393224 | tf_op jit(solution)/shard_map/ppermute | solution.py:17
  178.0 10.4 %collective-permute-start = (bf16[256,512]{0,1:T(8,128)(2,1)S(1)}, bf16[256,512]{0,1:T(8,128)(2,1)S(1)}, u32[]{:S(2)}, u32[]{:S(2)}) collective-permute-start(bf16[256,512]{0,1:T(8,128)(2,1)S(1)} %fusion.11), channel_id=1, source_target_pairs={{0,64},{64,0},{128,192},{192,128},{256,320},{320,256},{384,448},{4... | collective-permute-start | bytes 786440 | tf_op jit(solution)/shard_map/ppermute | solution.py:17
  180.2 19.2 %collective-permute-start.4 = (bf16[128,512]{1,0:T(8,128)(2,1)S(1)}, bf16[128,512]{1,0:T(8,128)(2,1)S(1)}, u32[]{:S(2)}, u32[]{:S(2)}) collective-permute-start(bf16[128,512]{1,0:T(8,128)(2,1)S(1)} %fusion.28), channel_id=1, source_target_pairs={{0,128},{128,0},{64,192},{192,64},{256,384},{384,256},{320,448},{4... | collective-permute-start | bytes 393224 | tf_op jit(solution)/shard_map/ppermute | solution.py:17
  188.5 23.2 %collective-permute-start.1 = (bf16[256,512]{0,1:T(8,128)(2,1)S(1)}, bf16[256,512]{0,1:T(8,128)(2,1)S(1)}, u32[]{:S(2)}, u32[]{:S(2)}) collective-permute-start(bf16[256,512]{0,1:T(8,128)(2,1)S(1)} %fusion.27), channel_id=1, source_target_pairs={{0,128},{128,0},{64,192},{192,64},{256,384},{384,256},{320,448},{4... | collective-permute-start | bytes 786440 | tf_op jit(solution)/shard_map/ppermute | solution.py:17
  199.5 26.3 %collective-permute-start.5 = (bf16[128,512]{1,0:T(8,128)(2,1)S(1)}, bf16[128,512]{1,0:T(8,128)(2,1)S(1)}, u32[]{:S(2)}, u32[]{:S(2)}) collective-permute-start(bf16[128,512]{1,0:T(8,128)(2,1)S(1)} %fusion.15), channel_id=1, source_target_pairs={{0,256},{256,0},{64,320},{320,64},{128,384},{384,128},{192,448},{4... | collective-permute-start | bytes 393224 | tf_op jit(solution)/shard_map/ppermute | solution.py:17
  211.8 26.1 %collective-permute-start.2 = (bf16[256,512]{0,1:T(8,128)(2,1)S(1)}, bf16[256,512]{0,1:T(8,128)(2,1)S(1)}, u32[]{:S(2)}, u32[]{:S(2)}) collective-permute-start(bf16[256,512]{0,1:T(8,128)(2,1)S(1)} %fusion.12), channel_id=1, source_target_pairs={{0,256},{256,0},{64,320},{320,64},{128,384},{384,128},{192,448},{4... | collective-permute-start | bytes 786440 | tf_op jit(solution)/shard_map/ppermute | solution.py:17
  226.1 356.2 %copy-start.5 = (f32[128]{0:T(128)S(1)}, f32[128]{0:T(128)}, u32[]{:S(2)}) copy-start(f32[128]{0:T(128)} %param.17) | copy-start | bytes 1540
  238.3 344.4 %copy-start.6 = (f32[128]{0:T(128)S(1)}, f32[128]{0:T(128)}, u32[]{:S(2)}) copy-start(f32[128]{0:T(128)} %param.18) | copy-start | bytes 1540
  582.8 0.7 copy-start.7
  583.4 4.0 copy-start.4
Sparse Core Ops, SparseCore 0:
  12.6 104.4 all-gather.5
where the time goes:
time: 595 us; the launch traced here: 594 us
  blocking collectives  504 us (85%)
  starting transfers between devices  49.8 us (8%)
  between operations  15.7 us (3%)
  waiting for transfers between devices  12.9 us (2%)
  matrix products  9.52 us (2%)
    unnamed x1, blocking collectives  282 us
    all_gather x2, blocking collectives, expert_pass(): shard_piece = lax.all_gather(slot_rows, 'dp', axis=0, tiled=True)  160 us
    all_gather x2, blocking collectives, expert_pass(): gathered = lax.all_gather(expert_out, 'expert', axis=0, tiled=True)  61.5 us
    ppermute x6, starting transfers between devices, partner(): return lax.ppermute(block, axis, route)  49.8 us
    ppermute x6, waiting for transfers between devices, partner(): return lax.ppermute(block, axis, route)  12.2 us
  transfers between devices with their start and end apart: 7, of which 2 were waited for; matrix products, arithmetic and copies ran while one was open for 1% of the time, Pallas kernels for 0%

commit v1 on v0

v1 whole, which is shorter than its diff:
```python
import jax
import jax.numpy as jnp
from jax import lax
from jax.sharding import Mesh, PartitionSpec as P

CAP1 = 4
CAP2 = 2
SLOTS = CAP1 + CAP2
EXPERT = ("y_lo", "z")
CHIPS = ("y_hi", "x")
DP = ("y_hi", "x", "core")
SIZES = {"y_lo": 2, "z": 8, "y_hi": 4, "x": 8, "core": 2}


def exchange(blocks, axes):
    return lax.all_to_all(blocks, axes, split_axis=0, concat_axis=0, tiled=True)


def spread(block, axes):
    count = lax.axis_size(axes)
    return exchange(jnp.broadcast_to(block[None], (count,) + block.shape), axes)


def other_core(block):
    return lax.ppermute(block, "core", [(0, 1), (1, 0)])


def local(
    tokens,
    first_expert,
    first_slot,
    second_expert,
    second_slot,
    first_gate,
    second_gate,
    w_gate,
    w_up,
    w_down,
    norm_gain,
    w_query,
):
    tok_count, width = tokens.shape
    blocks = lax.axis_size("z")
    experts = lax.axis_size("y_lo")
    chips = lax.axis_size(CHIPS)
    block_width = width // blocks
    units = w_gate.shape[1]
    own_expert = lax.axis_index("y_lo")
    own_block = lax.axis_index("z")

    w_query_full = lax.all_gather(w_query, DP, axis=0, tiled=True)
    w_gate_other = other_core(w_gate)
    w_up_other = other_core(w_up)
    w_down_other = other_core(w_down)

    served_first = first_slot >= 0
    served = served_first | (second_slot >= 0)
    expert_of = jnp.where(served_first, first_expert, second_expert)
    slot_of = jnp.where(served_first, first_slot, second_slot + CAP1)
    gate_of = jnp.where(served_first, first_gate, second_gate)

    token_block = lax.dynamic_slice_in_dim(tokens, own_block * block_width, block_width, 1)
    placement = jnp.where(served & (expert_of == own_expert), slot_of, -1)
    slot_hot = (jnp.arange(SLOTS, dtype=jnp.int32)[:, None] == placement[None, :]).astype(jnp.bfloat16)
    slot_rows = jnp.dot(slot_hot, token_block, preferred_element_type=jnp.float32).astype(jnp.bfloat16)

    rows = spread(slot_rows, CHIPS).reshape(chips * SLOTS, block_width)
    partial = jnp.concatenate(
        [
            jnp.dot(rows, w, preferred_element_type=jnp.float32).astype(jnp.bfloat16)
            for w in (w_gate, w_gate_other, w_up, w_up_other)
        ],
        axis=1,
    )
    share = chips * SLOTS // blocks
    summed = jnp.sum(
        exchange(partial.reshape(blocks, share, 4 * units), "z").astype(jnp.float32), axis=0
    )
    hidden_share = (jax.nn.silu(summed[:, : 2 * units]) * summed[:, 2 * units :]).astype(jnp.bfloat16)
    hidden = spread(hidden_share, "z").reshape(chips * SLOTS, 2 * units)
    out_part = jnp.dot(hidden[:, :units], w_down, preferred_element_type=jnp.float32) + jnp.dot(
        hidden[:, units:], w_down_other, preferred_element_type=jnp.float32
    )
    pieces = exchange(out_part.astype(jnp.bfloat16).reshape(chips, SLOTS, block_width), CHIPS)
    expert_out = jnp.sum(pieces.astype(jnp.float32), axis=0).astype(jnp.bfloat16)
    gathered = spread(expert_out, EXPERT).reshape(experts, blocks, SLOTS, block_width)
    expert_table = jnp.transpose(gathered, (0, 2, 1, 3)).reshape(experts * SLOTS, width)

    column = jnp.where(served, expert_of * SLOTS + slot_of, -1)
    pick_hot = (column[:, None] == jnp.arange(experts * SLOTS, dtype=jnp.int32)[None, :]).astype(jnp.bfloat16)
    picked = jnp.dot(pick_hot, expert_table, preferred_element_type=jnp.float32)
    mixed = (tokens.astype(jnp.float32) + gate_of[:, None] * picked).astype(jnp.bfloat16)
    values = mixed.astype(jnp.float32)
    scale = lax.rsqrt(jnp.mean(values * values, axis=-1, keepdims=True) + 1e-05)
    normed = (values * scale * norm_gain[None, :]).astype(jnp.bfloat16)
    query = jnp.dot(normed, w_query_full, preferred_element_type=jnp.float32).astype(jnp.bfloat16)
    return (mixed, query)


def solution(mesh):
    fine = Mesh(mesh.devices.reshape(tuple(SIZES.values())), tuple(SIZES))
    in_specs = (
        P(DP, None),
        P(DP),
        P(DP),
        P(DP),
        P(DP),
        P(DP),
        P(DP),
        P(EXPERT, DP),
        P(EXPERT, DP),
        P(DP, EXPERT),
        P(),
        P(DP, EXPERT),
    )
    out_specs = (P(DP, None), P(DP, EXPERT))
    return jax.shard_map(local, mesh=fine, in_specs=in_specs, out_specs=out_specs, check_vma=False)
```

time: 595 us -> 136 us (0.23)
  the two profiles are of different devices: /device:TPU:16 before, /device:TPU:1 now
where the time goes in v1:
time: 136 us; the launch traced here: 135 us
  blocking collectives  46.9 us (34%)
  starting transfers between devices  36.8 us (27%)
  waiting for transfers between devices  26.1 us (19%)
  between operations  14.3 us (11%)
  matrix products  7.57 us (6%)
  local copies, waits for them, and re-layouts  2.36 us (2%)
    all_to_all x2, blocking collectives, exchange(): return lax.all_to_all(blocks, axes, split_axis=0, concat_axis=0, tiled=True)  46.9 us
    all_to_all x3, starting transfers between devices, exchange(): return lax.all_to_all(blocks, axes, split_axis=0, concat_axis=0, tiled=True)  21.1 us
    ppermute x3, starting transfers between devices, other_core(): return lax.ppermute(block, 'core', [(0, 1), (1, 0)])  15.6 us
    all_to_all x3, waiting for transfers between devices, exchange(): return lax.all_to_all(blocks, axes, split_axis=0, concat_axis=0, tiled=True)  12.8 us
    all_gather x1, waiting for transfers between devices, local(): w_query_full = lax.all_gather(w_query, DP, axis=0, tiled=True)  12.6 us
    dot_general x1, matrix products, local(): jnp.dot(normed, w_query_full, preferred_element_type=jnp.float32)  3.67 us
  transfers between devices with their start and end apart: 7, of which 4 were waited for; matrix products, arithmetic and copies ran while one was open for 5% of the time, Pallas kernels for 0%

profile of v1, /device:TPU:1, one launch (start us, length us, event | category | flops | bytes accessed | tf_op | source)
XLA Modules:
  0.0 135.0 jit_solution(13790766191847815866)
XLA Ops:
  7.2 0.0 copy-start.1
  7.2 0.0 all-gather.2.cloned.1.call-start
  7.2 0.7 all-gather.2.cloned.1.call-update
  7.9 0.7 add_select_fusion
  8.6 1.0 convolution_convert_fusion.5
  9.7 0.7 broadcast_in_dim.12
  10.4 13.4 %all-to-all-start = ((bf16[32,6,512]{2,1,0:T(8,128)(2,1)}), bf16[32,6,512]{2,1,0:T(8,128)(2,1)S(1)}, u32[]{:S(2)}, u32[]{:S(2)}) async-start(bf16[32,6,512]{2,1,0:T(8,128)(2,1)} %broadcast_in_dim.12), calls=%async_computation | async-start | bytes 524288 | tf_op jit(solution)/shard_map/all_to_all | solution.py:16
  23.8 6.5 %collective-permute-start.1 = (bf16[512,256]{1,0:T(8,128)(2,1)}, bf16[512,256]{1,0:T(8,128)(2,1)S(1)}, u32[]{:S(2)}, u32[]{:S(2)}) collective-permute-start(bf16[512,256]{1,0:T(8,128)(2,1)} %param.20), channel_id=1, source_target_pairs={{0,1},{1,0},{2,3},{3,2},{4,5},{5,4},{6,7},{7,6},{8,9},{9,8},{10,11... | collective-permute-start | bytes 786440 | tf_op jit(solution)/shard_map/ppermute | solution.py:25
  30.3 1.9 %collective-permute-start = (bf16[512,256]{1,0:T(8,128)(2,1)}, bf16[512,256]{1,0:T(8,128)(2,1)S(1)}, u32[]{:S(2)}, u32[]{:S(2)}) collective-permute-start(bf16[512,256]{1,0:T(8,128)(2,1)} %param.19), channel_id=1, source_target_pairs={{0,1},{1,0},{2,3},{3,2},{4,5},{5,4},{6,7},{7,6},{8,9},{9,8},{10,11... | collective-permute-start | bytes 786440 | tf_op jit(solution)/shard_map/ppermute | solution.py:25
  32.3 3.7 %all-to-all-done = bf16[32,6,512]{2,1,0:T(8,128)(2,1)S(1)} async-done(((bf16[32,6,512]{2,1,0:T(8,128)(2,1)}), bf16[32,6,512]{2,1,0:T(8,128)(2,1)S(1)}, u32[]{:S(2)}, u32[]{:S(2)}) %all-to-all-start) | async-done | bytes 196640 | tf_op jit(solution)/shard_map/all_to_all | solution.py:16
  36.0 0.1 reshape.37
  36.0 1.2 convolution_convert_fusion.2
  37.2 0.0 copy-done.1
  37.2 0.2 convolution_convert_fusion.4
  37.4 0.0 copy-start
  37.4 0.0 collective-permute-done.1
  37.5 0.2 convolution_convert_fusion.1
  37.7 0.0 collective-permute-done
  37.7 0.2 convolution_convert_fusion.3
  38.0 27.1 %all_to_all.25 = bf16[8,24,1024]{2,1,0:T(8,128)(2,1)S(1)} all-to-all(bf16[8,24,1024]{2,1,0:T(8,128)(2,1)S(1)} %bitcast.21), channel_id=1, replica_groups=mesh['y_lo'=2,'z'=8,'y_hi'=4,'x'=8,'core'=2] {'z'}, dimensions={0} | all-to-all | bytes 786432 | tf_op jit(solution)/shard_map/all_to_all | solution.py:16
  65.1 0.1 convert_reduce_fusion
  65.1 0.0 copy-start.3
  65.1 0.0 copy-start.4
  65.1 0.0 copy-start.5
  65.2 0.7 broadcast_in_dim.13
  65.9 3.4 %all-to-all-start.2 = ((bf16[8,24,512]{2,1,0:T(8,128)(2,1)}), bf16[8,24,512]{2,1,0:T(8,128)(2,1)S(1)}, u32[]{:S(2)}, u32[]{:S(2)}) async-start(bf16[8,24,512]{2,1,0:T(8,128)(2,1)} %broadcast_in_dim.13), calls=%async_computation.2 | async-start | bytes 393216 | tf_op jit(solution)/shard_map/all_to_all | solution.py:16
  69.3 0.0 copy-done
  69.3 0.0 copy-start.2
  69.3 7.2 %collective-permute-start.2 = (bf16[256,512]{1,0:T(8,128)(2,1)S(1)}, bf16[256,512]{1,0:T(8,128)(2,1)S(1)}, u32[]{:S(2)}, u32[]{:S(2)}) collective-permute-start(bf16[256,512]{1,0:T(8,128)(2,1)S(1)} %copy-done), channel_id=1, source_target_pairs={{0,1},{1,0},{2,3},{3,2},{4,5},{5,4},{6,7},{7,6},{8,9},{9,8},{10,11... | collective-permute-start | bytes 786440 | tf_op jit(solution)/shard_map/ppermute | solution.py:25
  76.5 1.3 all-to-all-done.2
  77.8 0.2 fusion.11
  78.0 0.0 collective-permute-done.2
  78.0 0.2 fusion.5
  78.2 0.1 reshape.40
  78.3 19.8 %all_to_all.26 = bf16[32,6,512]{2,1,0:T(8,128)(2,1)S(1)} all-to-all(bf16[32,6,512]{2,1,0:T(8,128)(2,1)S(1)} %reshape.40), channel_id=1, replica_groups=mesh['y_lo'=2,'z'=8,'y_hi'=4,'x'=8,'core'=2] {'y_hi','x'}, dimensions={0} | all-to-all | bytes 393216 | tf_op jit(solution)/shard_map/all_to_all | solution.py:16
  98.2 0.1 reduce_sum.31
  98.2 0.7 broadcast_in_dim.14
  98.9 4.3 %all-to-all-start.4 = ((bf16[16,6,512]{2,1,0:T(8,128)(2,1)}), bf16[16,6,512]{2,1,0:T(8,128)(2,1)S(1)}, u32[]{:S(2)}, u32[]{:S(2)}) async-start(bf16[16,6,512]{2,1,0:T(8,128)(2,1)} %broadcast_in_dim.14), calls=%async_computation.4 | async-start | bytes 262144 | tf_op jit(solution)/shard_map/all_to_all | solution.py:16
  103.2 0.0 copy-done.3
  103.3 0.0 copy-done.4
  103.3 0.0 copy-done.5
  103.3 7.7 %all-to-all-done.4 = bf16[16,6,512]{2,1,0:T(8,128)(2,1)S(1)} async-done(((bf16[16,6,512]{2,1,0:T(8,128)(2,1)}), bf16[16,6,512]{2,1,0:T(8,128)(2,1)S(1)}, u32[]{:S(2)}, u32[]{:S(2)}) %all-to-all-start.4) | async-done | bytes 98336 | tf_op jit(solution)/shard_map/all_to_all | solution.py:16
  111.1 0.0 copy-done.2
  111.1 0.7 fusion.2
  111.8 0.0 copy-start.7
  111.8 12.6 %all-gather.2.cloned.1.call-done = bf16[4096,512]{1,0:T(8,128)(2,1)} async-done(((bf16[64,512]{1,0:T(8,128)(2,1)}), bf16[4096,512]{1,0:T(8,128)(2,1)}) %all-gather.2.cloned.1.call-update) | async-done | bytes 4194320 | tf_op jit(solution)/shard_map/all_gather | solution.py:51
  124.4 0.0 copy-done.6
  124.5 3.7 %convolution_convert_fusion = bf16[128,512]{1,0:T(8,128)(2,1)} fusion(bf16[4096,512]{1,0:T(8,128)(2,1)} %all-gather.2.cloned.1.call-done, bf16[128,4096]{1,0:T(8,128)(2,1)S(1)} %get-tuple-element.5, f32[4096]{0:T(1024)S(1)} %copy-done.6, f32[128]{0:T(128)S(1)} %add_rsqrt_fusion), kind=kOutput, calls=%fused_computation.10 | convolution fusion | flops 539033600 | bytes 5390848 | tf_op jit(solution)/shard_map/dot_general | solution.py:96
  (9 shorter events, 0.2 us)
Async XLA Ops:
  7.2 30.0 %copy-start.1 = (bf16[512,256]{1,0:T(8,128)(2,1)S(1)}, bf16[512,256]{1,0:T(8,128)(2,1)}, u32[]{:S(2)}) copy-start(bf16[512,256]{1,0:T(8,128)(2,1)} %param.19) | copy-start | bytes 786436
  7.2 117.3 %all-gather.2.cloned.1.call-start = ((), (), s32[]{:S(2)}) async-start(), calls=%async_computation.5 | async-start | bytes 4259840 | tf_op jit(solution)/shard_map/all_gather | solution.py:51
  10.4 25.6 %all-to-all-start = ((bf16[32,6,512]{2,1,0:T(8,128)(2,1)}), bf16[32,6,512]{2,1,0:T(8,128)(2,1)S(1)}, u32[]{:S(2)}, u32[]{:S(2)}) async-start(bf16[32,6,512]{2,1,0:T(8,128)(2,1)} %broadcast_in_dim.12), calls=%async_computation | async-start | bytes 524288 | tf_op jit(solution)/shard_map/all_to_all | solution.py:16
  23.8 13.6 %collective-permute-start.1 = (bf16[512,256]{1,0:T(8,128)(2,1)}, bf16[512,256]{1,0:T(8,128)(2,1)S(1)}, u32[]{:S(2)}, u32[]{:S(2)}) collective-permute-start(bf16[512,256]{1,0:T(8,128)(2,1)} %param.20), channel_id=1, source_target_pairs={{0,1},{1,0},{2,3},{3,2},{4,5},{5,4},{6,7},{7,6},{8,9},{9,8},{10,11... | collective-permute-start | bytes 786440 | tf_op jit(solution)/shard_map/ppermute | solution.py:25
  30.3 7.3 %collective-permute-start = (bf16[512,256]{1,0:T(8,128)(2,1)}, bf16[512,256]{1,0:T(8,128)(2,1)S(1)}, u32[]{:S(2)}, u32[]{:S(2)}) collective-permute-start(bf16[512,256]{1,0:T(8,128)(2,1)} %param.19), channel_id=1, source_target_pairs={{0,1},{1,0},{2,3},{3,2},{4,5},{5,4},{6,7},{7,6},{8,9},{9,8},{10,11... | collective-permute-start | bytes 786440 | tf_op jit(solution)/shard_map/ppermute | solution.py:25
  37.4 31.8 %copy-start = (bf16[256,512]{1,0:T(8,128)(2,1)S(1)}, bf16[256,512]{1,0:T(8,128)(2,1)}, u32[]{:S(2)}) copy-start(bf16[256,512]{1,0:T(8,128)(2,1)} %param.21) | copy-start | bytes 786436
  65.1 38.1 %copy-start.3 = (s32[128]{0:T(128)S(1)}, s32[128]{0:T(128)}, u32[]{:S(2)}) copy-start(s32[128]{0:T(128)} %param.14) | copy-start | bytes 1540
  65.1 38.1 %copy-start.4 = (f32[128]{0:T(128)S(1)}, f32[128]{0:T(128)}, u32[]{:S(2)}) copy-start(f32[128]{0:T(128)} %param.17) | copy-start | bytes 1540
  65.1 38.1 %copy-start.5 = (f32[128]{0:T(128)S(1)}, f32[128]{0:T(128)}, u32[]{:S(2)}) copy-start(f32[128]{0:T(128)} %param.18) | copy-start | bytes 1540
  65.9 11.9 %all-to-all-start.2 = ((bf16[8,24,512]{2,1,0:T(8,128)(2,1)}), bf16[8,24,512]{2,1,0:T(8,128)(2,1)S(1)}, u32[]{:S(2)}, u32[]{:S(2)}) async-start(bf16[8,24,512]{2,1,0:T(8,128)(2,1)} %broadcast_in_dim.13), calls=%async_computation.2 | async-start | bytes 393216 | tf_op jit(solution)/shard_map/all_to_all | solution.py:16
  69.3 41.8 %copy-start.2 = (bf16[128,4096]{1,0:T(8,128)(2,1)S(1)}, bf16[128,4096]{1,0:T(8,128)(2,1)}, u32[]{:S(2)}) copy-start(bf16[128,4096]{1,0:T(8,128)(2,1)} %param.12) | copy-start | bytes 3145732
  69.3 8.7 %collective-permute-start.2 = (bf16[256,512]{1,0:T(8,128)(2,1)S(1)}, bf16[256,512]{1,0:T(8,128)(2,1)S(1)}, u32[]{:S(2)}, u32[]{:S(2)}) collective-permute-start(bf16[256,512]{1,0:T(8,128)(2,1)S(1)} %copy-done), channel_id=1, source_target_pairs={{0,1},{1,0},{2,3},{3,2},{4,5},{5,4},{6,7},{7,6},{8,9},{9,8},{10,11... | collective-permute-start | bytes 786440 | tf_op jit(solution)/shard_map/ppermute | solution.py:25
  98.2 26.3 %copy-start.6 = (f32[4096]{0:T(1024)S(1)}, f32[4096]{0:T(1024)}, u32[]{:S(2)}) copy-start(f32[4096]{0:T(1024)} %param.22) | copy-start | bytes 49156
  98.9 12.1 %all-to-all-start.4 = ((bf16[16,6,512]{2,1,0:T(8,128)(2,1)}), bf16[16,6,512]{2,1,0:T(8,128)(2,1)S(1)}, u32[]{:S(2)}, u32[]{:S(2)}) async-start(bf16[16,6,512]{2,1,0:T(8,128)(2,1)} %broadcast_in_dim.14), calls=%async_computation.4 | async-start | bytes 262144 | tf_op jit(solution)/shard_map/all_to_all | solution.py:16
  111.8 16.3 %copy-start.7 = (bf16[128,4096]{1,0:T(8,128)(2,1)}, bf16[128,4096]{1,0:T(8,128)(2,1)S(1)}, u32[]{:S(2)}) copy-start(bf16[128,4096]{1,0:T(8,128)(2,1)S(1)} %get-tuple-element.5) | copy-start | bytes 3145732
Sparse Core Ops, SparseCore 0:
  12.5 111.8 all-gather.1

commit v2 on v1

v2 whole, which is shorter than its diff:
```python
import jax
import jax.numpy as jnp
from jax import lax
from jax.experimental import pallas as pl
from jax.experimental.pallas import tpu as pltpu
from jax.sharding import Mesh, PartitionSpec as P

CAP1 = 4
CAP2 = 2
SLOTS = CAP1 + CAP2
EXPERT = ("y_lo", "z")
CHIPS = ("y_hi", "x")
DP = ("y_hi", "x", "core")
SIZES = {"y_lo": 2, "z": 8, "y_hi": 4, "x": 8, "core": 2}
PADDED = 8
LANES = 128


def exchange(blocks, axes):
    return lax.all_to_all(blocks, axes, split_axis=0, concat_axis=0, tiled=True)


def spread(block, axes):
    count = lax.axis_size(axes)
    return exchange(jnp.broadcast_to(block[None], (count,) + block.shape), axes)


def other_core(block):
    return lax.ppermute(block, "core", [(0, 1), (1, 0)])


def from_above(block, distance):
    count = lax.axis_size("y_hi")
    return lax.ppermute(block, "y_hi", [((i + distance) % count, i) for i in range(count)])


def outward(block, distance):
    count = lax.axis_size("x")
    route = []
    for i in range(count):
        route.append((2 * i, 2 * ((i + distance) % count)))
        route.append((2 * i + 1, 2 * ((i - distance) % count) + 1))
    return lax.ppermute(block, ("x", "core"), route)


def tie(*values):
    return lax.optimization_barrier(values)


def finish_kernel(
    place_ref, tokens_ref, table_ref, column_ref, gate_ref, gain_ref, *refs
):
    w_refs, (mixed_ref, query_ref, normed_ref) = refs[:-3], refs[-3:]
    x, y, core = place_ref[0], place_ref[1], place_ref[2]
    blocks = table_ref.shape[0] // (2 * PADDED)
    tok_count, width = tokens_ref.shape
    block_width = width // blocks
    column = column_ref[...]
    slots = lax.broadcasted_iota(jnp.int32, (tok_count, PADDED), 1)
    hot = [
        (column == slots + e * PADDED).astype(jnp.bfloat16) for e in range(2)
    ]
    gate = gate_ref[...]
    square = jnp.zeros((tok_count, LANES), jnp.float32)
    for z in range(blocks):
        cols = pl.ds(z * block_width, block_width)
        picked = sum(
            jnp.dot(
                hot[e],
                table_ref[pl.ds((e * blocks + z) * PADDED, PADDED), :],
                preferred_element_type=jnp.float32,
            )
            for e in range(2)
        )
        mixed = (tokens_ref[:, cols].astype(jnp.float32) + gate * picked).astype(jnp.bfloat16)
        mixed_ref[:, cols] = mixed
        values = mixed.astype(jnp.float32)
        for i in range(block_width // LANES):
            part = values[:, i * LANES : (i + 1) * LANES]
            square += part * part
    mean = jnp.sum(square, axis=1, keepdims=True) * (1.0 / width)
    scale = lax.rsqrt(mean + 1e-05)
    for z in range(blocks):
        cols = pl.ds(z * block_width, block_width)
        values = mixed_ref[:, cols].astype(jnp.float32)
        normed_ref[:, cols] = (values * scale * gain_ref[:, cols]).astype(jnp.bfloat16)
    sign = 1 - 2 * core
    xs = [0, -1, -2, -3, 4, 1, 2, 3, 4]
    query = jnp.zeros(query_ref.shape, jnp.float32)
    for w_ref, offset in zip(w_refs, xs, strict=True):
        far = abs(offset) == 4
        chip_x = lax.rem(x + sign * offset + 8, 8)
        if far:
            half = core if w_ref is w_refs[4] else 1 - core
        for j in range(w_ref.shape[0]):
            rel = j + half * 2 if far else j
            chip_y = lax.rem(y + rel, 4)
            start = pl.multiple_of((chip_y * 8 + chip_x) * LANES, LANES)
            query += jnp.dot(
                normed_ref[:, pl.ds(start, LANES)], w_ref[j], preferred_element_type=jnp.float32
            )
    query_ref[...] = query.astype(query_ref.dtype)


def finish(place, tokens, table, column, gate, gain, weights):
    vmem = pl.BlockSpec(memory_space=pltpu.VMEM)
    tok_count, width = tokens.shape
    columns = weights[0].shape[-1]
    return pl.pallas_call(
        finish_kernel,
        out_shape=(
            jax.ShapeDtypeStruct((tok_count, width), jnp.bfloat16),
            jax.ShapeDtypeStruct((tok_count, columns), jnp.bfloat16),
        ),
        in_specs=[pl.BlockSpec(memory_space=pltpu.SMEM)] + [vmem] * (5 + len(weights)),
        out_specs=(vmem, vmem),
        scratch_shapes=[pltpu.VMEM((tok_count, width), jnp.bfloat16)],
        compiler_params=pltpu.CompilerParams(vmem_limit_bytes=24 * 1024 * 1024),
        cost_estimate=pl.CostEstimate(
            flops=2 * tok_count * width * columns, bytes_accessed=4 * width * columns, transcendentals=0
        ),
    )(place, tokens, table, column[:, None], gate[:, None], gain[None, :], *weights)


def local(
    tokens,
    first_expert,
    first_slot,
    second_expert,
    second_slot,
    first_gate,
    second_gate,
    w_gate,
    w_up,
    w_down,
    norm_gain,
    w_query,
):
    tok_count, width = tokens.shape
    blocks = lax.axis_size("z")
    chips = lax.axis_size(CHIPS)
    block_width = width // blocks
    units = w_gate.shape[1]
    own_expert = lax.axis_index("y_lo")
    own_block = lax.axis_index("z")
    core = lax.axis_index("core")

    served_first = first_slot >= 0
    served = served_first | (second_slot >= 0)
    expert_of = jnp.where(served_first, first_expert, second_expert)
    slot_of = jnp.where(served_first, first_slot, second_slot + CAP1)
    gate_of = jnp.where(served_first, first_gate, second_gate)

    token_block = lax.dynamic_slice_in_dim(tokens, own_block * block_width, block_width, 1)
    placement = jnp.where(served & (expert_of == own_expert), slot_of, -1)
    slot_hot = (jnp.arange(SLOTS, dtype=jnp.int32)[:, None] == placement[None, :]).astype(jnp.bfloat16)
    slot_rows = jnp.dot(slot_hot, token_block, preferred_element_type=jnp.float32).astype(jnp.bfloat16)

    chip_rows = other_core(w_query)
    chip_rows = jnp.where(
        core == 0, jnp.concatenate([w_query, chip_rows], 0), jnp.concatenate([chip_rows, w_query], 0)
    )
    slot_rows, chip_rows = tie(slot_rows, chip_rows)
    rows = spread(slot_rows, CHIPS).reshape(chips * SLOTS, block_width)
    w_gate_other = other_core(w_gate)
    w_up_other = other_core(w_up)
    query_own = jnp.stack([chip_rows] + [from_above(chip_rows, i) for i in (1, 2, 3)])

    partial = jnp.concatenate(
        [
            jnp.dot(rows, w, preferred_element_type=jnp.float32).astype(jnp.bfloat16)
            for w in (w_gate, w_gate_other, w_up, w_up_other)
        ],
        axis=1,
    )
    share = chips * SLOTS // blocks
    partial, query_own = tie(partial, query_own)
    summed = exchange(partial.reshape(blocks, share, 4 * units), "z")
    near = [outward(query_own, 1), outward(query_own, 2)]
    summed = jnp.sum(summed.astype(jnp.float32), axis=0)
    hidden_share = (jax.nn.silu(summed[:, : 2 * units]) * summed[:, 2 * units :]).astype(jnp.bfloat16)
    hidden_share, near[0], near[1] = tie(hidden_share, *near)
    hidden = spread(hidden_share, "z").reshape(chips * SLOTS, 2 * units)
    w_down_other = other_core(w_down)
    far_half = lax.dynamic_slice_in_dim(near[1], 2 * core, 2, 0)
    far = [outward(near[0], 2), outward(far_half, 2)]
    out_part = jnp.dot(hidden[:, :units], w_down, preferred_element_type=jnp.float32) + jnp.dot(
        hidden[:, units:], w_down_other, preferred_element_type=jnp.float32
    )
    out_part = out_part.astype(jnp.bfloat16)
    pieces = exchange(out_part.reshape(chips, SLOTS, block_width), CHIPS)
    expert_out = jnp.sum(pieces.astype(jnp.float32), axis=0).astype(jnp.bfloat16)
    expert_out = jnp.concatenate([expert_out, jnp.zeros((PADDED - SLOTS, block_width), jnp.bfloat16)], 0)
    expert_out, far[0], far[1] = tie(expert_out, *far)
    table = spread(expert_out, EXPERT).reshape(-1, block_width)
    arrived = near + far
    weights = [query_own] + arrived + [other_core(block) for block in arrived]

    column = jnp.where(served, expert_of * PADDED + slot_of, -1)
    place = jnp.stack([lax.axis_index("x"), lax.axis_index("y_hi"), core]).astype(jnp.int32)
    return finish(place, tokens, table, column, gate_of, norm_gain, weights)


def solution(mesh):
    fine = Mesh(mesh.devices.reshape(tuple(SIZES.values())), tuple(SIZES))
    in_specs = (
        P(DP, None),
        P(DP),
        P(DP),
        P(DP),
        P(DP),
        P(DP),
        P(DP),
        P(EXPERT, DP),
        P(EXPERT, DP),
        P(DP, EXPERT),
        P(),
        P(DP, EXPERT),
    )
    out_specs = (P(DP, None), P(DP, EXPERT))
    return jax.shard_map(local, mesh=fine, in_specs=in_specs, out_specs=out_specs, check_vma=False)
```

time: 136 us -> 152 us (1.12)
  the two profiles are of different devices: /device:TPU:1 before, /device:TPU:2 now
where the time goes in v2:
time: 152 us; the launch traced here: 151 us
  starting transfers between devices  102 us (67%)
  waiting for transfers between devices  33.3 us (22%)
  local copies, waits for them, and re-layouts  5.53 us (4%)
  Pallas kernels  4.55 us (3%)
  matrix products  2.33 us (2%)
  other arithmetic  2.08 us (1%)
    all_to_all x5, starting transfers between devices, exchange(): return lax.all_to_all(blocks, axes, split_axis=0, concat_axis=0, tiled=True)  52.7 us
    all_to_all x5, waiting for transfers between devices, exchange(): return lax.all_to_all(blocks, axes, split_axis=0, concat_axis=0, tiled=True)  21.8 us
    ppermute x4, starting transfers between devices, outward(): return lax.ppermute(block, ('x', 'core'), route)  17.6 us
    ppermute x8, starting transfers between devices, other_core(): return lax.ppermute(block, 'core', [(0, 1), (1, 0)])  16.8 us
    ppermute x3, starting transfers between devices, from_above(): lax.ppermute(block, 'y_hi', [((i + distance) % count, i) for i in range(c...  15.3 us
    ppermute x4, waiting for transfers between devices, outward(): return lax.ppermute(block, ('x', 'core'), route)  8.36 us
    pallas_call x1, Pallas kernels, finish(): pl.pallas_call(finish_kernel, out_shape=(jax.ShapeDtypeStruct((tok_count,...  4.55 us
    ppermute x3, waiting for transfers between devices, from_above(): lax.ppermute(block, 'y_hi', [((i + distance) % count, i) for i in range(c...  3.09 us
  transfers between devices with their start and end apart: 20, of which 7 were waited for; matrix products, arithmetic and copies ran while one was open for 4% of the time, Pallas kernels for 0%

profile of v2, /device:TPU:2, one launch (start us, length us, event | category | flops | bytes accessed | tf_op | source)
XLA Modules:
  0.0 151.3 jit_solution(14485141774672275385)
XLA Ops:
  0.6 1.9 %collective-permute-start = (bf16[64,512]{1,0:T(8,128)(2,1)}, bf16[64,512]{1,0:T(8,128)(2,1)S(1)}, u32[]{:S(2)}, u32[]{:S(2)}) collective-permute-start(bf16[64,512]{1,0:T(8,128)(2,1)} %param.23), channel_id=1, source_target_pairs={{0,1},{1,0},{2,3},{3,2},{4,5},{5,4},{6,7},{7,6},{8,9},{9,8},{10,11... | collective-permute-start | bytes 196616 | tf_op jit(solution)/shard_map/ppermute | solution.py:29
  2.6 0.6 copy-done.8
  3.3 1.1 convolution_convert_fusion.4
  4.4 0.7 broadcast_in_dim.18
  5.1 16.8 %all-to-all-start = ((bf16[32,6,512]{2,1,0:T(8,128)(2,1)}), bf16[32,6,512]{2,1,0:T(8,128)(2,1)S(1)}, u32[]{:S(2)}, u32[]{:S(2)}) async-start(bf16[32,6,512]{2,1,0:T(8,128)(2,1)} %broadcast_in_dim.18), calls=%async_computation | async-start | bytes 524288 | tf_op jit(solution)/shard_map/all_to_all | solution.py:20
  22.0 4.3 %collective-permute-start.5 = (bf16[128,512]{1,0:T(8,128)(2,1)S(1)}, bf16[128,512]{1,0:T(8,128)(2,1)S(1)}, u32[]{:S(2)}, u32[]{:S(2)}) collective-permute-start(bf16[128,512]{1,0:T(8,128)(2,1)S(1)} %maximum_select_fusion), channel_id=1, source_target_pairs={{48,0},{0,16},{16,32},{32,48},{49,1},{1,17},{17,33},{33,49},{50,2}... | collective-permute-start | bytes 393224 | tf_op jit(solution)/shard_map/ppermute | solution.py:34
  26.3 5.6 %collective-permute-start.4 = (bf16[128,512]{1,0:T(8,128)(2,1)S(1)}, bf16[128,512]{1,0:T(8,128)(2,1)S(1)}, u32[]{:S(2)}, u32[]{:S(2)}) collective-permute-start(bf16[128,512]{1,0:T(8,128)(2,1)S(1)} %maximum_select_fusion), channel_id=1, source_target_pairs={{32,0},{48,16},{0,32},{16,48},{33,1},{49,17},{1,33},{17,49},{34,2}... | collective-permute-start | bytes 393224 | tf_op jit(solution)/shard_map/ppermute | solution.py:34
  31.9 5.4 %collective-permute-start.3 = (bf16[128,512]{1,0:T(8,128)(2,1)S(1)}, bf16[128,512]{1,0:T(8,128)(2,1)S(1)}, u32[]{:S(2)}, u32[]{:S(2)}) collective-permute-start(bf16[128,512]{1,0:T(8,128)(2,1)S(1)} %maximum_select_fusion), channel_id=1, source_target_pairs={{16,0},{32,16},{48,32},{0,48},{17,1},{33,17},{49,33},{1,49},{18,2}... | collective-permute-start | bytes 393224 | tf_op jit(solution)/shard_map/ppermute | solution.py:34
  37.3 1.9 %collective-permute-start.1 = (bf16[512,256]{1,0:T(8,128)(2,1)S(1)}, bf16[512,256]{1,0:T(8,128)(2,1)S(1)}, u32[]{:S(2)}, u32[]{:S(2)}) collective-permute-start(bf16[512,256]{1,0:T(8,128)(2,1)S(1)} %copy-done.5), channel_id=1, source_target_pairs={{0,1},{1,0},{2,3},{3,2},{4,5},{5,4},{6,7},{7,6},{8,9},{9,8},{10,11... | collective-permute-start | bytes 786440 | tf_op jit(solution)/shard_map/ppermute | solution.py:29
  39.3 2.4 %collective-permute-start.2 = (bf16[512,256]{1,0:T(8,128)(2,1)S(1)}, bf16[512,256]{1,0:T(8,128)(2,1)S(1)}, u32[]{:S(2)}, u32[]{:S(2)}) collective-permute-start(bf16[512,256]{1,0:T(8,128)(2,1)S(1)} %copy-done.6), channel_id=1, source_target_pairs={{0,1},{1,0},{2,3},{3,2},{4,5},{5,4},{6,7},{7,6},{8,9},{9,8},{10,11... | collective-permute-start | bytes 786440 | tf_op jit(solution)/shard_map/ppermute | solution.py:29
  41.7 3.1 %collective-permute-done.4 = bf16[128,512]{1,0:T(8,128)(2,1)S(1)} collective-permute-done((bf16[128,512]{1,0:T(8,128)(2,1)S(1)}, bf16[128,512]{1,0:T(8,128)(2,1)S(1)}, u32[]{:S(2)}, u32[]{:S(2)}) %collective-permute-start.4) | collective-permute-done | bytes 131104 | tf_op jit(solution)/shard_map/ppermute | solution.py:34
  44.9 0.1 reshape.23
  45.0 0.2 convolution_convert_fusion.1
  45.2 0.2 convolution_convert_fusion.3
  45.4 0.2 convolution_convert_fusion.2
  45.6 0.2 convolution_convert_fusion
  45.8 0.8 pad_maximum_fusion.1
  46.6 13.5 %all-to-all-start.1 = ((bf16[8,24,1024]{2,1,0:T(8,128)(2,1)}), bf16[8,24,1024]{2,1,0:T(8,128)(2,1)S(1)}, u32[]{:S(2)}, u32[]{:S(2)}) async-start(bf16[8,24,1024]{2,1,0:T(8,128)(2,1)} %bitcast.7), calls=%async_computation.1 | async-start | bytes 786432 | tf_op jit(solution)/shard_map/all_to_all | solution.py:20
  60.2 4.5 %collective-permute-start.7 = (bf16[4,128,512]{2,1,0:T(8,128)(2,1)S(1)}, bf16[4,128,512]{2,1,0:T(8,128)(2,1)S(1)}, u32[]{:S(2)}, u32[]{:S(2)}) collective-permute-start(bf16[4,128,512]{2,1,0:T(8,128)(2,1)S(1)} %pad_maximum_fusion.refs_0_), channel_id=1, source_target_pairs={{0,4},{1,13},{2,6},{3,15},{4,8},{5,1},{6,10},{7,3},{8,12},{9,5},{1... | collective-permute-start | bytes 1572872 | tf_op jit(solution)/shard_map/ppermute | solution.py:43
  64.6 3.9 %collective-permute-start.6 = (bf16[4,128,512]{2,1,0:T(8,128)(2,1)S(1)}, bf16[4,128,512]{2,1,0:T(8,128)(2,1)S(1)}, u32[]{:S(2)}, u32[]{:S(2)}) collective-permute-start(bf16[4,128,512]{2,1,0:T(8,128)(2,1)S(1)} %pad_maximum_fusion.refs_0_), channel_id=1, source_target_pairs={{0,2},{1,15},{2,4},{3,1},{4,6},{5,3},{6,8},{7,5},{8,10},{9,7},{10,... | collective-permute-start | bytes 1572872 | tf_op jit(solution)/shard_map/ppermute | solution.py:43
  68.5 6.4 %all-to-all-done.1 = bf16[8,24,1024]{2,1,0:T(8,128)(2,1)S(1)} async-done(((bf16[8,24,1024]{2,1,0:T(8,128)(2,1)}), bf16[8,24,1024]{2,1,0:T(8,128)(2,1)S(1)}, u32[]{:S(2)}, u32[]{:S(2)}) %all-to-all-start.1) | async-done | bytes 393248 | tf_op jit(solution)/shard_map/all_to_all | solution.py:20
  75.0 3.8 %collective-permute-done.7.refs_2_ = bf16[4,128,512]{2,1,0:T(8,128)(2,1)S(1)} collective-permute-done((bf16[4,128,512]{2,1,0:T(8,128)(2,1)S(1)}, bf16[4,128,512]{2,1,0:T(8,128)(2,1)S(1)}, u32[]{:S(2)}, u32[]{:S(2)}) %collective-permute-start.7) | collective-permute-done | bytes 524320 | tf_op jit(solution)/shard_map/ppermute | solution.py:43
  78.8 4.6 %collective-permute-done.6.refs_1_ = bf16[4,128,512]{2,1,0:T(8,128)(2,1)S(1)} collective-permute-done((bf16[4,128,512]{2,1,0:T(8,128)(2,1)S(1)}, bf16[4,128,512]{2,1,0:T(8,128)(2,1)S(1)}, u32[]{:S(2)}, u32[]{:S(2)}) %collective-permute-start.6) | collective-permute-done | bytes 524320 | tf_op jit(solution)/shard_map/ppermute | solution.py:43
  83.4 0.7 broadcast_in_dim.19
  84.1 7.2 %all-to-all-start.2 = ((bf16[8,24,512]{2,1,0:T(8,128)(2,1)}), bf16[8,24,512]{2,1,0:T(8,128)(2,1)S(1)}, u32[]{:S(2)}, u32[]{:S(2)}) async-start(bf16[8,24,512]{2,1,0:T(8,128)(2,1)} %broadcast_in_dim.19), calls=%async_computation.2 | async-start | bytes 393216 | tf_op jit(solution)/shard_map/all_to_all | solution.py:20
  91.3 1.9 %collective-permute-start.8 = (bf16[256,512]{1,0:T(8,128)(2,1)S(1)}, bf16[256,512]{1,0:T(8,128)(2,1)S(1)}, u32[]{:S(2)}, u32[]{:S(2)}) collective-permute-start(bf16[256,512]{1,0:T(8,128)(2,1)S(1)} %copy-done.4), channel_id=1, source_target_pairs={{0,1},{1,0},{2,3},{3,2},{4,5},{5,4},{6,7},{7,6},{8,9},{9,8},{10,11... | collective-permute-start | bytes 786440 | tf_op jit(solution)/shard_map/ppermute | solution.py:29
  93.2 5.0 %collective-permute-start.9 = (bf16[4,128,512]{2,1,0:T(8,128)(2,1)S(1)}, bf16[4,128,512]{2,1,0:T(8,128)(2,1)S(1)}, u32[]{:S(2)}, u32[]{:S(2)}) collective-permute-start(bf16[4,128,512]{2,1,0:T(8,128)(2,1)S(1)} %collective-permute-done.6.refs_1_), channel_id=1, source_target_pairs={{0,4},{1,13},{2,6},{3,15},{4,8},{5,1},{6,10},{7,3},{8,12},{9,5},{1... | collective-permute-start | bytes 1572872 | tf_op jit(solution)/shard_map/ppermute | solution.py:43
  98.2 2.8 %all-to-all-done.2 = bf16[8,24,512]{2,1,0:T(8,128)(2,1)S(1)} async-done(((bf16[8,24,512]{2,1,0:T(8,128)(2,1)}), bf16[8,24,512]{2,1,0:T(8,128)(2,1)S(1)}, u32[]{:S(2)}, u32[]{:S(2)}) %all-to-all-start.2) | async-done | bytes 196640 | tf_op jit(solution)/shard_map/all_to_all | solution.py:20
  101.1 0.2 fusion.3
  101.3 0.2 fusion
  101.5 0.8 reshape.26
  102.3 11.5 %all-to-all-start.3 = ((bf16[32,6,512]{2,1,0:T(8,128)(2,1)}), bf16[32,6,512]{2,1,0:T(8,128)(2,1)}, u32[]{:S(2)}, u32[]{:S(2)}) async-start(bf16[32,6,512]{2,1,0:T(8,128)(2,1)} %reshape.26), calls=%async_computation.3 | async-start | bytes 524288 | tf_op jit(solution)/shard_map/all_to_all | solution.py:20
  113.8 0.7 constant_dynamic-slice_fusion
  114.5 4.3 %collective-permute-start.10 = (bf16[2,128,512]{2,1,0:T(8,128)(2,1)}, bf16[2,128,512]{2,1,0:T(8,128)(2,1)S(1)}, u32[]{:S(2)}, u32[]{:S(2)}) collective-permute-start(bf16[2,128,512]{2,1,0:T(8,128)(2,1)} %constant_dynamic-slice_fusion), channel_id=1, source_target_pairs={{0,4},{1,13},{2,6},{3,15},{4,8},{5,1},{6,10},{7,3},{8,12},{9,5},{1... | collective-permute-start | bytes 786440 | tf_op jit(solution)/shard_map/ppermute | solution.py:43
  118.7 1.9 %collective-permute-start.11 = (bf16[4,128,512]{2,1,0:T(8,128)(2,1)S(1)}, bf16[4,128,512]{2,1,0:T(8,128)(2,1)}, u32[]{:S(2)}, u32[]{:S(2)}) collective-permute-start(bf16[4,128,512]{2,1,0:T(8,128)(2,1)S(1)} %collective-permute-done.6.refs_1_), channel_id=1, source_target_pairs={{0,1},{1,0},{2,3},{3,2},{4,5},{5,4},{6,7},{7,6},{8,9},{9,8},{10,11... | collective-permute-start | bytes 1572872 | tf_op jit(solution)/shard_map/ppermute | solution.py:29
  120.7 2.4 %collective-permute-start.12 = (bf16[4,128,512]{2,1,0:T(8,128)(2,1)S(1)}, bf16[4,128,512]{2,1,0:T(8,128)(2,1)}, u32[]{:S(2)}, u32[]{:S(2)}) collective-permute-start(bf16[4,128,512]{2,1,0:T(8,128)(2,1)S(1)} %collective-permute-done.7.refs_2_), channel_id=1, source_target_pairs={{0,1},{1,0},{2,3},{3,2},{4,5},{5,4},{6,7},{7,6},{8,9},{9,8},{10,11... | collective-permute-start | bytes 1572872 | tf_op jit(solution)/shard_map/ppermute | solution.py:29
  123.1 6.6 %all-to-all-done.3 = bf16[32,6,512]{2,1,0:T(8,128)(2,1)} async-done(((bf16[32,6,512]{2,1,0:T(8,128)(2,1)}), bf16[32,6,512]{2,1,0:T(8,128)(2,1)}, u32[]{:S(2)}, u32[]{:S(2)}) %all-to-all-start.3) | async-done | bytes 196640 | tf_op jit(solution)/shard_map/all_to_all | solution.py:20
  129.7 1.0 reduce_sum.22
  130.7 1.9 %collective-permute-start.13 = (bf16[4,128,512]{2,1,0:T(8,128)(2,1)S(1)}, bf16[4,128,512]{2,1,0:T(8,128)(2,1)}, u32[]{:S(2)}, u32[]{:S(2)}) collective-permute-start(bf16[4,128,512]{2,1,0:T(8,128)(2,1)S(1)} %collective-permute-done.9.refs_3_), channel_id=1, source_target_pairs={{0,1},{1,0},{2,3},{3,2},{4,5},{5,4},{6,7},{7,6},{8,9},{9,8},{10,11... | collective-permute-start | bytes 1572872 | tf_op jit(solution)/shard_map/ppermute | solution.py:29
  132.7 0.1 copy.16.column_ref
  132.8 0.7 broadcast_in_dim.38
  133.5 3.6 %all-to-all-start.4 = ((bf16[16,8,512]{2,1,0:T(8,128)(2,1)}), bf16[16,8,512]{2,1,0:T(8,128)(2,1)S(1)}, u32[]{:S(2)}, u32[]{:S(2)}) async-start(bf16[16,8,512]{2,1,0:T(8,128)(2,1)} %broadcast_in_dim.38), calls=%async_computation.4 | async-start | bytes 262144 | tf_op jit(solution)/shard_map/all_to_all | solution.py:20
  137.1 2.4 %collective-permute-start.14 = (bf16[2,128,512]{2,1,0:T(8,128)(2,1)}, bf16[2,128,512]{2,1,0:T(8,128)(2,1)}, u32[]{:S(2)}, u32[]{:S(2)}) collective-permute-start(bf16[2,128,512]{2,1,0:T(8,128)(2,1)} %copy-done.1), channel_id=1, source_target_pairs={{0,1},{1,0},{2,3},{3,2},{4,5},{5,4},{6,7},{7,6},{8,9},{9,8},{10,11... | collective-permute-start | bytes 786440 | tf_op jit(solution)/shard_map/ppermute | solution.py:29
  139.6 0.1 copy.17.gate_ref
  139.7 0.1 pad_add_fusion.place_ref
  139.8 6.1 %all-to-all-done.4 = bf16[16,8,512]{2,1,0:T(8,128)(2,1)S(1)} async-done(((bf16[16,8,512]{2,1,0:T(8,128)(2,1)}), bf16[16,8,512]{2,1,0:T(8,128)(2,1)S(1)}, u32[]{:S(2)}, u32[]{:S(2)}) %all-to-all-start.4) | async-done | bytes 131104 | tf_op jit(solution)/shard_map/all_to_all | solution.py:20
  145.8 0.9 copy-done.2
  146.8 4.5 %shard_map.131 = (bf16[128,4096]{1,0:T(8,128)(2,1)}, bf16[128,512]{1,0:T(8,128)(2,1)}) custom-call(s32[3]{0:T(128)S(1)} %pad_add_fusion.place_ref, bf16[128,4096]{1,0:T(8,128)(2,1)S(1)} %copy-done, bf16[128,512]{1,0:T(8,128)(2,1)S(1)} %bitcast.25, s32[128,1]{1,0:T(8,128)S(1)} %copy.16.column_ref, f32[128,1]{1,0:T(8,128)S(1)} %copy.17.gate_ref, ...), custom_call_target="tpu_custom_call" | custom-call | flops 536870912 | bytes 8388608 | tf_op jit(solution)/shard_map/pallas_call | solution.py:109
  (46 shorter events, 0.3 us)
Async XLA Ops:
  0.6 3.7 %collective-permute-start = (bf16[64,512]{1,0:T(8,128)(2,1)}, bf16[64,512]{1,0:T(8,128)(2,1)S(1)}, u32[]{:S(2)}, u32[]{:S(2)}) collective-permute-start(bf16[64,512]{1,0:T(8,128)(2,1)} %param.23), channel_id=1, source_target_pairs={{0,1},{1,0},{2,3},{3,2},{4,5},{5,4},{6,7},{7,6},{8,9},{9,8},{10,11... | collective-permute-start | bytes 196616 | tf_op jit(solution)/shard_map/ppermute | solution.py:29
  2.6 0.7 copy-start.8
  2.6 0.7 copy-start.9
  2.6 0.7 copy-start.10
  2.6 0.7 copy-start.11
  3.3 1.1 copy-start.7
  5.1 32.2 %copy-start.5 = (bf16[512,256]{1,0:T(8,128)(2,1)S(1)}, bf16[512,256]{1,0:T(8,128)(2,1)}, u32[]{:S(2)}) copy-start(bf16[512,256]{1,0:T(8,128)(2,1)} %param.19) | copy-start | bytes 786436
  5.1 34.2 %copy-start.6 = (bf16[512,256]{1,0:T(8,128)(2,1)S(1)}, bf16[512,256]{1,0:T(8,128)(2,1)}, u32[]{:S(2)}) copy-start(bf16[512,256]{1,0:T(8,128)(2,1)} %param.20) | copy-start | bytes 786436
  5.1 39.7 %all-to-all-start = ((bf16[32,6,512]{2,1,0:T(8,128)(2,1)}), bf16[32,6,512]{2,1,0:T(8,128)(2,1)S(1)}, u32[]{:S(2)}, u32[]{:S(2)}) async-start(bf16[32,6,512]{2,1,0:T(8,128)(2,1)} %broadcast_in_dim.18), calls=%async_computation | async-start | bytes 524288 | tf_op jit(solution)/shard_map/all_to_all | solution.py:20
  22.0 19.7 %collective-permute-start.5 = (bf16[128,512]{1,0:T(8,128)(2,1)S(1)}, bf16[128,512]{1,0:T(8,128)(2,1)S(1)}, u32[]{:S(2)}, u32[]{:S(2)}) collective-permute-start(bf16[128,512]{1,0:T(8,128)(2,1)S(1)} %maximum_select_fusion), channel_id=1, source_target_pairs={{48,0},{0,16},{16,32},{32,48},{49,1},{1,17},{17,33},{33,49},{50,2}... | collective-permute-start | bytes 393224 | tf_op jit(solution)/shard_map/ppermute | solution.py:34
  26.3 18.5 %collective-permute-start.4 = (bf16[128,512]{1,0:T(8,128)(2,1)S(1)}, bf16[128,512]{1,0:T(8,128)(2,1)S(1)}, u32[]{:S(2)}, u32[]{:S(2)}) collective-permute-start(bf16[128,512]{1,0:T(8,128)(2,1)S(1)} %maximum_select_fusion), channel_id=1, source_target_pairs={{32,0},{48,16},{0,32},{16,48},{33,1},{49,17},{1,33},{17,49},{34,2}... | collective-permute-start | bytes 393224 | tf_op jit(solution)/shard_map/ppermute | solution.py:34
  31.9 12.9 %collective-permute-start.3 = (bf16[128,512]{1,0:T(8,128)(2,1)S(1)}, bf16[128,512]{1,0:T(8,128)(2,1)S(1)}, u32[]{:S(2)}, u32[]{:S(2)}) collective-permute-start(bf16[128,512]{1,0:T(8,128)(2,1)S(1)} %maximum_select_fusion), channel_id=1, source_target_pairs={{16,0},{32,16},{48,32},{0,48},{17,1},{33,17},{49,33},{1,49},{18,2}... | collective-permute-start | bytes 393224 | tf_op jit(solution)/shard_map/ppermute | solution.py:34
  37.3 8.0 %collective-permute-start.1 = (bf16[512,256]{1,0:T(8,128)(2,1)S(1)}, bf16[512,256]{1,0:T(8,128)(2,1)S(1)}, u32[]{:S(2)}, u32[]{:S(2)}) collective-permute-start(bf16[512,256]{1,0:T(8,128)(2,1)S(1)} %copy-done.5), channel_id=1, source_target_pairs={{0,1},{1,0},{2,3},{3,2},{4,5},{5,4},{6,7},{7,6},{8,9},{9,8},{10,11... | collective-permute-start | bytes 786440 | tf_op jit(solution)/shard_map/ppermute | solution.py:29
  39.3 6.3 %collective-permute-start.2 = (bf16[512,256]{1,0:T(8,128)(2,1)S(1)}, bf16[512,256]{1,0:T(8,128)(2,1)S(1)}, u32[]{:S(2)}, u32[]{:S(2)}) collective-permute-start(bf16[512,256]{1,0:T(8,128)(2,1)S(1)} %copy-done.6), channel_id=1, source_target_pairs={{0,1},{1,0},{2,3},{3,2},{4,5},{5,4},{6,7},{7,6},{8,9},{9,8},{10,11... | collective-permute-start | bytes 786440 | tf_op jit(solution)/shard_map/ppermute | solution.py:29
  46.6 28.3 %all-to-all-start.1 = ((bf16[8,24,1024]{2,1,0:T(8,128)(2,1)}), bf16[8,24,1024]{2,1,0:T(8,128)(2,1)S(1)}, u32[]{:S(2)}, u32[]{:S(2)}) async-start(bf16[8,24,1024]{2,1,0:T(8,128)(2,1)} %bitcast.7), calls=%async_computation.1 | async-start | bytes 786432 | tf_op jit(solution)/shard_map/all_to_all | solution.py:20
  60.2 18.7 %collective-permute-start.7 = (bf16[4,128,512]{2,1,0:T(8,128)(2,1)S(1)}, bf16[4,128,512]{2,1,0:T(8,128)(2,1)S(1)}, u32[]{:S(2)}, u32[]{:S(2)}) collective-permute-start(bf16[4,128,512]{2,1,0:T(8,128)(2,1)S(1)} %pad_maximum_fusion.refs_0_), channel_id=1, source_target_pairs={{0,4},{1,13},{2,6},{3,15},{4,8},{5,1},{6,10},{7,3},{8,12},{9,5},{1... | collective-permute-start | bytes 1572872 | tf_op jit(solution)/shard_map/ppermute | solution.py:43
  64.6 18.7 %collective-permute-start.6 = (bf16[4,128,512]{2,1,0:T(8,128)(2,1)S(1)}, bf16[4,128,512]{2,1,0:T(8,128)(2,1)S(1)}, u32[]{:S(2)}, u32[]{:S(2)}) collective-permute-start(bf16[4,128,512]{2,1,0:T(8,128)(2,1)S(1)} %pad_maximum_fusion.refs_0_), channel_id=1, source_target_pairs={{0,2},{1,15},{2,4},{3,1},{4,6},{5,3},{6,8},{7,5},{8,10},{9,7},{10,... | collective-permute-start | bytes 1572872 | tf_op jit(solution)/shard_map/ppermute | solution.py:43
  75.0 16.3 %copy-start.4 = (bf16[256,512]{1,0:T(8,128)(2,1)S(1)}, bf16[256,512]{1,0:T(8,128)(2,1)}, u32[]{:S(2)}) copy-start(bf16[256,512]{1,0:T(8,128)(2,1)} %param.21) | copy-start | bytes 786436
  84.1 17.0 %all-to-all-start.2 = ((bf16[8,24,512]{2,1,0:T(8,128)(2,1)}), bf16[8,24,512]{2,1,0:T(8,128)(2,1)S(1)}, u32[]{:S(2)}, u32[]{:S(2)}) async-start(bf16[8,24,512]{2,1,0:T(8,128)(2,1)} %broadcast_in_dim.19), calls=%async_computation.2 | async-start | bytes 393216 | tf_op jit(solution)/shard_map/all_to_all | solution.py:20
  91.3 10.0 %collective-permute-start.8 = (bf16[256,512]{1,0:T(8,128)(2,1)S(1)}, bf16[256,512]{1,0:T(8,128)(2,1)S(1)}, u32[]{:S(2)}, u32[]{:S(2)}) collective-permute-start(bf16[256,512]{1,0:T(8,128)(2,1)S(1)} %copy-done.4), channel_id=1, source_target_pairs={{0,1},{1,0},{2,3},{3,2},{4,5},{5,4},{6,7},{7,6},{8,9},{9,8},{10,11... | collective-permute-start | bytes 786440 | tf_op jit(solution)/shard_map/ppermute | solution.py:29
  93.2 37.5 %collective-permute-start.9 = (bf16[4,128,512]{2,1,0:T(8,128)(2,1)S(1)}, bf16[4,128,512]{2,1,0:T(8,128)(2,1)S(1)}, u32[]{:S(2)}, u32[]{:S(2)}) collective-permute-start(bf16[4,128,512]{2,1,0:T(8,128)(2,1)S(1)} %collective-permute-done.6.refs_1_), channel_id=1, source_target_pairs={{0,4},{1,13},{2,6},{3,15},{4,8},{5,1},{6,10},{7,3},{8,12},{9,5},{1... | collective-permute-start | bytes 1572872 | tf_op jit(solution)/shard_map/ppermute | solution.py:43
  102.3 43.6 %copy-start = (bf16[128,4096]{1,0:T(8,128)(2,1)S(1)}, bf16[128,4096]{1,0:T(8,128)(2,1)}, u32[]{:S(2)}) copy-start(bf16[128,4096]{1,0:T(8,128)(2,1)} %tokens_ref.1) | copy-start | bytes 3145732
  102.3 27.4 %all-to-all-start.3 = ((bf16[32,6,512]{2,1,0:T(8,128)(2,1)}), bf16[32,6,512]{2,1,0:T(8,128)(2,1)}, u32[]{:S(2)}, u32[]{:S(2)}) async-start(bf16[32,6,512]{2,1,0:T(8,128)(2,1)} %reshape.26), calls=%async_computation.3 | async-start | bytes 524288 | tf_op jit(solution)/shard_map/all_to_all | solution.py:20
  114.5 16.2 %collective-permute-start.10 = (bf16[2,128,512]{2,1,0:T(8,128)(2,1)}, bf16[2,128,512]{2,1,0:T(8,128)(2,1)S(1)}, u32[]{:S(2)}, u32[]{:S(2)}) collective-permute-start(bf16[2,128,512]{2,1,0:T(8,128)(2,1)} %constant_dynamic-slice_fusion), channel_id=1, source_target_pairs={{0,4},{1,13},{2,6},{3,15},{4,8},{5,1},{6,10},{7,3},{8,12},{9,5},{1... | collective-permute-start | bytes 786440 | tf_op jit(solution)/shard_map/ppermute | solution.py:43
  118.7 21.0 %collective-permute-start.11 = (bf16[4,128,512]{2,1,0:T(8,128)(2,1)S(1)}, bf16[4,128,512]{2,1,0:T(8,128)(2,1)}, u32[]{:S(2)}, u32[]{:S(2)}) collective-permute-start(bf16[4,128,512]{2,1,0:T(8,128)(2,1)S(1)} %collective-permute-done.6.refs_1_), channel_id=1, source_target_pairs={{0,1},{1,0},{2,3},{3,2},{4,5},{5,4},{6,7},{7,6},{8,9},{9,8},{10,11... | collective-permute-start | bytes 1572872 | tf_op jit(solution)/shard_map/ppermute | solution.py:29
  120.7 19.1 %collective-permute-start.12 = (bf16[4,128,512]{2,1,0:T(8,128)(2,1)S(1)}, bf16[4,128,512]{2,1,0:T(8,128)(2,1)}, u32[]{:S(2)}, u32[]{:S(2)}) collective-permute-start(bf16[4,128,512]{2,1,0:T(8,128)(2,1)S(1)} %collective-permute-done.7.refs_2_), channel_id=1, source_target_pairs={{0,1},{1,0},{2,3},{3,2},{4,5},{5,4},{6,7},{7,6},{8,9},{9,8},{10,11... | collective-permute-start | bytes 1572872 | tf_op jit(solution)/shard_map/ppermute | solution.py:29
  130.7 2.0 %copy-start.1 = (bf16[2,128,512]{2,1,0:T(8,128)(2,1)}, bf16[2,128,512]{2,1,0:T(8,128)(2,1)S(1)}, u32[]{:S(2)}) copy-start(bf16[2,128,512]{2,1,0:T(8,128)(2,1)S(1)} %collective-permute-done.10.refs_4_) | copy-start | bytes 786436
  130.7 15.1 %collective-permute-start.13 = (bf16[4,128,512]{2,1,0:T(8,128)(2,1)S(1)}, bf16[4,128,512]{2,1,0:T(8,128)(2,1)}, u32[]{:S(2)}, u32[]{:S(2)}) collective-permute-start(bf16[4,128,512]{2,1,0:T(8,128)(2,1)S(1)} %collective-permute-done.9.refs_3_), channel_id=1, source_target_pairs={{0,1},{1,0},{2,3},{3,2},{4,5},{5,4},{6,7},{7,6},{8,9},{9,8},{10,11... | collective-permute-start | bytes 1572872 | tf_op jit(solution)/shard_map/ppermute | solution.py:29
  133.4 6.1 %copy-start.12 = (f32[128]{0:T(128)S(1)}, f32[128]{0:T(128)}, u32[]{:S(2)}) copy-start(f32[128]{0:T(128)} %param.17) | copy-start | bytes 1540
  133.4 6.1 %copy-start.13 = (f32[128]{0:T(128)S(1)}, f32[128]{0:T(128)}, u32[]{:S(2)}) copy-start(f32[128]{0:T(128)} %param.18) | copy-start | bytes 1540
  133.5 12.4 %all-to-all-start.4 = ((bf16[16,8,512]{2,1,0:T(8,128)(2,1)}), bf16[16,8,512]{2,1,0:T(8,128)(2,1)S(1)}, u32[]{:S(2)}, u32[]{:S(2)}) async-start(bf16[16,8,512]{2,1,0:T(8,128)(2,1)} %broadcast_in_dim.38), calls=%async_computation.4 | async-start | bytes 262144 | tf_op jit(solution)/shard_map/all_to_all | solution.py:20
  137.1 8.7 %collective-permute-start.14 = (bf16[2,128,512]{2,1,0:T(8,128)(2,1)}, bf16[2,128,512]{2,1,0:T(8,128)(2,1)}, u32[]{:S(2)}, u32[]{:S(2)}) collective-permute-start(bf16[2,128,512]{2,1,0:T(8,128)(2,1)} %copy-done.1), channel_id=1, source_target_pairs={{0,1},{1,0},{2,3},{3,2},{4,5},{5,4},{6,7},{7,6},{8,9},{9,8},{10,11... | collective-permute-start | bytes 786440 | tf_op jit(solution)/shard_map/ppermute | solution.py:29
  139.6 6.3 %copy-start.3 = (f32[4096]{0:T(1024)S(1)}, f32[4096]{0:T(1024)}, u32[]{:S(2)}) copy-start(f32[4096]{0:T(1024)} %param.22) | copy-start | bytes 49156
  145.8 1.0 copy-start.2

commit v3 on v2

v3 whole, which is shorter than its diff:
```python
import jax
import jax.numpy as jnp
from jax import lax
from jax.experimental import pallas as pl
from jax.experimental.pallas import tpu as pltpu
from jax.sharding import Mesh, PartitionSpec as P

CAP1 = 4
CAP2 = 2
SLOTS = CAP1 + CAP2
EXPERT = ("y_lo", "z")
CHIPS = ("y_hi", "x")
DP = ("y_hi", "x", "core")
SIZES = {"y_lo": 2, "z": 8, "y_hi": 4, "x": 8, "core": 2}
PADDED = 8
LANES = 128


def exchange(blocks, axes):
    return lax.all_to_all(blocks, axes, split_axis=0, concat_axis=0, tiled=True)


def spread(block, axes):
    count = lax.axis_size(axes)
    return exchange(jnp.broadcast_to(block[None], (count,) + block.shape), axes)


def other_core(block):
    return lax.ppermute(block, "core", [(0, 1), (1, 0)])


def pack(rows):
    lead, (count, width) = rows.shape[:-2], rows.shape[-2:]
    rows = jnp.pad(rows, [(0, 0)] * len(lead) + [(0, PADDED - count), (0, 0)])
    rows = jnp.moveaxis(rows.reshape(lead + (PADDED, width // LANES, LANES)), -2, -3)
    return rows.reshape(lead + (PADDED * width // LANES, LANES))


def finish_kernel(
    core_ref, tokens_ref, table_ref, column_ref, gate_ref, gain_ref, a_ref, b_ref, a_other_ref, b_other_ref,
    mixed_ref, query_ref, normed_ref,
):
    core = core_ref[0]
    experts = 2
    blocks = table_ref.shape[0] // experts
    packed = table_ref.shape[1]
    groups = packed // PADDED
    tok_count, width = tokens_ref.shape
    block_width = width // blocks
    column = column_ref[...]
    slots = lax.broadcasted_iota(jnp.int32, (tok_count, PADDED), 1)
    hot = [(column == slots + e * PADDED).astype(jnp.bfloat16) for e in range(experts)]
    gate = gate_ref[...]
    square = jnp.zeros((tok_count, LANES), jnp.float32)
    for z in range(blocks):
        cols = pl.ds(z * block_width, block_width)
        picked = jnp.zeros((tok_count, block_width), jnp.float32)
        for e in range(experts):
            rows = [table_ref[e * blocks + z, pl.ds(g * PADDED, PADDED), :] for g in range(groups)]
            picked += jnp.dot(hot[e], jnp.concatenate(rows, axis=1), preferred_element_type=jnp.float32)
        mixed = (tokens_ref[:, cols].astype(jnp.float32) + gate * picked).astype(jnp.bfloat16)
        mixed_ref[:, cols] = mixed
        values = mixed.astype(jnp.float32)
        for i in range(block_width // LANES):
            part = values[:, i * LANES : (i + 1) * LANES]
            square += part * part
    mean = jnp.sum(square, axis=1, keepdims=True) * (1.0 / width)
    scale = lax.rsqrt(mean + 1e-05)
    for z in range(blocks):
        cols = pl.ds(z * block_width, block_width)
        values = mixed_ref[:, cols].astype(jnp.float32)
        normed_ref[:, cols] = (values * scale * gain_ref[:, cols]).astype(jnp.bfloat16)

    def product(w_ref):
        w = w_ref[:, pl.ds(packed, w_ref.shape[1] - packed), :].reshape(width, LANES)
        return jnp.dot(normed_ref[...], w, preferred_element_type=jnp.float32)

    own = jnp.concatenate([product(a_ref), product(b_ref)], axis=1).astype(query_ref.dtype)
    other = jnp.concatenate([product(a_other_ref), product(b_other_ref)], axis=1).astype(query_ref.dtype)
    half = own.shape[1]
    query_ref[:, pl.ds(0, half)] = jnp.where(core == 0, own, other)
    query_ref[:, pl.ds(half, half)] = jnp.where(core == 0, other, own)


def finish(core, tokens, table, column, gate, gain, weights):
    vmem = pl.BlockSpec(memory_space=pltpu.VMEM)
    tok_count, width = tokens.shape
    columns = len(weights) * LANES
    return pl.pallas_call(
        finish_kernel,
        out_shape=(
            jax.ShapeDtypeStruct((tok_count, width), jnp.bfloat16),
            jax.ShapeDtypeStruct((tok_count, columns), jnp.bfloat16),
        ),
        in_specs=[pl.BlockSpec(memory_space=pltpu.SMEM)] + [vmem] * (5 + len(weights)),
        out_specs=(vmem, vmem),
        scratch_shapes=[pltpu.VMEM((tok_count, width), jnp.bfloat16)],
        compiler_params=pltpu.CompilerParams(vmem_limit_bytes=24 * 1024 * 1024),
        cost_estimate=pl.CostEstimate(
            flops=2 * tok_count * width * columns, bytes_accessed=4 * width * columns, transcendentals=0
        ),
    )(core[None], tokens, table, column[:, None], gate[:, None], gain[None, :], *weights)


def local(
    tokens,
    first_expert,
    first_slot,
    second_expert,
    second_slot,
    first_gate,
    second_gate,
    w_gate,
    w_up,
    w_down,
    norm_gain,
    w_query,
):
    tok_count, width = tokens.shape
    blocks = lax.axis_size("z")
    chips = lax.axis_size(CHIPS)
    block_width = width // blocks
    units = w_gate.shape[1]
    own_expert = lax.axis_index("y_lo")
    own_block = lax.axis_index("z")
    core = lax.axis_index("core")

    served_first = first_slot >= 0
    served = served_first | (second_slot >= 0)
    expert_of = jnp.where(served_first, first_expert, second_expert)
    slot_of = jnp.where(served_first, first_slot, second_slot + CAP1)
    gate_of = jnp.where(served_first, first_gate, second_gate)

    token_block = lax.dynamic_slice_in_dim(tokens, own_block * block_width, block_width, 1)
    placement = jnp.where(served & (expert_of == own_expert), slot_of, -1)
    slot_hot = (jnp.arange(SLOTS, dtype=jnp.int32)[:, None] == placement[None, :]).astype(jnp.bfloat16)
    slot_rows = jnp.dot(slot_hot, token_block, preferred_element_type=jnp.float32).astype(jnp.bfloat16)

    half = w_query.shape[1] // 2
    own_cols = lax.dynamic_slice_in_dim(w_query, core * half, half, 1)
    came = other_core(lax.dynamic_slice_in_dim(w_query, (1 - core) * half, half, 1))
    pair = jnp.where(core == 0, jnp.concatenate([own_cols, came], 0), jnp.concatenate([came, own_cols], 0))
    w_a, w_b = pair[:, :LANES], pair[:, LANES:]

    packed = PADDED * block_width // LANES
    query_a = spread(jnp.concatenate([pack(slot_rows), w_a], 0), CHIPS)
    w_gate_other = other_core(w_gate)
    w_up_other = other_core(w_up)
    query_a_other = other_core(query_a)
    rows = query_a[:, :packed].reshape(chips, -1, PADDED, LANES)[:, :, :SLOTS]
    rows = jnp.moveaxis(rows, 1, 2).reshape(chips * SLOTS, block_width)

    partial = jnp.concatenate(
        [
            jnp.dot(rows, w, preferred_element_type=jnp.float32).astype(jnp.bfloat16)
            for w in (w_gate, w_gate_other, w_up, w_up_other)
        ],
        axis=1,
    )
    share = chips * SLOTS // blocks
    summed = exchange(partial.reshape(blocks, share, 4 * units), "z")
    summed = jnp.sum(summed.astype(jnp.float32), axis=0)
    hidden_share = (jax.nn.silu(summed[:, : 2 * units]) * summed[:, 2 * units :]).astype(jnp.bfloat16)
    hidden = spread(hidden_share, "z").reshape(chips * SLOTS, 2 * units)
    w_down_other = other_core(w_down)
    out_part = jnp.dot(hidden[:, :units], w_down, preferred_element_type=jnp.float32) + jnp.dot(
        hidden[:, units:], w_down_other, preferred_element_type=jnp.float32
    )
    out_part = pack(out_part.astype(jnp.bfloat16).reshape(chips, SLOTS, block_width))
    query_b = exchange(
        jnp.concatenate([out_part, jnp.broadcast_to(w_b[None], (chips,) + w_b.shape)], 1), CHIPS
    )
    query_b_other = other_core(query_b)
    expert_out = jnp.sum(query_b[:, :packed].astype(jnp.float32), axis=0).astype(jnp.bfloat16)
    table = spread(expert_out, EXPERT)

    column = jnp.where(served, expert_of * PADDED + slot_of, -1)
    return finish(
        core, tokens, table, column, gate_of, norm_gain, [query_a, query_b, query_a_other, query_b_other]
    )


def solution(mesh):
    fine = Mesh(mesh.devices.reshape(tuple(SIZES.values())), tuple(SIZES))
    in_specs = (
        P(DP, None),
        P(DP),
        P(DP),
        P(DP),
        P(DP),
        P(DP),
        P(DP),
        P(EXPERT, DP),
        P(EXPERT, DP),
        P(DP, EXPERT),
        P(),
        P(DP, EXPERT),
    )
    out_specs = (P(DP, None), P(DP, EXPERT))
    return jax.shard_map(local, mesh=fine, in_specs=in_specs, out_specs=out_specs, check_vma=False)
```

time: 152 us -> 169 us (1.11)
  the two profiles are of different devices: /device:TPU:2 before, /device:TPU:6 now
where the time goes in v3:
time: 169 us; the launch traced here: 168 us
  waiting for transfers between devices  80.4 us (48%)
  starting transfers between devices  46.7 us (28%)
  blocking collectives  26 us (15%)
  local copies, waits for them, and re-layouts  5.35 us (3%)
  Pallas kernels  4.48 us (3%)
  matrix products  2.28 us (1%)
  other arithmetic  2.07 us (1%)
    all_to_all x4, waiting for transfers between devices, exchange(): return lax.all_to_all(blocks, axes, split_axis=0, concat_axis=0, tiled=True)  80.4 us
    all_to_all x4, starting transfers between devices, exchange(): return lax.all_to_all(blocks, axes, split_axis=0, concat_axis=0, tiled=True)  34.7 us
    all_to_all x1, blocking collectives, exchange(): return lax.all_to_all(blocks, axes, split_axis=0, concat_axis=0, tiled=True)  26 us
    ppermute x6, starting transfers between devices, other_core(): return lax.ppermute(block, 'core', [(0, 1), (1, 0)])  12 us
    pallas_call x1, Pallas kernels, finish(): pl.pallas_call(finish_kernel, out_shape=(jax.ShapeDtypeStruct((tok_count,...  4.48 us
  transfers between devices with their start and end apart: 10, of which 4 were waited for; matrix products, arithmetic and copies ran while one was open for 2% of the time, Pallas kernels for 0%

profile of v3, /device:TPU:6, one launch (start us, length us, event | category | flops | bytes accessed | tf_op | source)
XLA Modules:
  0.0 168.2 jit_solution(2249856148822488418)
XLA Ops:
  0.6 0.8 constant_dynamic-slice_fusion.1
  1.4 1.9 %collective-permute-start = (bf16[64,256]{1,0:T(8,128)(2,1)S(1)}, bf16[64,256]{1,0:T(8,128)(2,1)S(1)}, u32[]{:S(2)}, u32[]{:S(2)}) collective-permute-start(bf16[64,256]{1,0:T(8,128)(2,1)S(1)} %get-tuple-element.5), channel_id=1, source_target_pairs={{0,1},{1,0},{2,3},{3,2},{4,5},{5,4},{6,7},{7,6},{8,9},{9,8},{10,11... | collective-permute-start | bytes 98312 | tf_op jit(solution)/shard_map/ppermute | solution.py:29
  3.3 0.7 select_bitcast_fusion.1
  4.1 1.0 convolution_convert_fusion.4
  5.1 0.0 collective-permute-done
  5.2 1.3 broadcast_in_dim.23
  6.4 16.9 %all-to-all-start = ((bf16[32,160,128]{2,1,0:T(8,128)(2,1)}), bf16[32,160,128]{2,1,0:T(8,128)(2,1)S(1)}, u32[]{:S(2)}, u32[]{:S(2)}) async-start(bf16[32,160,128]{2,1,0:T(8,128)(2,1)} %broadcast_in_dim.23), calls=%async_computation | async-start | bytes 2621440 | tf_op jit(solution)/shard_map/all_to_all | solution.py:20
  23.3 0.0 copy-done.4
  23.3 2.1 %collective-permute-start.1 = (bf16[512,256]{1,0:T(8,128)(2,1)S(1)}, bf16[512,256]{1,0:T(8,128)(2,1)S(1)}, u32[]{:S(2)}, u32[]{:S(2)}) collective-permute-start(bf16[512,256]{1,0:T(8,128)(2,1)S(1)} %copy-done.4), channel_id=1, source_target_pairs={{0,1},{1,0},{2,3},{3,2},{4,5},{5,4},{6,7},{7,6},{8,9},{9,8},{10,11... | collective-permute-start | bytes 786440 | tf_op jit(solution)/shard_map/ppermute | solution.py:29
  25.4 0.0 copy-done.3
  25.5 2.2 %collective-permute-start.2 = (bf16[512,256]{1,0:T(8,128)(2,1)S(1)}, bf16[512,256]{1,0:T(8,128)(2,1)S(1)}, u32[]{:S(2)}, u32[]{:S(2)}) collective-permute-start(bf16[512,256]{1,0:T(8,128)(2,1)S(1)} %copy-done.3), channel_id=1, source_target_pairs={{0,1},{1,0},{2,3},{3,2},{4,5},{5,4},{6,7},{7,6},{8,9},{9,8},{10,11... | collective-permute-start | bytes 786440 | tf_op jit(solution)/shard_map/ppermute | solution.py:29
  27.7 32.7 %all-to-all-done.a_ref = bf16[32,160,128]{2,1,0:T(8,128)(2,1)S(1)} async-done(((bf16[32,160,128]{2,1,0:T(8,128)(2,1)}), bf16[32,160,128]{2,1,0:T(8,128)(2,1)S(1)}, u32[]{:S(2)}, u32[]{:S(2)}) %all-to-all-start) | async-done | bytes 1310752 | tf_op jit(solution)/shard_map/all_to_all | solution.py:20
  60.4 0.1 copy.19
  60.5 0.2 convolution_convert_fusion.1
  60.7 0.2 convolution_convert_fusion.3
  60.9 0.0 collective-permute-done.2
  61.0 0.2 convolution_convert_fusion
  61.2 0.0 collective-permute-done.1
  61.2 0.2 convolution_convert_fusion.2
  61.4 0.0 copy-start.2
  61.5 26.0 %all_to_all.25 = bf16[8,24,1024]{2,1,0:T(8,128)(2,1)S(1)} all-to-all(bf16[8,24,1024]{2,1,0:T(8,128)(2,1)S(1)} %bitcast.46), channel_id=1, replica_groups=mesh['y_lo'=2,'z'=8,'y_hi'=4,'x'=8,'core'=2] {'z'}, dimensions={0} | all-to-all | bytes 786432 | tf_op jit(solution)/shard_map/all_to_all | solution.py:20
  87.4 0.1 convert_reduce_fusion
  87.5 0.7 broadcast_in_dim.46
  88.2 3.4 %all-to-all-start.2 = ((bf16[8,24,512]{2,1,0:T(8,128)(2,1)}), bf16[8,24,512]{2,1,0:T(8,128)(2,1)S(1)}, u32[]{:S(2)}, u32[]{:S(2)}) async-start(bf16[8,24,512]{2,1,0:T(8,128)(2,1)} %broadcast_in_dim.46), calls=%async_computation.2 | async-start | bytes 393216 | tf_op jit(solution)/shard_map/all_to_all | solution.py:20
  91.6 0.0 copy-done.2
  91.6 1.9 %collective-permute-start.3 = (bf16[256,512]{1,0:T(8,128)(2,1)S(1)}, bf16[256,512]{1,0:T(8,128)(2,1)S(1)}, u32[]{:S(2)}, u32[]{:S(2)}) collective-permute-start(bf16[256,512]{1,0:T(8,128)(2,1)S(1)} %copy-done.2), channel_id=1, source_target_pairs={{0,1},{1,0},{2,3},{3,2},{4,5},{5,4},{6,7},{7,6},{8,9},{9,8},{10,11... | collective-permute-start | bytes 786440 | tf_op jit(solution)/shard_map/ppermute | solution.py:29
  93.6 7.7 %all-to-all-done.2 = bf16[8,24,512]{2,1,0:T(8,128)(2,1)S(1)} async-done(((bf16[8,24,512]{2,1,0:T(8,128)(2,1)}), bf16[8,24,512]{2,1,0:T(8,128)(2,1)S(1)}, u32[]{:S(2)}, u32[]{:S(2)}) %all-to-all-start.2) | async-done | bytes 196640 | tf_op jit(solution)/shard_map/all_to_all | solution.py:20
  101.3 0.2 fusion.11
  101.5 0.0 collective-permute-done.3
  101.5 0.2 fusion
  101.7 0.1 reshape.42
  101.8 0.1 pad_bitcast_fusion
  101.9 0.2 broadcast_in_dim.47
  102.1 1.2 pad_maximum_fusion
  103.3 9.1 %all-to-all-start.3 = ((bf16[32,160,128]{2,1,0:T(8,128)(2,1)}), bf16[32,160,128]{2,1,0:T(8,128)(2,1)S(1)}, u32[]{:S(2)}, u32[]{:S(2)}) async-start(bf16[32,160,128]{2,1,0:T(8,128)(2,1)} %pad_maximum_fusion), calls=%async_computation.3 | async-start | bytes 2621440 | tf_op jit(solution)/shard_map/all_to_all | solution.py:20
  112.4 1.9 %collective-permute-start.4 = (bf16[32,160,128]{2,1,0:T(8,128)(2,1)S(1)}, bf16[32,160,128]{2,1,0:T(8,128)(2,1)}, u32[]{:S(2)}, u32[]{:S(2)}) collective-permute-start(bf16[32,160,128]{2,1,0:T(8,128)(2,1)S(1)} %all-to-all-done.a_ref), channel_id=1, source_target_pairs={{0,1},{1,0},{2,3},{3,2},{4,5},{5,4},{6,7},{7,6},{8,9},{9,8},{10,11... | collective-permute-start | bytes 3932168 | tf_op jit(solution)/shard_map/ppermute | solution.py:29
  114.4 31.5 %all-to-all-done.3.b_ref = bf16[32,160,128]{2,1,0:T(8,128)(2,1)S(1)} async-done(((bf16[32,160,128]{2,1,0:T(8,128)(2,1)}), bf16[32,160,128]{2,1,0:T(8,128)(2,1)S(1)}, u32[]{:S(2)}, u32[]{:S(2)}) %all-to-all-start.3) | async-done | bytes 1310752 | tf_op jit(solution)/shard_map/all_to_all | solution.py:20
  145.8 1.9 %collective-permute-start.5 = (bf16[32,160,128]{2,1,0:T(8,128)(2,1)S(1)}, bf16[32,160,128]{2,1,0:T(8,128)(2,1)}, u32[]{:S(2)}, u32[]{:S(2)}) collective-permute-start(bf16[32,160,128]{2,1,0:T(8,128)(2,1)S(1)} %all-to-all-done.3.b_ref), channel_id=1, source_target_pairs={{0,1},{1,0},{2,3},{3,2},{4,5},{5,4},{6,7},{7,6},{8,9},{9,8},{10,11... | collective-permute-start | bytes 3932168 | tf_op jit(solution)/shard_map/ppermute | solution.py:29
  147.8 0.1 slice_reduce_fusion
  147.8 0.7 broadcast_in_dim.48
  148.5 5.4 %all-to-all-start.4 = ((bf16[16,32,128]{2,1,0:T(8,128)(2,1)}), bf16[16,32,128]{2,1,0:T(8,128)(2,1)S(1)}, u32[]{:S(2)}, u32[]{:S(2)}) async-start(bf16[16,32,128]{2,1,0:T(8,128)(2,1)} %broadcast_in_dim.48), calls=%async_computation.4 | async-start | bytes 262144 | tf_op jit(solution)/shard_map/all_to_all | solution.py:20
  153.8 0.1 copy.17.column_ref
  154.0 0.1 copy.18.gate_ref
  154.1 0.0 collective-permute-done.4.a_other_ref
  154.1 8.4 %all-to-all-done.4.table_ref = bf16[16,32,128]{2,1,0:T(8,128)(2,1)S(1)} async-done(((bf16[16,32,128]{2,1,0:T(8,128)(2,1)}), bf16[16,32,128]{2,1,0:T(8,128)(2,1)S(1)}, u32[]{:S(2)}, u32[]{:S(2)}) %all-to-all-start.4) | async-done | bytes 131104 | tf_op jit(solution)/shard_map/all_to_all | solution.py:20
  162.5 0.0 collective-permute-done.5.b_other_ref
  162.5 1.2 copy-done
  163.8 4.5 %shard_map.131 = (bf16[128,4096]{1,0:T(8,128)(2,1)}, bf16[128,512]{1,0:T(8,128)(2,1)}) custom-call(s32[1]{0:T(128)} %bitcast.core_ref, bf16[128,4096]{1,0:T(8,128)(2,1)S(1)} %copy-done, bf16[16,32,128]{2,1,0:T(8,128)(2,1)S(1)} %all-to-all-done.4.table_ref, s32[128,1]{1,0:T(8,128)S(1)} %copy.17.column_ref, f32[128,1]{1,0:T(8,128)S(1)} %copy.18.gate_ref, ...), custom_call_target="tpu_custom_call" | custom-call | flops 536870912 | bytes 8388608 | tf_op jit(solution)/shard_map/pallas_call | solution.py:89
  (19 shorter events, 0.1 us)
Async XLA Ops:
  1.4 3.7 %collective-permute-start = (bf16[64,256]{1,0:T(8,128)(2,1)S(1)}, bf16[64,256]{1,0:T(8,128)(2,1)S(1)}, u32[]{:S(2)}, u32[]{:S(2)}) collective-permute-start(bf16[64,256]{1,0:T(8,128)(2,1)S(1)} %get-tuple-element.5), channel_id=1, source_target_pairs={{0,1},{1,0},{2,3},{3,2},{4,5},{5,4},{6,7},{7,6},{8,9},{9,8},{10,11... | collective-permute-start | bytes 98312 | tf_op jit(solution)/shard_map/ppermute | solution.py:29
  6.4 16.9 %copy-start.4 = (bf16[512,256]{1,0:T(8,128)(2,1)S(1)}, bf16[512,256]{1,0:T(8,128)(2,1)}, u32[]{:S(2)}) copy-start(bf16[512,256]{1,0:T(8,128)(2,1)} %param.19) | copy-start | bytes 786436
  6.4 19.0 %copy-start.3 = (bf16[512,256]{1,0:T(8,128)(2,1)S(1)}, bf16[512,256]{1,0:T(8,128)(2,1)}, u32[]{:S(2)}) copy-start(bf16[512,256]{1,0:T(8,128)(2,1)} %param.20) | copy-start | bytes 786436
  6.4 54.0 %all-to-all-start = ((bf16[32,160,128]{2,1,0:T(8,128)(2,1)}), bf16[32,160,128]{2,1,0:T(8,128)(2,1)S(1)}, u32[]{:S(2)}, u32[]{:S(2)}) async-start(bf16[32,160,128]{2,1,0:T(8,128)(2,1)} %broadcast_in_dim.23), calls=%async_computation | async-start | bytes 2621440 | tf_op jit(solution)/shard_map/all_to_all | solution.py:20
  23.3 37.9 %collective-permute-start.1 = (bf16[512,256]{1,0:T(8,128)(2,1)S(1)}, bf16[512,256]{1,0:T(8,128)(2,1)S(1)}, u32[]{:S(2)}, u32[]{:S(2)}) collective-permute-start(bf16[512,256]{1,0:T(8,128)(2,1)S(1)} %copy-done.4), channel_id=1, source_target_pairs={{0,1},{1,0},{2,3},{3,2},{4,5},{5,4},{6,7},{7,6},{8,9},{9,8},{10,11... | collective-permute-start | bytes 786440 | tf_op jit(solution)/shard_map/ppermute | solution.py:29
  25.5 35.5 %collective-permute-start.2 = (bf16[512,256]{1,0:T(8,128)(2,1)S(1)}, bf16[512,256]{1,0:T(8,128)(2,1)S(1)}, u32[]{:S(2)}, u32[]{:S(2)}) collective-permute-start(bf16[512,256]{1,0:T(8,128)(2,1)S(1)} %copy-done.3), channel_id=1, source_target_pairs={{0,1},{1,0},{2,3},{3,2},{4,5},{5,4},{6,7},{7,6},{8,9},{9,8},{10,11... | collective-permute-start | bytes 786440 | tf_op jit(solution)/shard_map/ppermute | solution.py:29
  61.4 30.2 %copy-start.2 = (bf16[256,512]{1,0:T(8,128)(2,1)S(1)}, bf16[256,512]{1,0:T(8,128)(2,1)}, u32[]{:S(2)}) copy-start(bf16[256,512]{1,0:T(8,128)(2,1)} %param.21) | copy-start | bytes 786436
  88.2 13.1 %all-to-all-start.2 = ((bf16[8,24,512]{2,1,0:T(8,128)(2,1)}), bf16[8,24,512]{2,1,0:T(8,128)(2,1)S(1)}, u32[]{:S(2)}, u32[]{:S(2)}) async-start(bf16[8,24,512]{2,1,0:T(8,128)(2,1)} %broadcast_in_dim.46), calls=%async_computation.2 | async-start | bytes 393216 | tf_op jit(solution)/shard_map/all_to_all | solution.py:20
  91.6 9.9 %collective-permute-start.3 = (bf16[256,512]{1,0:T(8,128)(2,1)S(1)}, bf16[256,512]{1,0:T(8,128)(2,1)S(1)}, u32[]{:S(2)}, u32[]{:S(2)}) collective-permute-start(bf16[256,512]{1,0:T(8,128)(2,1)S(1)} %copy-done.2), channel_id=1, source_target_pairs={{0,1},{1,0},{2,3},{3,2},{4,5},{5,4},{6,7},{7,6},{8,9},{9,8},{10,11... | collective-permute-start | bytes 786440 | tf_op jit(solution)/shard_map/ppermute | solution.py:29
  103.3 50.7 %copy-start.5 = (s32[128]{0:T(128)S(1)}, s32[128]{0:T(128)}, u32[]{:S(2)}) copy-start(s32[128]{0:T(128)} %param.14) | copy-start | bytes 1540
  103.3 50.7 %copy-start.6 = (f32[128]{0:T(128)S(1)}, f32[128]{0:T(128)}, u32[]{:S(2)}) copy-start(f32[128]{0:T(128)} %param.17) | copy-start | bytes 1540
  103.3 50.7 %copy-start.7 = (f32[128]{0:T(128)S(1)}, f32[128]{0:T(128)}, u32[]{:S(2)}) copy-start(f32[128]{0:T(128)} %param.18) | copy-start | bytes 1540
  103.3 59.3 %copy-start.1 = (f32[4096]{0:T(1024)S(1)}, f32[4096]{0:T(1024)}, u32[]{:S(2)}) copy-start(f32[4096]{0:T(1024)} %param.22) | copy-start | bytes 49156
  103.3 42.5 %all-to-all-start.3 = ((bf16[32,160,128]{2,1,0:T(8,128)(2,1)}), bf16[32,160,128]{2,1,0:T(8,128)(2,1)S(1)}, u32[]{:S(2)}, u32[]{:S(2)}) async-start(bf16[32,160,128]{2,1,0:T(8,128)(2,1)} %pad_maximum_fusion), calls=%async_computation.3 | async-start | bytes 2621440 | tf_op jit(solution)/shard_map/all_to_all | solution.py:20
  112.4 41.7 %collective-permute-start.4 = (bf16[32,160,128]{2,1,0:T(8,128)(2,1)S(1)}, bf16[32,160,128]{2,1,0:T(8,128)(2,1)}, u32[]{:S(2)}, u32[]{:S(2)}) collective-permute-start(bf16[32,160,128]{2,1,0:T(8,128)(2,1)S(1)} %all-to-all-done.a_ref), channel_id=1, source_target_pairs={{0,1},{1,0},{2,3},{3,2},{4,5},{5,4},{6,7},{7,6},{8,9},{9,8},{10,11... | collective-permute-start | bytes 3932168 | tf_op jit(solution)/shard_map/ppermute | solution.py:29
  145.8 16.7 %collective-permute-start.5 = (bf16[32,160,128]{2,1,0:T(8,128)(2,1)S(1)}, bf16[32,160,128]{2,1,0:T(8,128)(2,1)}, u32[]{:S(2)}, u32[]{:S(2)}) collective-permute-start(bf16[32,160,128]{2,1,0:T(8,128)(2,1)S(1)} %all-to-all-done.3.b_ref), channel_id=1, source_target_pairs={{0,1},{1,0},{2,3},{3,2},{4,5},{5,4},{6,7},{7,6},{8,9},{9,8},{10,11... | collective-permute-start | bytes 3932168 | tf_op jit(solution)/shard_map/ppermute | solution.py:29
  148.5 14.1 %all-to-all-start.4 = ((bf16[16,32,128]{2,1,0:T(8,128)(2,1)}), bf16[16,32,128]{2,1,0:T(8,128)(2,1)S(1)}, u32[]{:S(2)}, u32[]{:S(2)}) async-start(bf16[16,32,128]{2,1,0:T(8,128)(2,1)} %broadcast_in_dim.48), calls=%async_computation.4 | async-start | bytes 262144 | tf_op jit(solution)/shard_map/all_to_all | solution.py:20
  162.5 1.2 copy-start

commit v4 on v2

--- a/solution.py
+++ b/solution.py
@@ -14,33 +14,24 @@
 SIZES = {"y_lo": 2, "z": 8, "y_hi": 4, "x": 8, "core": 2}
 PADDED = 8
 LANES = 128
+Y_OFFSETS = (0, -1, 1, 2)
 
 
 def exchange(blocks, axes):
     return lax.all_to_all(blocks, axes, split_axis=0, concat_axis=0, tiled=True)
 
 
-def spread(block, axes):
-    count = lax.axis_size(axes)
-    return exchange(jnp.broadcast_to(block[None], (count,) + block.shape), axes)
+def copies(block, axes):
+    return jnp.broadcast_to(block[None], (lax.axis_size(axes),) + block.shape)
 
 
 def other_core(block):
     return lax.ppermute(block, "core", [(0, 1), (1, 0)])
 
 
-def from_above(block, distance):
-    count = lax.axis_size("y_hi")
-    return lax.ppermute(block, "y_hi", [((i + distance) % count, i) for i in range(count)])
-
-
-def outward(block, distance):
-    count = lax.axis_size("x")
-    route = []
-    for i in range(count):
-        route.append((2 * i, 2 * ((i + distance) % count)))
-        route.append((2 * i + 1, 2 * ((i - distance) % count) + 1))
-    return lax.ppermute(block, ("x", "core"), route)
+def along(axis, block, distance):
+    count = lax.axis_size(axis)
+    return lax.ppermute(block, axis, [(i, (i + distance) % count) for i in range(count)])
 
 
 def tie(*values):
@@ -84,22 +75,30 @@
         cols = pl.ds(z * block_width, block_width)
         values = mixed_ref[:, cols].astype(jnp.float32)
         normed_ref[:, cols] = (values * scale * gain_ref[:, cols]).astype(jnp.bfloat16)
-    sign = 1 - 2 * core
-    xs = [0, -1, -2, -3, 4, 1, 2, 3, 4]
-    query = jnp.zeros(query_ref.shape, jnp.float32)
-    for w_ref, offset in zip(w_refs, xs, strict=True):
-        far = abs(offset) == 4
-        chip_x = lax.rem(x + sign * offset + 8, 8)
-        if far:
-            half = core if w_ref is w_refs[4] else 1 - core
-        for j in range(w_ref.shape[0]):
-            rel = j + half * 2 if far else j
-            chip_y = lax.rem(y + rel, 4)
-            start = pl.multiple_of((chip_y * 8 + chip_x) * LANES, LANES)
-            query += jnp.dot(
-                normed_ref[:, pl.ds(start, LANES)], w_ref[j], preferred_element_type=jnp.float32
-            )
-    query_ref[...] = query.astype(query_ref.dtype)
+
+    def product(low_refs, high_refs):
+        query = jnp.zeros(query_ref.shape, jnp.float32)
+        for low, high, base, count in zip(low_refs, high_refs, (x, x - 1, x + 1), (3, 3, 2), strict=True):
+            for j, y_offset in enumerate(Y_OFFSETS):
+                for i in range(count):
+                    chip_x = lax.rem(base + 3 * (i - 1) + 8, 8)
+                    chip_y = lax.rem(y + y_offset + 4, 4)
+                    start = pl.multiple_of((chip_y * 8 + chip_x) * LANES, LANES)
+                    block = jnp.concatenate([low[j, i], high[j, i]], axis=0)
+                    query += jnp.dot(
+                        normed_ref[:, pl.ds(start, LANES)], block, preferred_element_type=jnp.float32
+                    )
+        query_ref[...] = query.astype(query_ref.dtype)
+
+    own, other = w_refs[:3], w_refs[3:]
+
+    @pl.when(core == 0)
+    def _():
+        product(own, other)
+
+    @pl.when(core != 0)
+    def _():
+        product(other, own)
 
 
 def finish(place, tokens, table, column, gate, gain, weights):
@@ -156,15 +155,11 @@
     slot_hot = (jnp.arange(SLOTS, dtype=jnp.int32)[:, None] == placement[None, :]).astype(jnp.bfloat16)
     slot_rows = jnp.dot(slot_hot, token_block, preferred_element_type=jnp.float32).astype(jnp.bfloat16)
 
-    chip_rows = other_core(w_query)
-    chip_rows = jnp.where(
-        core == 0, jnp.concatenate([w_query, chip_rows], 0), jnp.concatenate([chip_rows, w_query], 0)
-    )
-    slot_rows, chip_rows = tie(slot_rows, chip_rows)
-    rows = spread(slot_rows, CHIPS).reshape(chips * SLOTS, block_width)
+    slot_copies, w_query = tie(copies(slot_rows, CHIPS), w_query)
+    rows = exchange(slot_copies, CHIPS).reshape(chips * SLOTS, block_width)
     w_gate_other = other_core(w_gate)
     w_up_other = other_core(w_up)
-    query_own = jnp.stack([chip_rows] + [from_above(chip_rows, i) for i in (1, 2, 3)])
+    chip_set = jnp.stack([along("x", w_query, 3), w_query, along("x", w_query, -3)])
 
     partial = jnp.concatenate(
         [
@@ -174,16 +169,16 @@
         axis=1,
     )
     share = chips * SLOTS // blocks
-    partial, query_own = tie(partial, query_own)
+    partial, chip_set = tie(partial, chip_set)
     summed = exchange(partial.reshape(blocks, share, 4 * units), "z")
-    near = [outward(query_own, 1), outward(query_own, 2)]
+    beside = [along("y_hi", chip_set, -offset) for offset in Y_OFFSETS[1:]]
     summed = jnp.sum(summed.astype(jnp.float32), axis=0)
     hidden_share = (jax.nn.silu(summed[:, : 2 * units]) * summed[:, 2 * units :]).astype(jnp.bfloat16)
-    hidden_share, near[0], near[1] = tie(hidden_share, *near)
-    hidden = spread(hidden_share, "z").reshape(chips * SLOTS, 2 * units)
+    hidden_copies, *beside = tie(copies(hidden_share, "z"), *beside)
+    hidden = exchange(hidden_copies, "z").reshape(chips * SLOTS, 2 * units)
     w_down_other = other_core(w_down)
-    far_half = lax.dynamic_slice_in_dim(near[1], 2 * core, 2, 0)
-    far = [outward(near[0], 2), outward(far_half, 2)]
+    column_set = jnp.stack([chip_set] + beside)
+    below, above = along("x", column_set, 1), along("x", column_set, -1)
     out_part = jnp.dot(hidden[:, :units], w_down, preferred_element_type=jnp.float32) + jnp.dot(
         hidden[:, units:], w_down_other, preferred_element_type=jnp.float32
     )
@@ -191,10 +186,10 @@
     pieces = exchange(out_part.reshape(chips, SLOTS, block_width), CHIPS)
     expert_out = jnp.sum(pieces.astype(jnp.float32), axis=0).astype(jnp.bfloat16)
     expert_out = jnp.concatenate([expert_out, jnp.zeros((PADDED - SLOTS, block_width), jnp.bfloat16)], 0)
-    expert_out, far[0], far[1] = tie(expert_out, *far)
-    table = spread(expert_out, EXPERT).reshape(-1, block_width)
-    arrived = near + far
-    weights = [query_own] + arrived + [other_core(block) for block in arrived]
+    out_copies, below, above = tie(copies(expert_out, EXPERT), below, above)
+    table = exchange(out_copies, EXPERT).reshape(-1, block_width)
+    weights = [column_set, below, above]
+    weights += [other_core(w) for w in weights]
 
     column = jnp.where(served, expert_of * PADDED + slot_of, -1)
     place = jnp.stack([lax.axis_index("x"), lax.axis_index("y_hi"), core]).astype(jnp.int32)

time: 152 us -> 151 us (level)
  starting transfers between devices: 102 us -> 95.5 us
  local copies, waits for them, and re-layouts: 5.53 us -> 8.99 us
    ppermute x8 -> x6, starting transfers between devices: 16.8 us -> 12.5 us  [other_core(): return lax.ppermute(block, 'core', [(0, 1), (1, 0)])]
    ppermute x7, starting transfers between devices: 33 us -> 28.7 us  [along(): lax.ppermute(block, axis, [(i, (i + distance) % count) for i in range(cou...]
    all_to_all x5, starting transfers between devices: 52.7 us -> 54.3 us  [exchange(): return lax.all_to_all(blocks, axes, split_axis=0, concat_axis=0, tiled=True)]
  transfers between devices with their start and end apart: 20 -> 18, of which waited for: 7 -> 5; matrix products, arithmetic and copies ran while one was open for 4% -> 6% of each run, Pallas kernels for 0% -> 0%
where the time goes in v4:
time: 151 us; the launch traced here: 150 us
  starting transfers between devices  95.5 us (63%)
  waiting for transfers between devices  33.5 us (22%)
  local copies, waits for them, and re-layouts  8.99 us (6%)
  Pallas kernels  4.91 us (3%)
  other arithmetic  3.15 us (2%)
  matrix products  2.95 us (2%)
    all_to_all x5, starting transfers between devices, exchange(): return lax.all_to_all(blocks, axes, split_axis=0, concat_axis=0, tiled=True)  54.3 us
    ppermute x7, starting transfers between devices, along(): lax.ppermute(block, axis, [(i, (i + distance) % count) for i in range(cou...  28.7 us
    all_to_all x5, waiting for transfers between devices, exchange(): return lax.all_to_all(blocks, axes, split_axis=0, concat_axis=0, tiled=True)  21.6 us
    ppermute x6, starting transfers between devices, other_core(): return lax.ppermute(block, 'core', [(0, 1), (1, 0)])  12.5 us
    ppermute x7, waiting for transfers between devices, along(): lax.ppermute(block, axis, [(i, (i + distance) % count) for i in range(cou...  11.9 us
    pallas_call x1, Pallas kernels, finish(): pl.pallas_call(finish_kernel, out_shape=(jax.ShapeDtypeStruct((tok_count,...  4.91 us
  transfers between devices with their start and end apart: 18, of which 5 were waited for; matrix products, arithmetic and copies ran while one was open for 6% of the time, Pallas kernels for 0%

profile of v4, /device:TPU:2, one launch (start us, length us, event | category | flops | bytes accessed | tf_op | source)
XLA Modules:
  0.0 150.1 jit_solution(14119242310871668142)
XLA Ops:
  0.7 0.6 copy-done.9
  1.3 1.0 convolution_convert_fusion.4
  2.4 0.7 broadcast_in_dim.18
  3.1 16.8 %all-to-all-start = ((bf16[32,6,512]{2,1,0:T(8,128)(2,1)}), bf16[32,6,512]{2,1,0:T(8,128)(2,1)S(1)}, u32[]{:S(2)}, u32[]{:S(2)}) async-start(bf16[32,6,512]{2,1,0:T(8,128)(2,1)} %broadcast_in_dim.18), calls=%async_computation | async-start | bytes 524288 | tf_op jit(solution)/shard_map/all_to_all | solution.py:21
  20.0 5.5 %collective-permute-start.3 = (bf16[64,512]{1,0:T(8,128)(2,1)S(1)}, bf16[64,512]{1,0:T(8,128)(2,1)S(1)}, u32[]{:S(2)}, u32[]{:S(2)}) collective-permute-start(bf16[64,512]{1,0:T(8,128)(2,1)S(1)} %copy-done.8), channel_id=1, source_target_pairs={{0,10},{2,12},{4,14},{6,0},{8,2},{10,4},{12,6},{14,8},{1,11},{3,13... | collective-permute-start | bytes 196616 | tf_op jit(solution)/shard_map/ppermute | solution.py:34
  25.5 3.3 %collective-permute-start.2 = (bf16[64,512]{1,0:T(8,128)(2,1)S(1)}, bf16[64,512]{1,0:T(8,128)(2,1)S(1)}, u32[]{:S(2)}, u32[]{:S(2)}) collective-permute-start(bf16[64,512]{1,0:T(8,128)(2,1)S(1)} %copy-done.8), channel_id=1, source_target_pairs={{0,6},{2,8},{4,10},{6,12},{8,14},{10,0},{12,2},{14,4},{1,7},{3,9},... | collective-permute-start | bytes 196616 | tf_op jit(solution)/shard_map/ppermute | solution.py:34
  28.8 1.9 %collective-permute-start = (bf16[512,256]{1,0:T(8,128)(2,1)S(1)}, bf16[512,256]{1,0:T(8,128)(2,1)S(1)}, u32[]{:S(2)}, u32[]{:S(2)}) collective-permute-start(bf16[512,256]{1,0:T(8,128)(2,1)S(1)} %copy-done.6), channel_id=1, source_target_pairs={{0,1},{1,0},{2,3},{3,2},{4,5},{5,4},{6,7},{7,6},{8,9},{9,8},{10,11... | collective-permute-start | bytes 786440 | tf_op jit(solution)/shard_map/ppermute | solution.py:29
  30.8 2.4 %collective-permute-start.1 = (bf16[512,256]{1,0:T(8,128)(2,1)S(1)}, bf16[512,256]{1,0:T(8,128)(2,1)S(1)}, u32[]{:S(2)}, u32[]{:S(2)}) collective-permute-start(bf16[512,256]{1,0:T(8,128)(2,1)S(1)} %copy-done.7), channel_id=1, source_target_pairs={{0,1},{1,0},{2,3},{3,2},{4,5},{5,4},{6,7},{7,6},{8,9},{9,8},{10,11... | collective-permute-start | bytes 786440 | tf_op jit(solution)/shard_map/ppermute | solution.py:29
  33.2 2.7 %collective-permute-done.2 = bf16[64,512]{1,0:T(8,128)(2,1)S(1)} collective-permute-done((bf16[64,512]{1,0:T(8,128)(2,1)S(1)}, bf16[64,512]{1,0:T(8,128)(2,1)S(1)}, u32[]{:S(2)}, u32[]{:S(2)}) %collective-permute-start.2) | collective-permute-done | bytes 65568 | tf_op jit(solution)/shard_map/ppermute | solution.py:34
  36.0 0.1 reshape.23
  36.0 0.2 convolution_convert_fusion.1
  36.2 0.2 convolution_convert_fusion.3
  36.5 0.2 convolution_convert_fusion.2
  36.7 0.2 convolution_convert_fusion
  36.9 0.8 pad_maximum_fusion.1
  37.7 13.0 %all-to-all-start.1 = ((bf16[8,24,1024]{2,1,0:T(8,128)(2,1)}), bf16[8,24,1024]{2,1,0:T(8,128)(2,1)S(1)}, u32[]{:S(2)}, u32[]{:S(2)}) async-start(bf16[8,24,1024]{2,1,0:T(8,128)(2,1)} %bitcast.6), calls=%async_computation.1 | async-start | bytes 786432 | tf_op jit(solution)/shard_map/all_to_all | solution.py:21
  50.7 7.3 %collective-permute-start.6 = (bf16[3,64,512]{2,1,0:T(8,128)(2,1)S(1)}, bf16[3,64,512]{2,1,0:T(8,128)(2,1)S(1)}, u32[]{:S(2)}, u32[]{:S(2)}) collective-permute-start(bf16[3,64,512]{2,1,0:T(8,128)(2,1)S(1)} %pad_maximum_fusion.2), channel_id=1, source_target_pairs={{0,32},{16,48},{32,0},{48,16},{1,33},{17,49},{33,1},{49,17},{2,34}... | collective-permute-start | bytes 589832 | tf_op jit(solution)/shard_map/ppermute | solution.py:34
  58.0 2.5 %collective-permute-start.5 = (bf16[3,64,512]{2,1,0:T(8,128)(2,1)S(1)}, bf16[3,64,512]{2,1,0:T(8,128)(2,1)S(1)}, u32[]{:S(2)}, u32[]{:S(2)}) collective-permute-start(bf16[3,64,512]{2,1,0:T(8,128)(2,1)S(1)} %pad_maximum_fusion.2), channel_id=1, source_target_pairs={{0,48},{16,0},{32,16},{48,32},{1,49},{17,1},{33,17},{49,33},{2,50}... | collective-permute-start | bytes 589832 | tf_op jit(solution)/shard_map/ppermute | solution.py:34
  60.5 4.3 %collective-permute-start.4 = (bf16[3,64,512]{2,1,0:T(8,128)(2,1)S(1)}, bf16[3,64,512]{2,1,0:T(8,128)(2,1)S(1)}, u32[]{:S(2)}, u32[]{:S(2)}) collective-permute-start(bf16[3,64,512]{2,1,0:T(8,128)(2,1)S(1)} %pad_maximum_fusion.2), channel_id=1, source_target_pairs={{0,16},{16,32},{32,48},{48,0},{1,17},{17,33},{33,49},{49,1},{2,18}... | collective-permute-start | bytes 589832 | tf_op jit(solution)/shard_map/ppermute | solution.py:34
  64.8 0.1 convert_reduce_fusion
  64.9 9.2 %collective-permute-done.5 = bf16[3,64,512]{2,1,0:T(8,128)(2,1)S(1)} collective-permute-done((bf16[3,64,512]{2,1,0:T(8,128)(2,1)S(1)}, bf16[3,64,512]{2,1,0:T(8,128)(2,1)S(1)}, u32[]{:S(2)}, u32[]{:S(2)}) %collective-permute-start.5) | collective-permute-done | bytes 196640 | tf_op jit(solution)/shard_map/ppermute | solution.py:34
  74.1 0.7 broadcast_in_dim.19
  74.8 6.9 %all-to-all-start.2 = ((bf16[8,24,512]{2,1,0:T(8,128)(2,1)}), bf16[8,24,512]{2,1,0:T(8,128)(2,1)S(1)}, u32[]{:S(2)}, u32[]{:S(2)}) async-start(bf16[8,24,512]{2,1,0:T(8,128)(2,1)} %broadcast_in_dim.19), calls=%async_computation.2 | async-start | bytes 393216 | tf_op jit(solution)/shard_map/all_to_all | solution.py:21
  81.8 1.9 %collective-permute-start.7 = (bf16[256,512]{1,0:T(8,128)(2,1)S(1)}, bf16[256,512]{1,0:T(8,128)(2,1)S(1)}, u32[]{:S(2)}, u32[]{:S(2)}) collective-permute-start(bf16[256,512]{1,0:T(8,128)(2,1)S(1)} %copy-done.5), channel_id=1, source_target_pairs={{0,1},{1,0},{2,3},{3,2},{4,5},{5,4},{6,7},{7,6},{8,9},{9,8},{10,11... | collective-permute-start | bytes 786440 | tf_op jit(solution)/shard_map/ppermute | solution.py:29
  83.7 0.1 pad_maximum_fusion.refs_0_
  83.8 2.9 %collective-permute-start.9 = (bf16[4,3,64,512]{3,2,1,0:T(8,128)(2,1)S(1)}, bf16[4,3,64,512]{3,2,1,0:T(8,128)(2,1)S(1)}, u32[]{:S(2)}, u32[]{:S(2)}) collective-permute-start(bf16[4,3,64,512]{3,2,1,0:T(8,128)(2,1)S(1)} %pad_maximum_fusion.refs_0_), channel_id=1, source_target_pairs={{0,14},{2,0},{4,2},{6,4},{8,6},{10,8},{12,10},{14,12},{1,15},{3,1}... | collective-permute-start | bytes 2359304 | tf_op jit(solution)/shard_map/ppermute | solution.py:34
  86.8 2.9 %collective-permute-start.8 = (bf16[4,3,64,512]{3,2,1,0:T(8,128)(2,1)S(1)}, bf16[4,3,64,512]{3,2,1,0:T(8,128)(2,1)S(1)}, u32[]{:S(2)}, u32[]{:S(2)}) collective-permute-start(bf16[4,3,64,512]{3,2,1,0:T(8,128)(2,1)S(1)} %pad_maximum_fusion.refs_0_), channel_id=1, source_target_pairs={{0,2},{2,4},{4,6},{6,8},{8,10},{10,12},{12,14},{14,0},{1,3},{3,5},... | collective-permute-start | bytes 2359304 | tf_op jit(solution)/shard_map/ppermute | solution.py:34
  89.7 2.8 %all-to-all-done.2 = bf16[8,24,512]{2,1,0:T(8,128)(2,1)S(1)} async-done(((bf16[8,24,512]{2,1,0:T(8,128)(2,1)}), bf16[8,24,512]{2,1,0:T(8,128)(2,1)S(1)}, u32[]{:S(2)}, u32[]{:S(2)}) %all-to-all-start.2) | async-done | bytes 196640 | tf_op jit(solution)/shard_map/all_to_all | solution.py:21
  92.4 0.2 fusion.3
  92.6 0.9 fusion
  93.5 1.8 %reshape.26 = bf16[32,6,512]{2,1,0:T(8,128)(2,1)} reshape(bf16[192,512]{1,0:T(8,128)(2,1)} %fusion) | data formatting | bytes 393216 | tf_op jit(solution)/shard_map/reshape | solution.py:186
  95.3 9.4 %all-to-all-start.3 = ((bf16[32,6,512]{2,1,0:T(8,128)(2,1)}), bf16[32,6,512]{2,1,0:T(8,128)(2,1)}, u32[]{:S(2)}, u32[]{:S(2)}) async-start(bf16[32,6,512]{2,1,0:T(8,128)(2,1)} %reshape.26), calls=%async_computation.3 | async-start | bytes 524288 | tf_op jit(solution)/shard_map/all_to_all | solution.py:21
  104.8 1.9 %collective-permute-start.10 = (bf16[4,3,64,512]{3,2,1,0:T(8,128)(2,1)S(1)}, bf16[4,3,64,512]{3,2,1,0:T(8,128)(2,1)}, u32[]{:S(2)}, u32[]{:S(2)}) collective-permute-start(bf16[4,3,64,512]{3,2,1,0:T(8,128)(2,1)S(1)} %pad_maximum_fusion.refs_0_), channel_id=1, source_target_pairs={{0,1},{1,0},{2,3},{3,2},{4,5},{5,4},{6,7},{7,6},{8,9},{9,8},{10,11... | collective-permute-start | bytes 2359304 | tf_op jit(solution)/shard_map/ppermute | solution.py:29
  106.7 12.7 %all-to-all-done.3 = bf16[32,6,512]{2,1,0:T(8,128)(2,1)} async-done(((bf16[32,6,512]{2,1,0:T(8,128)(2,1)}), bf16[32,6,512]{2,1,0:T(8,128)(2,1)}, u32[]{:S(2)}, u32[]{:S(2)}) %all-to-all-start.3) | async-done | bytes 196640 | tf_op jit(solution)/shard_map/all_to_all | solution.py:21
  119.4 1.0 reduce_sum.22
  120.5 0.7 broadcast_in_dim.38
  121.1 1.9 %collective-permute-start.11 = (bf16[4,3,64,512]{3,2,1,0:T(8,128)(2,1)S(1)}, bf16[4,3,64,512]{3,2,1,0:T(8,128)(2,1)}, u32[]{:S(2)}, u32[]{:S(2)}) collective-permute-start(bf16[4,3,64,512]{3,2,1,0:T(8,128)(2,1)S(1)} %collective-permute-done.8.refs_1_), channel_id=1, source_target_pairs={{0,1},{1,0},{2,3},{3,2},{4,5},{5,4},{6,7},{7,6},{8,9},{9,8},{10,11... | collective-permute-start | bytes 2359304 | tf_op jit(solution)/shard_map/ppermute | solution.py:29
  123.0 2.4 %collective-permute-start.12 = (bf16[4,3,64,512]{3,2,1,0:T(8,128)(2,1)S(1)}, bf16[4,3,64,512]{3,2,1,0:T(8,128)(2,1)}, u32[]{:S(2)}, u32[]{:S(2)}) collective-permute-start(bf16[4,3,64,512]{3,2,1,0:T(8,128)(2,1)S(1)} %collective-permute-done.9.refs_2_), channel_id=1, source_target_pairs={{0,1},{1,0},{2,3},{3,2},{4,5},{5,4},{6,7},{7,6},{8,9},{9,8},{10,11... | collective-permute-start | bytes 2359304 | tf_op jit(solution)/shard_map/ppermute | solution.py:29
  125.5 0.7 copy.16.column_ref
  126.2 8.1 %all-to-all-start.4 = ((bf16[16,8,512]{2,1,0:T(8,128)(2,1)}), bf16[16,8,512]{2,1,0:T(8,128)(2,1)S(1)}, u32[]{:S(2)}, u32[]{:S(2)}) async-start(bf16[16,8,512]{2,1,0:T(8,128)(2,1)} %broadcast_in_dim.38), calls=%async_computation.4 | async-start | bytes 262144 | tf_op jit(solution)/shard_map/all_to_all | solution.py:21
  134.3 0.5 select_bitcast_fusion
  134.8 1.3 copy.17.gate_ref
  136.2 0.6 pad_add_fusion.place_ref
  136.8 6.1 %all-to-all-done.4 = bf16[16,8,512]{2,1,0:T(8,128)(2,1)S(1)} async-done(((bf16[16,8,512]{2,1,0:T(8,128)(2,1)}), bf16[16,8,512]{2,1,0:T(8,128)(2,1)S(1)}, u32[]{:S(2)}, u32[]{:S(2)}) %all-to-all-start.4) | async-done | bytes 131104 | tf_op jit(solution)/shard_map/all_to_all | solution.py:21
  142.9 0.6 copy-done.4
  143.5 0.8 copy-done.1
  144.3 0.8 copy-done.2
  145.2 4.9 %shard_map.131 = (bf16[128,4096]{1,0:T(8,128)(2,1)}, bf16[128,512]{1,0:T(8,128)(2,1)}) custom-call(s32[3]{0:T(128)S(1)} %copy-done.4, bf16[128,4096]{1,0:T(8,128)(2,1)S(1)} %copy-done, bf16[128,512]{1,0:T(8,128)(2,1)S(1)} %bitcast.28, s32[128,1]{1,0:T(8,128)S(1)} %copy-done.1, f32[128,1]{1,0:T(8,128)S(1)} %copy-done.2, f32[1,4096]{1,0:T(1,128)S(1)} %bitcast.29, ...), custom_call_target="tpu_custom_call" | custom-call | flops 536870912 | bytes 8388608 | tf_op jit(solution)/shard_map/pallas_call | solution.py:108
  (43 shorter events, 0.2 us)
Async XLA Ops:
  0.6 0.7 copy-start.9
  0.6 0.7 copy-start.10
  0.7 0.7 copy-start.11
  0.7 0.7 copy-start.12
  2.4 17.6 %copy-start.8 = (bf16[64,512]{1,0:T(8,128)(2,1)S(1)}, bf16[64,512]{1,0:T(8,128)(2,1)}, u32[]{:S(2)}) copy-start(bf16[64,512]{1,0:T(8,128)(2,1)} %param.23) | copy-start | bytes 196612
  3.1 25.7 %copy-start.6 = (bf16[512,256]{1,0:T(8,128)(2,1)S(1)}, bf16[512,256]{1,0:T(8,128)(2,1)}, u32[]{:S(2)}) copy-start(bf16[512,256]{1,0:T(8,128)(2,1)} %param.19) | copy-start | bytes 786436
  3.1 27.7 %copy-start.7 = (bf16[512,256]{1,0:T(8,128)(2,1)S(1)}, bf16[512,256]{1,0:T(8,128)(2,1)}, u32[]{:S(2)}) copy-start(bf16[512,256]{1,0:T(8,128)(2,1)} %param.20) | copy-start | bytes 786436
  3.1 32.8 %all-to-all-start = ((bf16[32,6,512]{2,1,0:T(8,128)(2,1)}), bf16[32,6,512]{2,1,0:T(8,128)(2,1)S(1)}, u32[]{:S(2)}, u32[]{:S(2)}) async-start(bf16[32,6,512]{2,1,0:T(8,128)(2,1)} %broadcast_in_dim.18), calls=%async_computation | async-start | bytes 524288 | tf_op jit(solution)/shard_map/all_to_all | solution.py:21
  20.0 13.2 %collective-permute-start.3 = (bf16[64,512]{1,0:T(8,128)(2,1)S(1)}, bf16[64,512]{1,0:T(8,128)(2,1)S(1)}, u32[]{:S(2)}, u32[]{:S(2)}) collective-permute-start(bf16[64,512]{1,0:T(8,128)(2,1)S(1)} %copy-done.8), channel_id=1, source_target_pairs={{0,10},{2,12},{4,14},{6,0},{8,2},{10,4},{12,6},{14,8},{1,11},{3,13... | collective-permute-start | bytes 196616 | tf_op jit(solution)/shard_map/ppermute | solution.py:34
  25.5 10.4 %collective-permute-start.2 = (bf16[64,512]{1,0:T(8,128)(2,1)S(1)}, bf16[64,512]{1,0:T(8,128)(2,1)S(1)}, u32[]{:S(2)}, u32[]{:S(2)}) collective-permute-start(bf16[64,512]{1,0:T(8,128)(2,1)S(1)} %copy-done.8), channel_id=1, source_target_pairs={{0,6},{2,8},{4,10},{6,12},{8,14},{10,0},{12,2},{14,4},{1,7},{3,9},... | collective-permute-start | bytes 196616 | tf_op jit(solution)/shard_map/ppermute | solution.py:34
  28.8 7.6 %collective-permute-start = (bf16[512,256]{1,0:T(8,128)(2,1)S(1)}, bf16[512,256]{1,0:T(8,128)(2,1)S(1)}, u32[]{:S(2)}, u32[]{:S(2)}) collective-permute-start(bf16[512,256]{1,0:T(8,128)(2,1)S(1)} %copy-done.6), channel_id=1, source_target_pairs={{0,1},{1,0},{2,3},{3,2},{4,5},{5,4},{6,7},{7,6},{8,9},{9,8},{10,11... | collective-permute-start | bytes 786440 | tf_op jit(solution)/shard_map/ppermute | solution.py:29
  30.8 5.9 %collective-permute-start.1 = (bf16[512,256]{1,0:T(8,128)(2,1)S(1)}, bf16[512,256]{1,0:T(8,128)(2,1)S(1)}, u32[]{:S(2)}, u32[]{:S(2)}) collective-permute-start(bf16[512,256]{1,0:T(8,128)(2,1)S(1)} %copy-done.7), channel_id=1, source_target_pairs={{0,1},{1,0},{2,3},{3,2},{4,5},{5,4},{6,7},{7,6},{8,9},{9,8},{10,11... | collective-permute-start | bytes 786440 | tf_op jit(solution)/shard_map/ppermute | solution.py:29
  37.7 27.1 %all-to-all-start.1 = ((bf16[8,24,1024]{2,1,0:T(8,128)(2,1)}), bf16[8,24,1024]{2,1,0:T(8,128)(2,1)S(1)}, u32[]{:S(2)}, u32[]{:S(2)}) async-start(bf16[8,24,1024]{2,1,0:T(8,128)(2,1)} %bitcast.6), calls=%async_computation.1 | async-start | bytes 786432 | tf_op jit(solution)/shard_map/all_to_all | solution.py:21
  50.7 14.2 %collective-permute-start.6 = (bf16[3,64,512]{2,1,0:T(8,128)(2,1)S(1)}, bf16[3,64,512]{2,1,0:T(8,128)(2,1)S(1)}, u32[]{:S(2)}, u32[]{:S(2)}) collective-permute-start(bf16[3,64,512]{2,1,0:T(8,128)(2,1)S(1)} %pad_maximum_fusion.2), channel_id=1, source_target_pairs={{0,32},{16,48},{32,0},{48,16},{1,33},{17,49},{33,1},{49,17},{2,34}... | collective-permute-start | bytes 589832 | tf_op jit(solution)/shard_map/ppermute | solution.py:34
  58.0 16.1 %collective-permute-start.5 = (bf16[3,64,512]{2,1,0:T(8,128)(2,1)S(1)}, bf16[3,64,512]{2,1,0:T(8,128)(2,1)S(1)}, u32[]{:S(2)}, u32[]{:S(2)}) collective-permute-start(bf16[3,64,512]{2,1,0:T(8,128)(2,1)S(1)} %pad_maximum_fusion.2), channel_id=1, source_target_pairs={{0,48},{16,0},{32,16},{48,32},{1,49},{17,1},{33,17},{49,33},{2,50}... | collective-permute-start | bytes 589832 | tf_op jit(solution)/shard_map/ppermute | solution.py:34
  60.5 13.6 %collective-permute-start.4 = (bf16[3,64,512]{2,1,0:T(8,128)(2,1)S(1)}, bf16[3,64,512]{2,1,0:T(8,128)(2,1)S(1)}, u32[]{:S(2)}, u32[]{:S(2)}) collective-permute-start(bf16[3,64,512]{2,1,0:T(8,128)(2,1)S(1)} %pad_maximum_fusion.2), channel_id=1, source_target_pairs={{0,16},{16,32},{32,48},{48,0},{1,17},{17,33},{33,49},{49,1},{2,18}... | collective-permute-start | bytes 589832 | tf_op jit(solution)/shard_map/ppermute | solution.py:34
  64.9 16.9 %copy-start.5 = (bf16[256,512]{1,0:T(8,128)(2,1)S(1)}, bf16[256,512]{1,0:T(8,128)(2,1)}, u32[]{:S(2)}) copy-start(bf16[256,512]{1,0:T(8,128)(2,1)} %param.21) | copy-start | bytes 786436
  74.8 17.6 %all-to-all-start.2 = ((bf16[8,24,512]{2,1,0:T(8,128)(2,1)}), bf16[8,24,512]{2,1,0:T(8,128)(2,1)S(1)}, u32[]{:S(2)}, u32[]{:S(2)}) async-start(bf16[8,24,512]{2,1,0:T(8,128)(2,1)} %broadcast_in_dim.19), calls=%async_computation.2 | async-start | bytes 393216 | tf_op jit(solution)/shard_map/all_to_all | solution.py:21
  81.8 10.9 %collective-permute-start.7 = (bf16[256,512]{1,0:T(8,128)(2,1)S(1)}, bf16[256,512]{1,0:T(8,128)(2,1)S(1)}, u32[]{:S(2)}, u32[]{:S(2)}) collective-permute-start(bf16[256,512]{1,0:T(8,128)(2,1)S(1)} %copy-done.5), channel_id=1, source_target_pairs={{0,1},{1,0},{2,3},{3,2},{4,5},{5,4},{6,7},{7,6},{8,9},{9,8},{10,11... | collective-permute-start | bytes 786440 | tf_op jit(solution)/shard_map/ppermute | solution.py:29
  83.8 36.6 %collective-permute-start.9 = (bf16[4,3,64,512]{3,2,1,0:T(8,128)(2,1)S(1)}, bf16[4,3,64,512]{3,2,1,0:T(8,128)(2,1)S(1)}, u32[]{:S(2)}, u32[]{:S(2)}) collective-permute-start(bf16[4,3,64,512]{3,2,1,0:T(8,128)(2,1)S(1)} %pad_maximum_fusion.refs_0_), channel_id=1, source_target_pairs={{0,14},{2,0},{4,2},{6,4},{8,6},{10,8},{12,10},{14,12},{1,15},{3,1}... | collective-permute-start | bytes 2359304 | tf_op jit(solution)/shard_map/ppermute | solution.py:34
  86.8 33.7 %collective-permute-start.8 = (bf16[4,3,64,512]{3,2,1,0:T(8,128)(2,1)S(1)}, bf16[4,3,64,512]{3,2,1,0:T(8,128)(2,1)S(1)}, u32[]{:S(2)}, u32[]{:S(2)}) collective-permute-start(bf16[4,3,64,512]{3,2,1,0:T(8,128)(2,1)S(1)} %pad_maximum_fusion.refs_0_), channel_id=1, source_target_pairs={{0,2},{2,4},{4,6},{6,8},{8,10},{10,12},{12,14},{14,0},{1,3},{3,5},... | collective-permute-start | bytes 2359304 | tf_op jit(solution)/shard_map/ppermute | solution.py:34
  93.5 49.4 %copy-start = (bf16[128,4096]{1,0:T(8,128)(2,1)S(1)}, bf16[128,4096]{1,0:T(8,128)(2,1)}, u32[]{:S(2)}) copy-start(bf16[128,4096]{1,0:T(8,128)(2,1)} %tokens_ref.1) | copy-start | bytes 3145732
  95.3 24.1 %all-to-all-start.3 = ((bf16[32,6,512]{2,1,0:T(8,128)(2,1)}), bf16[32,6,512]{2,1,0:T(8,128)(2,1)}, u32[]{:S(2)}, u32[]{:S(2)}) async-start(bf16[32,6,512]{2,1,0:T(8,128)(2,1)} %reshape.26), calls=%async_computation.3 | async-start | bytes 524288 | tf_op jit(solution)/shard_map/all_to_all | solution.py:21
  104.8 32.0 %collective-permute-start.10 = (bf16[4,3,64,512]{3,2,1,0:T(8,128)(2,1)S(1)}, bf16[4,3,64,512]{3,2,1,0:T(8,128)(2,1)}, u32[]{:S(2)}, u32[]{:S(2)}) collective-permute-start(bf16[4,3,64,512]{3,2,1,0:T(8,128)(2,1)S(1)} %pad_maximum_fusion.refs_0_), channel_id=1, source_target_pairs={{0,1},{1,0},{2,3},{3,2},{4,5},{5,4},{6,7},{7,6},{8,9},{9,8},{10,11... | collective-permute-start | bytes 2359304 | tf_op jit(solution)/shard_map/ppermute | solution.py:29
  121.1 21.8 %collective-permute-start.11 = (bf16[4,3,64,512]{3,2,1,0:T(8,128)(2,1)S(1)}, bf16[4,3,64,512]{3,2,1,0:T(8,128)(2,1)}, u32[]{:S(2)}, u32[]{:S(2)}) collective-permute-start(bf16[4,3,64,512]{3,2,1,0:T(8,128)(2,1)S(1)} %collective-permute-done.8.refs_1_), channel_id=1, source_target_pairs={{0,1},{1,0},{2,3},{3,2},{4,5},{5,4},{6,7},{7,6},{8,9},{9,8},{10,11... | collective-permute-start | bytes 2359304 | tf_op jit(solution)/shard_map/ppermute | solution.py:29
  123.0 19.8 %collective-permute-start.12 = (bf16[4,3,64,512]{3,2,1,0:T(8,128)(2,1)S(1)}, bf16[4,3,64,512]{3,2,1,0:T(8,128)(2,1)}, u32[]{:S(2)}, u32[]{:S(2)}) collective-permute-start(bf16[4,3,64,512]{3,2,1,0:T(8,128)(2,1)S(1)} %collective-permute-done.9.refs_2_), channel_id=1, source_target_pairs={{0,1},{1,0},{2,3},{3,2},{4,5},{5,4},{6,7},{7,6},{8,9},{9,8},{10,11... | collective-permute-start | bytes 2359304 | tf_op jit(solution)/shard_map/ppermute | solution.py:29
  126.2 8.1 %copy-start.13 = (f32[128]{0:T(128)S(1)}, f32[128]{0:T(128)}, u32[]{:S(2)}) copy-start(f32[128]{0:T(128)} %param.17) | copy-start | bytes 1540
  126.2 8.1 %copy-start.14 = (f32[128]{0:T(128)S(1)}, f32[128]{0:T(128)}, u32[]{:S(2)}) copy-start(f32[128]{0:T(128)} %param.18) | copy-start | bytes 1540
  126.2 16.7 %all-to-all-start.4 = ((bf16[16,8,512]{2,1,0:T(8,128)(2,1)}), bf16[16,8,512]{2,1,0:T(8,128)(2,1)S(1)}, u32[]{:S(2)}, u32[]{:S(2)}) async-start(bf16[16,8,512]{2,1,0:T(8,128)(2,1)} %broadcast_in_dim.38), calls=%async_computation.4 | async-start | bytes 262144 | tf_op jit(solution)/shard_map/all_to_all | solution.py:21
  134.8 8.1 %copy-start.3 = (f32[4096]{0:T(1024)S(1)}, f32[4096]{0:T(1024)}, u32[]{:S(2)}) copy-start(f32[4096]{0:T(1024)} %param.22) | copy-start | bytes 49156
  142.9 0.6 copy-start.4
  143.5 0.8 copy-start.1
  144.3 0.8 copy-start.2

commit v5 on v4

--- a/solution.py
+++ b/solution.py
@@ -14,7 +14,6 @@
 SIZES = {"y_lo": 2, "z": 8, "y_hi": 4, "x": 8, "core": 2}
 PADDED = 8
 LANES = 128
-Y_OFFSETS = (0, -1, 1, 2)
 
 
 def exchange(blocks, axes):
@@ -39,18 +38,18 @@
 
 
 def finish_kernel(
-    place_ref, tokens_ref, table_ref, column_ref, gate_ref, gain_ref, *refs
+    tokens_ref, table_ref, column_ref, gate_ref, gain_ref, w_hbm, mixed_ref, query_ref, normed_ref, w_ref, sem
 ):
-    w_refs, (mixed_ref, query_ref, normed_ref) = refs[:-3], refs[-3:]
-    x, y, core = place_ref[0], place_ref[1], place_ref[2]
+    parts = w_ref.shape[0]
+    loads = [pltpu.make_async_copy(w_hbm.at[i], w_ref.at[i], sem.at[i]) for i in range(parts)]
+    for load in loads:
+        load.start()
     blocks = table_ref.shape[0] // (2 * PADDED)
     tok_count, width = tokens_ref.shape
     block_width = width // blocks
     column = column_ref[...]
     slots = lax.broadcasted_iota(jnp.int32, (tok_count, PADDED), 1)
-    hot = [
-        (column == slots + e * PADDED).astype(jnp.bfloat16) for e in range(2)
-    ]
+    hot = [(column == slots + e * PADDED).astype(jnp.bfloat16) for e in range(2)]
     gate = gate_ref[...]
     square = jnp.zeros((tok_count, LANES), jnp.float32)
     for z in range(blocks):
@@ -75,50 +74,43 @@
         cols = pl.ds(z * block_width, block_width)
         values = mixed_ref[:, cols].astype(jnp.float32)
         normed_ref[:, cols] = (values * scale * gain_ref[:, cols]).astype(jnp.bfloat16)
-
-    def product(low_refs, high_refs):
-        query = jnp.zeros(query_ref.shape, jnp.float32)
-        for low, high, base, count in zip(low_refs, high_refs, (x, x - 1, x + 1), (3, 3, 2), strict=True):
-            for j, y_offset in enumerate(Y_OFFSETS):
-                for i in range(count):
-                    chip_x = lax.rem(base + 3 * (i - 1) + 8, 8)
-                    chip_y = lax.rem(y + y_offset + 4, 4)
-                    start = pl.multiple_of((chip_y * 8 + chip_x) * LANES, LANES)
-                    block = jnp.concatenate([low[j, i], high[j, i]], axis=0)
-                    query += jnp.dot(
-                        normed_ref[:, pl.ds(start, LANES)], block, preferred_element_type=jnp.float32
-                    )
-        query_ref[...] = query.astype(query_ref.dtype)
-
-    own, other = w_refs[:3], w_refs[3:]
-
-    @pl.when(core == 0)
-    def _():
-        product(own, other)
-
-    @pl.when(core != 0)
-    def _():
-        product(other, own)
-
-
-def finish(place, tokens, table, column, gate, gain, weights):
+    for load in loads:
+        load.wait()
+    cores, ys, rows = w_ref.shape[1:4]
+    pair = 2 * cores * rows
+    query = jnp.zeros(query_ref.shape, jnp.float32)
+    for x in range(0, parts, 2):
+        for y in range(ys):
+            block = jnp.concatenate([w_ref[x + i, c, y] for i in range(2) for c in range(cores)], axis=0)
+            start = (y * parts + x) * cores * rows
+            query += jnp.dot(
+                normed_ref[:, start : start + pair], block, preferred_element_type=jnp.float32
+            )
+    query_ref[...] = query.astype(query_ref.dtype)
+
+
+def finish(tokens, table, column, gate, gain, w_query):
     vmem = pl.BlockSpec(memory_space=pltpu.VMEM)
     tok_count, width = tokens.shape
-    columns = weights[0].shape[-1]
+    columns = w_query.shape[-1]
     return pl.pallas_call(
         finish_kernel,
         out_shape=(
             jax.ShapeDtypeStruct((tok_count, width), jnp.bfloat16),
             jax.ShapeDtypeStruct((tok_count, columns), jnp.bfloat16),
         ),
-        in_specs=[pl.BlockSpec(memory_space=pltpu.SMEM)] + [vmem] * (5 + len(weights)),
+        in_specs=[vmem] * 5 + [pl.BlockSpec(memory_space=pl.ANY)],
         out_specs=(vmem, vmem),
-        scratch_shapes=[pltpu.VMEM((tok_count, width), jnp.bfloat16)],
+        scratch_shapes=[
+            pltpu.VMEM((tok_count, width), jnp.bfloat16),
+            pltpu.VMEM(w_query.shape, jnp.bfloat16),
+            pltpu.SemaphoreType.DMA((w_query.shape[0],)),
+        ],
         compiler_params=pltpu.CompilerParams(vmem_limit_bytes=24 * 1024 * 1024),
         cost_estimate=pl.CostEstimate(
             flops=2 * tok_count * width * columns, bytes_accessed=4 * width * columns, transcendentals=0
         ),
-    )(place, tokens, table, column[:, None], gate[:, None], gain[None, :], *weights)
+    )(tokens, table, column[:, None], gate[:, None], gain[None, :], w_query)
 
 
 def local(
@@ -142,7 +134,6 @@
     units = w_gate.shape[1]
     own_expert = lax.axis_index("y_lo")
     own_block = lax.axis_index("z")
-    core = lax.axis_index("core")
 
     served_first = first_slot >= 0
     served = served_first | (second_slot >= 0)
@@ -159,7 +150,7 @@
     rows = exchange(slot_copies, CHIPS).reshape(chips * SLOTS, block_width)
     w_gate_other = other_core(w_gate)
     w_up_other = other_core(w_up)
-    chip_set = jnp.stack([along("x", w_query, 3), w_query, along("x", w_query, -3)])
+    query_rows = [w_query, along("y_hi", w_query, -1)]
 
     partial = jnp.concatenate(
         [
@@ -169,16 +160,21 @@
         axis=1,
     )
     share = chips * SLOTS // blocks
-    partial, chip_set = tie(partial, chip_set)
+    partial, *query_rows = tie(partial, *query_rows)
     summed = exchange(partial.reshape(blocks, share, 4 * units), "z")
-    beside = [along("y_hi", chip_set, -offset) for offset in Y_OFFSETS[1:]]
+    query_rows += [along("y_hi", query_rows[0], -2), along("y_hi", query_rows[0], -3)]
     summed = jnp.sum(summed.astype(jnp.float32), axis=0)
     hidden_share = (jax.nn.silu(summed[:, : 2 * units]) * summed[:, 2 * units :]).astype(jnp.bfloat16)
-    hidden_copies, *beside = tie(copies(hidden_share, "z"), *beside)
+    hidden_copies, *query_rows = tie(copies(hidden_share, "z"), *query_rows)
+    for bit in (1, 2):
+        turned = query_rows[-bit:] + query_rows[:-bit]
+        set_bit = (lax.axis_index("y_hi") & bit) != 0
+        query_rows = [jnp.where(set_bit, t, q) for t, q in zip(turned, query_rows, strict=True)]
+    column_rows = jnp.stack(query_rows)
+    w_query_full = lax.all_gather(column_rows, ("x", "core"), axis=0)
+    w_query_full = w_query_full.reshape((-1, 2) + column_rows.shape)
     hidden = exchange(hidden_copies, "z").reshape(chips * SLOTS, 2 * units)
     w_down_other = other_core(w_down)
-    column_set = jnp.stack([chip_set] + beside)
-    below, above = along("x", column_set, 1), along("x", column_set, -1)
     out_part = jnp.dot(hidden[:, :units], w_down, preferred_element_type=jnp.float32) + jnp.dot(
         hidden[:, units:], w_down_other, preferred_element_type=jnp.float32
     )
@@ -186,14 +182,10 @@
     pieces = exchange(out_part.reshape(chips, SLOTS, block_width), CHIPS)
     expert_out = jnp.sum(pieces.astype(jnp.float32), axis=0).astype(jnp.bfloat16)
     expert_out = jnp.concatenate([expert_out, jnp.zeros((PADDED - SLOTS, block_width), jnp.bfloat16)], 0)
-    out_copies, below, above = tie(copies(expert_out, EXPERT), below, above)
-    table = exchange(out_copies, EXPERT).reshape(-1, block_width)
-    weights = [column_set, below, above]
-    weights += [other_core(w) for w in weights]
+    table = exchange(copies(expert_out, EXPERT), EXPERT).reshape(-1, block_width)
 
     column = jnp.where(served, expert_of * PADDED + slot_of, -1)
-    place = jnp.stack([lax.axis_index("x"), lax.axis_index("y_hi"), core]).astype(jnp.int32)
-    return finish(place, tokens, table, column, gate_of, norm_gain, weights)
+    return finish(tokens, table, column, gate_of, norm_gain, w_query_full)
 
 
 def solution(mesh):

time: 151 us -> 138 us (0.914)
  the two profiles are of different devices: /device:TPU:2 before, /device:TPU:4 now
where the time goes in v5:
time: 138 us; the launch traced here: 137 us
  starting transfers between devices  60.9 us (44%)
  waiting for transfers between devices  25.3 us (18%)
  blocking collectives  22.3 us (16%)
  between operations  14.3 us (10%)
  local copies, waits for them, and re-layouts  4.7 us (3%)
  matrix products  4.19 us (3%)
  Pallas kernels  2.79 us (2%)
  other arithmetic  2.47 us (2%)
    all_to_all x4, starting transfers between devices, exchange(): return lax.all_to_all(blocks, axes, split_axis=0, concat_axis=0, tiled=True)  42.2 us
    all_to_all x4, waiting for transfers between devices, exchange(): return lax.all_to_all(blocks, axes, split_axis=0, concat_axis=0, tiled=True)  25.3 us
    all_to_all x1, blocking collectives, exchange(): return lax.all_to_all(blocks, axes, split_axis=0, concat_axis=0, tiled=True)  22.3 us
    ppermute x3, starting transfers between devices, along(): lax.ppermute(block, axis, [(i, (i + distance) % count) for i in range(cou...  12.4 us
    ppermute x3, starting transfers between devices, other_core(): return lax.ppermute(block, 'core', [(0, 1), (1, 0)])  6.25 us
    pallas_call x1, Pallas kernels, finish(): pl.pallas_call(finish_kernel, out_shape=(jax.ShapeDtypeStruct((tok_count,...  2.79 us
  transfers between devices with their start and end apart: 11, of which 4 were waited for; matrix products, arithmetic and copies ran while one was open for 4% of the time, Pallas kernels for 0%

profile of v5, /device:TPU:4, one launch (start us, length us, event | category | flops | bytes accessed | tf_op | source)
XLA Modules:
  0.0 137.0 jit_solution(1979710556691640501)
XLA Ops:
  7.2 0.0 copy-start.4
  7.2 0.8 select_bitcast_fusion.5
  8.0 1.0 convolution_convert_fusion.4
  9.0 0.7 broadcast_in_dim.18
  9.7 16.7 %all-to-all-start = ((bf16[32,6,512]{2,1,0:T(8,128)(2,1)}), bf16[32,6,512]{2,1,0:T(8,128)(2,1)S(1)}, u32[]{:S(2)}, u32[]{:S(2)}) async-start(bf16[32,6,512]{2,1,0:T(8,128)(2,1)} %broadcast_in_dim.18), calls=%async_computation | async-start | bytes 524288 | tf_op jit(solution)/shard_map/all_to_all | solution.py:20
  26.4 5.6 %collective-permute-start.2 = (bf16[64,512]{1,0:T(8,128)(2,1)}, bf16[64,512]{1,0:T(8,128)(2,1)S(1)}, u32[]{:S(2)}, u32[]{:S(2)}) collective-permute-start(bf16[64,512]{1,0:T(8,128)(2,1)} %param.23), channel_id=1, source_target_pairs={{0,48},{16,0},{32,16},{48,32},{1,49},{17,1},{33,17},{49,33},{2,50}... | collective-permute-start | bytes 196616 | tf_op jit(solution)/shard_map/ppermute | solution.py:33
  32.1 1.9 %collective-permute-start = (bf16[512,256]{1,0:T(8,128)(2,1)}, bf16[512,256]{1,0:T(8,128)(2,1)S(1)}, u32[]{:S(2)}, u32[]{:S(2)}) collective-permute-start(bf16[512,256]{1,0:T(8,128)(2,1)} %param.19), channel_id=1, source_target_pairs={{0,1},{1,0},{2,3},{3,2},{4,5},{5,4},{6,7},{7,6},{8,9},{9,8},{10,11... | collective-permute-start | bytes 786440 | tf_op jit(solution)/shard_map/ppermute | solution.py:28
  34.0 2.4 %collective-permute-start.1 = (bf16[512,256]{1,0:T(8,128)(2,1)}, bf16[512,256]{1,0:T(8,128)(2,1)S(1)}, u32[]{:S(2)}, u32[]{:S(2)}) collective-permute-start(bf16[512,256]{1,0:T(8,128)(2,1)} %param.20), channel_id=1, source_target_pairs={{0,1},{1,0},{2,3},{3,2},{4,5},{5,4},{6,7},{7,6},{8,9},{9,8},{10,11... | collective-permute-start | bytes 786440 | tf_op jit(solution)/shard_map/ppermute | solution.py:28
  36.4 2.6 %all-to-all-done = bf16[32,6,512]{2,1,0:T(8,128)(2,1)S(1)} async-done(((bf16[32,6,512]{2,1,0:T(8,128)(2,1)}), bf16[32,6,512]{2,1,0:T(8,128)(2,1)S(1)}, u32[]{:S(2)}, u32[]{:S(2)}) %all-to-all-start) | async-done | bytes 196640 | tf_op jit(solution)/shard_map/all_to_all | solution.py:20
  39.0 0.1 reshape.26
  39.1 1.2 convolution_convert_fusion.1
  40.2 1.2 convolution_convert_fusion.3
  41.4 0.2 convolution_convert_fusion.2
  41.6 0.0 copy-start.5
  41.7 0.0 copy-start.6
  41.7 0.0 copy-start.7
  41.7 0.0 copy-start.1
  41.7 0.0 copy-start.2
  41.7 0.0 collective-permute-done.1
  41.7 0.2 convolution_convert_fusion
  41.9 0.8 pad_maximum_fusion
  42.7 0.0 collective-permute-done.2
  42.7 14.6 %all-to-all-start.1 = ((bf16[8,24,1024]{2,1,0:T(8,128)(2,1)}), bf16[8,24,1024]{2,1,0:T(8,128)(2,1)S(1)}, u32[]{:S(2)}, u32[]{:S(2)}) async-start(bf16[8,24,1024]{2,1,0:T(8,128)(2,1)} %bitcast), calls=%async_computation.1 | async-start | bytes 786432 | tf_op jit(solution)/shard_map/all_to_all | solution.py:20
  57.3 0.0 all-gather.3.cloned.1.call-start
  57.4 2.7 %collective-permute-start.4 = (bf16[64,512]{1,0:T(8,128)(2,1)S(1)}, bf16[64,512]{1,0:T(8,128)(2,1)S(1)}, u32[]{:S(2)}, u32[]{:S(2)}) collective-permute-start(bf16[64,512]{1,0:T(8,128)(2,1)S(1)} %copy-done.4), channel_id=1, source_target_pairs={{0,16},{16,32},{32,48},{48,0},{1,17},{17,33},{33,49},{49,1},{2,18}... | collective-permute-start | bytes 196616 | tf_op jit(solution)/shard_map/ppermute | solution.py:33
  60.1 4.0 %collective-permute-start.3 = (bf16[64,512]{1,0:T(8,128)(2,1)S(1)}, bf16[64,512]{1,0:T(8,128)(2,1)S(1)}, u32[]{:S(2)}, u32[]{:S(2)}) collective-permute-start(bf16[64,512]{1,0:T(8,128)(2,1)S(1)} %copy-done.4), channel_id=1, source_target_pairs={{0,32},{16,48},{32,0},{48,16},{1,33},{17,49},{33,1},{49,17},{2,34}... | collective-permute-start | bytes 196616 | tf_op jit(solution)/shard_map/ppermute | solution.py:33
  64.1 6.5 %all-to-all-done.1 = bf16[8,24,1024]{2,1,0:T(8,128)(2,1)S(1)} async-done(((bf16[8,24,1024]{2,1,0:T(8,128)(2,1)}), bf16[8,24,1024]{2,1,0:T(8,128)(2,1)S(1)}, u32[]{:S(2)}, u32[]{:S(2)}) %all-to-all-start.1) | async-done | bytes 393248 | tf_op jit(solution)/shard_map/all_to_all | solution.py:20
  70.6 0.1 convert_reduce_fusion
  70.7 0.0 collective-permute-done.4
  70.7 0.7 broadcast_in_dim.19
  71.5 0.7 pad_maximum_fusion.1
  72.2 0.0 all-gather.3.cloned.1.call-update
  72.2 6.7 %all-to-all-start.2 = ((bf16[8,24,512]{2,1,0:T(8,128)(2,1)}), bf16[8,24,512]{2,1,0:T(8,128)(2,1)S(1)}, u32[]{:S(2)}, u32[]{:S(2)}) async-start(bf16[8,24,512]{2,1,0:T(8,128)(2,1)} %broadcast_in_dim.19), calls=%async_computation.2 | async-start | bytes 393216 | tf_op jit(solution)/shard_map/all_to_all | solution.py:20
  78.9 1.9 %collective-permute-start.5 = (bf16[256,512]{1,0:T(8,128)(2,1)S(1)}, bf16[256,512]{1,0:T(8,128)(2,1)S(1)}, u32[]{:S(2)}, u32[]{:S(2)}) collective-permute-start(bf16[256,512]{1,0:T(8,128)(2,1)S(1)} %copy-done.3), channel_id=1, source_target_pairs={{0,1},{1,0},{2,3},{3,2},{4,5},{5,4},{6,7},{7,6},{8,9},{9,8},{10,11... | collective-permute-start | bytes 786440 | tf_op jit(solution)/shard_map/ppermute | solution.py:28
  80.9 7.8 %all-to-all-done.2 = bf16[8,24,512]{2,1,0:T(8,128)(2,1)S(1)} async-done(((bf16[8,24,512]{2,1,0:T(8,128)(2,1)}), bf16[8,24,512]{2,1,0:T(8,128)(2,1)S(1)}, u32[]{:S(2)}, u32[]{:S(2)}) %all-to-all-start.2) | async-done | bytes 196640 | tf_op jit(solution)/shard_map/all_to_all | solution.py:20
  88.7 0.2 fusion.3
  88.9 0.0 collective-permute-done.5
  88.9 0.2 fusion
  89.2 0.1 reshape.29
  89.2 22.3 %all_to_all.25 = bf16[32,6,512]{2,1,0:T(8,128)(2,1)S(1)} all-to-all(bf16[32,6,512]{2,1,0:T(8,128)(2,1)S(1)} %reshape.29), channel_id=1, replica_groups=mesh['y_lo'=2,'z'=8,'y_hi'=4,'x'=8,'core'=2] {'y_hi','x'}, dimensions={0} | all-to-all | bytes 393216 | tf_op jit(solution)/shard_map/all_to_all | solution.py:20
  111.6 0.1 reduce_sum.22
  111.6 0.7 broadcast_in_dim.38
  112.3 4.2 %all-to-all-start.4 = ((bf16[16,8,512]{2,1,0:T(8,128)(2,1)}), bf16[16,8,512]{2,1,0:T(8,128)(2,1)S(1)}, u32[]{:S(2)}, u32[]{:S(2)}) async-start(bf16[16,8,512]{2,1,0:T(8,128)(2,1)} %broadcast_in_dim.38), calls=%async_computation.4 | async-start | bytes 262144 | tf_op jit(solution)/shard_map/all_to_all | solution.py:20
  116.5 0.1 copy.18.column_ref
  116.7 0.1 copy.19.gate_ref
  116.8 8.3 %all-to-all-done.4 = bf16[16,8,512]{2,1,0:T(8,128)(2,1)S(1)} async-done(((bf16[16,8,512]{2,1,0:T(8,128)(2,1)}), bf16[16,8,512]{2,1,0:T(8,128)(2,1)S(1)}, u32[]{:S(2)}, u32[]{:S(2)}) %all-to-all-start.4) | async-done | bytes 131104 | tf_op jit(solution)/shard_map/all_to_all | solution.py:20
  125.1 2.2 %copy-done = bf16[64,64,512]{2,1,0:T(8,128)(2,1)S(1)} copy-done((bf16[64,64,512]{2,1,0:T(8,128)(2,1)S(1)}, bf16[64,64,512]{2,1,0:T(8,128)(2,1)}, u32[]{:S(2)}) %copy-start) | copy-done | bytes 4194328
  127.3 2.8 %shard_map.131 = (bf16[128,4096]{1,0:T(8,128)(2,1)}, bf16[128,512]{1,0:T(8,128)(2,1)}) custom-call(bf16[128,4096]{1,0:T(8,128)(2,1)S(1)} %copy-done.1, bf16[128,512]{1,0:T(8,128)(2,1)S(1)} %bitcast.28, s32[128,1]{1,0:T(8,128)S(1)} %copy.18.column_ref, f32[128,1]{1,0:T(8,128)S(1)} %copy.19.gate_ref, f32[1,4096]{1,0:T(1,128)S(1)} %bitcast.29, ...), custom_call_target="tpu_custom_call" | custom-call | flops 536870912 | bytes 8388608 | tf_op jit(solution)/shard_map/pallas_call | solution.py:96
  (16 shorter events, 0.1 us)
Async XLA Ops:
  7.2 50.2 %copy-start.4 = (bf16[64,512]{1,0:T(8,128)(2,1)S(1)}, bf16[64,512]{1,0:T(8,128)(2,1)}, u32[]{:S(2)}) copy-start(bf16[64,512]{1,0:T(8,128)(2,1)} %param.23) | copy-start | bytes 196612
  7.2 71.8 %copy-start.3 = (bf16[256,512]{1,0:T(8,128)(2,1)S(1)}, bf16[256,512]{1,0:T(8,128)(2,1)}, u32[]{:S(2)}) copy-start(bf16[256,512]{1,0:T(8,128)(2,1)} %param.21) | copy-start | bytes 786436
  9.7 29.3 %all-to-all-start = ((bf16[32,6,512]{2,1,0:T(8,128)(2,1)}), bf16[32,6,512]{2,1,0:T(8,128)(2,1)S(1)}, u32[]{:S(2)}, u32[]{:S(2)}) async-start(bf16[32,6,512]{2,1,0:T(8,128)(2,1)} %broadcast_in_dim.18), calls=%async_computation | async-start | bytes 524288 | tf_op jit(solution)/shard_map/all_to_all | solution.py:20
  26.4 16.3 %collective-permute-start.2 = (bf16[64,512]{1,0:T(8,128)(2,1)}, bf16[64,512]{1,0:T(8,128)(2,1)S(1)}, u32[]{:S(2)}, u32[]{:S(2)}) collective-permute-start(bf16[64,512]{1,0:T(8,128)(2,1)} %param.23), channel_id=1, source_target_pairs={{0,48},{16,0},{32,16},{48,32},{1,49},{17,1},{33,17},{49,33},{2,50}... | collective-permute-start | bytes 196616 | tf_op jit(solution)/shard_map/ppermute | solution.py:33
  32.1 9.4 %collective-permute-start = (bf16[512,256]{1,0:T(8,128)(2,1)}, bf16[512,256]{1,0:T(8,128)(2,1)S(1)}, u32[]{:S(2)}, u32[]{:S(2)}) collective-permute-start(bf16[512,256]{1,0:T(8,128)(2,1)} %param.19), channel_id=1, source_target_pairs={{0,1},{1,0},{2,3},{3,2},{4,5},{5,4},{6,7},{7,6},{8,9},{9,8},{10,11... | collective-permute-start | bytes 786440 | tf_op jit(solution)/shard_map/ppermute | solution.py:28
  34.0 7.7 %collective-permute-start.1 = (bf16[512,256]{1,0:T(8,128)(2,1)}, bf16[512,256]{1,0:T(8,128)(2,1)S(1)}, u32[]{:S(2)}, u32[]{:S(2)}) collective-permute-start(bf16[512,256]{1,0:T(8,128)(2,1)} %param.20), channel_id=1, source_target_pairs={{0,1},{1,0},{2,3},{3,2},{4,5},{5,4},{6,7},{7,6},{8,9},{9,8},{10,11... | collective-permute-start | bytes 786440 | tf_op jit(solution)/shard_map/ppermute | solution.py:28
  41.6 75.0 %copy-start.5 = (s32[128]{0:T(128)S(1)}, s32[128]{0:T(128)}, u32[]{:S(2)}) copy-start(s32[128]{0:T(128)} %param.14) | copy-start | bytes 1540
  41.7 75.0 %copy-start.6 = (f32[128]{0:T(128)S(1)}, f32[128]{0:T(128)}, u32[]{:S(2)}) copy-start(f32[128]{0:T(128)} %param.17) | copy-start | bytes 1540
  41.7 75.0 %copy-start.7 = (f32[128]{0:T(128)S(1)}, f32[128]{0:T(128)}, u32[]{:S(2)}) copy-start(f32[128]{0:T(128)} %param.18) | copy-start | bytes 1540
  41.7 83.4 %copy-start.1 = (bf16[128,4096]{1,0:T(8,128)(2,1)S(1)}, bf16[128,4096]{1,0:T(8,128)(2,1)}, u32[]{:S(2)}) copy-start(bf16[128,4096]{1,0:T(8,128)(2,1)} %tokens_ref.1) | copy-start | bytes 3145732
  41.7 83.4 %copy-start.2 = (f32[4096]{0:T(1024)S(1)}, f32[4096]{0:T(1024)}, u32[]{:S(2)}) copy-start(f32[4096]{0:T(1024)} %param.22) | copy-start | bytes 49156
  42.7 27.9 %all-to-all-start.1 = ((bf16[8,24,1024]{2,1,0:T(8,128)(2,1)}), bf16[8,24,1024]{2,1,0:T(8,128)(2,1)S(1)}, u32[]{:S(2)}, u32[]{:S(2)}) async-start(bf16[8,24,1024]{2,1,0:T(8,128)(2,1)} %bitcast), calls=%async_computation.1 | async-start | bytes 786432 | tf_op jit(solution)/shard_map/all_to_all | solution.py:20
  57.3 67.8 %all-gather.3.cloned.1.call-start = ((), (), s32[]{:S(2)}) async-start(), calls=%async_computation.5 | async-start | bytes 4456448 | tf_op jit(solution)/shard_map/all_gather | solution.py:174
  57.4 13.3 %collective-permute-start.4 = (bf16[64,512]{1,0:T(8,128)(2,1)S(1)}, bf16[64,512]{1,0:T(8,128)(2,1)S(1)}, u32[]{:S(2)}, u32[]{:S(2)}) collective-permute-start(bf16[64,512]{1,0:T(8,128)(2,1)S(1)} %copy-done.4), channel_id=1, source_target_pairs={{0,16},{16,32},{32,48},{48,0},{1,17},{17,33},{33,49},{49,1},{2,18}... | collective-permute-start | bytes 196616 | tf_op jit(solution)/shard_map/ppermute | solution.py:33
  60.1 10.6 %collective-permute-start.3 = (bf16[64,512]{1,0:T(8,128)(2,1)S(1)}, bf16[64,512]{1,0:T(8,128)(2,1)S(1)}, u32[]{:S(2)}, u32[]{:S(2)}) collective-permute-start(bf16[64,512]{1,0:T(8,128)(2,1)S(1)} %copy-done.4), channel_id=1, source_target_pairs={{0,32},{16,48},{32,0},{48,16},{1,33},{17,49},{33,1},{49,17},{2,34}... | collective-permute-start | bytes 196616 | tf_op jit(solution)/shard_map/ppermute | solution.py:33
  72.2 16.5 %all-to-all-start.2 = ((bf16[8,24,512]{2,1,0:T(8,128)(2,1)}), bf16[8,24,512]{2,1,0:T(8,128)(2,1)S(1)}, u32[]{:S(2)}, u32[]{:S(2)}) async-start(bf16[8,24,512]{2,1,0:T(8,128)(2,1)} %broadcast_in_dim.19), calls=%async_computation.2 | async-start | bytes 393216 | tf_op jit(solution)/shard_map/all_to_all | solution.py:20
  78.9 10.0 %collective-permute-start.5 = (bf16[256,512]{1,0:T(8,128)(2,1)S(1)}, bf16[256,512]{1,0:T(8,128)(2,1)S(1)}, u32[]{:S(2)}, u32[]{:S(2)}) collective-permute-start(bf16[256,512]{1,0:T(8,128)(2,1)S(1)} %copy-done.3), channel_id=1, source_target_pairs={{0,1},{1,0},{2,3},{3,2},{4,5},{5,4},{6,7},{7,6},{8,9},{9,8},{10,11... | collective-permute-start | bytes 786440 | tf_op jit(solution)/shard_map/ppermute | solution.py:28
  112.3 12.8 %all-to-all-start.4 = ((bf16[16,8,512]{2,1,0:T(8,128)(2,1)}), bf16[16,8,512]{2,1,0:T(8,128)(2,1)S(1)}, u32[]{:S(2)}, u32[]{:S(2)}) async-start(bf16[16,8,512]{2,1,0:T(8,128)(2,1)} %broadcast_in_dim.38), calls=%async_computation.4 | async-start | bytes 262144 | tf_op jit(solution)/shard_map/all_to_all | solution.py:20
  125.1 2.2 %copy-start = (bf16[64,64,512]{2,1,0:T(8,128)(2,1)S(1)}, bf16[64,64,512]{2,1,0:T(8,128)(2,1)}, u32[]{:S(2)}) copy-start(bf16[64,64,512]{2,1,0:T(8,128)(2,1)} %all-gather.3.cloned.1.call-done) | copy-start | bytes 12582916
Sparse Core Ops, SparseCore 0:
  72.3 45.4 all-gather.2

commit v6 on v5

--- a/solution.py
+++ b/solution.py
@@ -20,21 +20,83 @@
     return lax.all_to_all(blocks, axes, split_axis=0, concat_axis=0, tiled=True)
 
 
-def copies(block, axes):
-    return jnp.broadcast_to(block[None], (lax.axis_size(axes),) + block.shape)
-
-
 def other_core(block):
     return lax.ppermute(block, "core", [(0, 1), (1, 0)])
 
 
-def along(axis, block, distance):
-    count = lax.axis_size(axis)
-    return lax.ppermute(block, axis, [(i, (i + distance) % count) for i in range(count)])
+def across(block, bit):
+    return lax.ppermute(block, "y_hi", [(i, i ^ bit) for i in range(lax.axis_size("y_hi"))])
+
+
+def in_order(own, other, bit):
+    upper = (lax.axis_index("y_hi") & bit) != 0
+    return jnp.concatenate([jnp.where(upper, other, own), jnp.where(upper, own, other)], axis=0)
 
 
 def tie(*values):
     return lax.optimization_barrier(values)
+
+
+def small_call(kernel, shape, vmem_count, *operands, scratch=()):
+    vmem = pl.BlockSpec(memory_space=pltpu.VMEM)
+    outside = len(operands) - vmem_count
+    size = 1
+    for extent in shape:
+        size *= extent
+    return pl.pallas_call(
+        kernel,
+        out_shape=jax.ShapeDtypeStruct(shape, jnp.bfloat16),
+        in_specs=[pl.BlockSpec(memory_space=pltpu.HBM)] * outside + [vmem] * vmem_count,
+        out_specs=vmem,
+        scratch_shapes=list(scratch),
+        compiler_params=pltpu.CompilerParams(vmem_limit_bytes=16 * 1024 * 1024),
+        cost_estimate=pl.CostEstimate(flops=2 * size, bytes_accessed=4 * size, transcendentals=0),
+    )(*operands)
+
+
+def slots_kernel(tokens_hbm, expert_ref, slot_ref, out_ref, block_ref, sem):
+    width = block_ref.shape[1]
+    start = pl.multiple_of(lax.axis_index("z") * width, LANES)
+    load = pltpu.make_async_copy(tokens_hbm.at[:, pl.ds(start, width)], block_ref, sem)
+    load.start()
+    placement = jnp.where(expert_ref[...] == lax.axis_index("y_lo"), slot_ref[...], -1)
+    slots = lax.broadcasted_iota(jnp.int32, (PADDED, placement.shape[1]), 0)
+    hot = (slots == placement).astype(jnp.bfloat16)
+    load.wait()
+    rows = jnp.dot(hot, block_ref[...], preferred_element_type=jnp.float32).astype(jnp.bfloat16)
+    for i in range(out_ref.shape[0]):
+        out_ref[i] = rows[:SLOTS]
+
+
+def products_kernel(rows_ref, *refs):
+    out_ref = refs[-1]
+    rows = rows_ref[...]
+    units = refs[0].shape[1]
+    for i, w_ref in enumerate(refs[:-1]):
+        out_ref[:, i * units : (i + 1) * units] = jnp.dot(
+            rows, w_ref[...], preferred_element_type=jnp.float32
+        ).astype(jnp.bfloat16)
+
+
+def hidden_kernel(parts_ref, out_ref):
+    units = out_ref.shape[2]
+    total = parts_ref[0].astype(jnp.float32)
+    for i in range(1, parts_ref.shape[0]):
+        total += parts_ref[i].astype(jnp.float32)
+    gate, up = total[:, :units], total[:, units:]
+    hidden = (gate / (1.0 + jnp.exp(-gate)) * up).astype(jnp.bfloat16)
+    for i in range(out_ref.shape[0]):
+        out_ref[i] = hidden
+
+
+def total_kernel(parts_ref, out_ref):
+    total = parts_ref[0].astype(jnp.float32)
+    for i in range(1, parts_ref.shape[0]):
+        total += parts_ref[i].astype(jnp.float32)
+    rows = jnp.concatenate([total, jnp.zeros((PADDED - SLOTS, total.shape[1]), jnp.float32)], axis=0)
+    rows = rows.astype(jnp.bfloat16)
+    for i in range(out_ref.shape[0]):
+        out_ref[i] = rows
 
 
 def finish_kernel(
@@ -99,7 +161,7 @@
             jax.ShapeDtypeStruct((tok_count, width), jnp.bfloat16),
             jax.ShapeDtypeStruct((tok_count, columns), jnp.bfloat16),
         ),
-        in_specs=[vmem] * 5 + [pl.BlockSpec(memory_space=pl.ANY)],
+        in_specs=[vmem] * 5 + [pl.BlockSpec(memory_space=pltpu.HBM)],
         out_specs=(vmem, vmem),
         scratch_shapes=[
             pltpu.VMEM((tok_count, width), jnp.bfloat16),
@@ -132,8 +194,7 @@
     chips = lax.axis_size(CHIPS)
     block_width = width // blocks
     units = w_gate.shape[1]
-    own_expert = lax.axis_index("y_lo")
-    own_block = lax.axis_index("z")
+    experts = lax.axis_size("y_lo")
 
     served_first = first_slot >= 0
     served = served_first | (second_slot >= 0)
@@ -141,36 +202,32 @@
     slot_of = jnp.where(served_first, first_slot, second_slot + CAP1)
     gate_of = jnp.where(served_first, first_gate, second_gate)
 
-    token_block = lax.dynamic_slice_in_dim(tokens, own_block * block_width, block_width, 1)
-    placement = jnp.where(served & (expert_of == own_expert), slot_of, -1)
-    slot_hot = (jnp.arange(SLOTS, dtype=jnp.int32)[:, None] == placement[None, :]).astype(jnp.bfloat16)
-    slot_rows = jnp.dot(slot_hot, token_block, preferred_element_type=jnp.float32).astype(jnp.bfloat16)
-
-    slot_copies, w_query = tie(copies(slot_rows, CHIPS), w_query)
+    slot_copies = small_call(
+        slots_kernel,
+        (chips, SLOTS, block_width),
+        2,
+        tokens,
+        expert_of[None, :],
+        jnp.where(served, slot_of, -1)[None, :],
+        scratch=(pltpu.VMEM((tok_count, block_width), jnp.bfloat16), pltpu.SemaphoreType.DMA(())),
+    )
+    slot_copies, w_query = tie(slot_copies, w_query)
     rows = exchange(slot_copies, CHIPS).reshape(chips * SLOTS, block_width)
     w_gate_other = other_core(w_gate)
     w_up_other = other_core(w_up)
-    query_rows = [w_query, along("y_hi", w_query, -1)]
-
-    partial = jnp.concatenate(
-        [
-            jnp.dot(rows, w, preferred_element_type=jnp.float32).astype(jnp.bfloat16)
-            for w in (w_gate, w_gate_other, w_up, w_up_other)
-        ],
-        axis=1,
+    w_query_beside = across(w_query, 1)
+
+    partial = small_call(
+        products_kernel, (chips * SLOTS, 4 * units), 5, rows, w_gate, w_gate_other, w_up, w_up_other
     )
     share = chips * SLOTS // blocks
-    partial, *query_rows = tie(partial, *query_rows)
+    partial, w_query, w_query_beside = tie(partial, w_query, w_query_beside)
     summed = exchange(partial.reshape(blocks, share, 4 * units), "z")
-    query_rows += [along("y_hi", query_rows[0], -2), along("y_hi", query_rows[0], -3)]
-    summed = jnp.sum(summed.astype(jnp.float32), axis=0)
-    hidden_share = (jax.nn.silu(summed[:, : 2 * units]) * summed[:, 2 * units :]).astype(jnp.bfloat16)
-    hidden_copies, *query_rows = tie(copies(hidden_share, "z"), *query_rows)
-    for bit in (1, 2):
-        turned = query_rows[-bit:] + query_rows[:-bit]
-        set_bit = (lax.axis_index("y_hi") & bit) != 0
-        query_rows = [jnp.where(set_bit, t, q) for t, q in zip(turned, query_rows, strict=True)]
-    column_rows = jnp.stack(query_rows)
+    query_rows = in_order(w_query, w_query_beside, 1)
+    query_rows_other = across(query_rows, 2)
+    hidden_copies = small_call(hidden_kernel, (blocks, share, 2 * units), 1, summed)
+    hidden_copies, query_rows_other = tie(hidden_copies, query_rows_other)
+    column_rows = in_order(query_rows, query_rows_other, 2).reshape((-1,) + w_query.shape)
     w_query_full = lax.all_gather(column_rows, ("x", "core"), axis=0)
     w_query_full = w_query_full.reshape((-1, 2) + column_rows.shape)
     hidden = exchange(hidden_copies, "z").reshape(chips * SLOTS, 2 * units)
@@ -180,9 +237,8 @@
     )
     out_part = out_part.astype(jnp.bfloat16)
     pieces = exchange(out_part.reshape(chips, SLOTS, block_width), CHIPS)
-    expert_out = jnp.sum(pieces.astype(jnp.float32), axis=0).astype(jnp.bfloat16)
-    expert_out = jnp.concatenate([expert_out, jnp.zeros((PADDED - SLOTS, block_width), jnp.bfloat16)], 0)
-    table = exchange(copies(expert_out, EXPERT), EXPERT).reshape(-1, block_width)
+    out_copies = small_call(total_kernel, (experts * blocks, PADDED, block_width), 1, pieces)
+    table = exchange(out_copies, EXPERT).reshape(-1, block_width)
 
     column = jnp.where(served, expert_of * PADDED + slot_of, -1)
     return finish(tokens, table, column, gate_of, norm_gain, w_query_full)

time: 138 us -> 136 us (0.986)
  starting transfers between devices: 60.9 us -> 53.5 us
  waiting for transfers between devices: 25.3 us -> 30.5 us
  matrix products: 4.19 us -> 0.41 us
  Pallas kernels: 2.79 us -> 6.27 us
    ppermute x3 -> x2, starting transfers between devices: 12.4 us -> 7.11 us  [across(): lax.ppermute(block, 'y_hi', [(i, i ^ bit) for i in range(lax.axis_size('y...]
    all_to_all x4, waiting for transfers between devices: 25.3 us -> 30.4 us  [exchange(): return lax.all_to_all(blocks, axes, split_axis=0, concat_axis=0, tiled=True)]
    dot_general x5 -> x0, matrix products: 3.77 us -> none  [the longest x4 2.74 us: local(): jnp.dot(rows, w, preferred_element_type=jnp.float32).astype(jnp.bfloat16)]
    pallas_call x0 -> x4, Pallas kernels: none -> 3.48 us  [small_call(): pl.pallas_call(kernel, out_shape=jax.ShapeDtypeStruct(shape, jnp.bfloat16...]
    unnamed x16 -> x22, local copies, waits for them, and re-layouts: 2.23 us -> 5.42 us
    broadcast_in_dim x3 -> x0, local copies, waits for them, and re-layouts: 2.09 us -> none  [copies(): return jnp.broadcast_to(block[None], (lax.axis_size(axes),) + block.shape)]
    all_to_all x4, starting transfers between devices: 42.2 us -> 40.1 us  [exchange(): return lax.all_to_all(blocks, axes, split_axis=0, concat_axis=0, tiled=True)]
  transfers between devices with their start and end apart: 11 -> 10, of which waited for: 4 -> 4; matrix products, arithmetic and copies ran while one was open for 4% -> 1% of each run, Pallas kernels for 0% -> 2%
where the time goes in v6:
time: 136 us
  starting transfers between devices  53.5 us (39%)
  waiting for transfers between devices  30.5 us (22%)
  blocking collectives  23.5 us (17%)
  between operations  14.3 us (11%)
  Pallas kernels  6.27 us (5%)
  local copies, waits for them, and re-layouts  5.78 us (4%)
  other arithmetic  1.51 us (1%)
    all_to_all x4, starting transfers between devices, exchange(): return lax.all_to_all(blocks, axes, split_axis=0, concat_axis=0, tiled=True)  40.1 us
    all_to_all x4, waiting for transfers between devices, exchange(): return lax.all_to_all(blocks, axes, split_axis=0, concat_axis=0, tiled=True)  30.4 us
    all_to_all x1, blocking collectives, exchange(): return lax.all_to_all(blocks, axes, split_axis=0, concat_axis=0, tiled=True)  23.5 us
    ppermute x2, starting transfers between devices, across(): lax.ppermute(block, 'y_hi', [(i, i ^ bit) for i in range(lax.axis_size('y...  7.11 us
    ppermute x3, starting transfers between devices, other_core(): return lax.ppermute(block, 'core', [(0, 1), (1, 0)])  6.25 us
    unnamed x22, local copies, waits for them, and re-layouts  5.42 us
    pallas_call x4, Pallas kernels, small_call(): pl.pallas_call(kernel, out_shape=jax.ShapeDtypeStruct(shape, jnp.bfloat16...  3.48 us
    pallas_call x1, Pallas kernels, finish(): pl.pallas_call(finish_kernel, out_shape=(jax.ShapeDtypeStruct((tok_count,...  2.79 us
  transfers between devices with their start and end apart: 10, of which 4 were waited for; matrix products, arithmetic and copies ran while one was open for 1% of the time, Pallas kernels for 2%

profile of v6, /device:TPU:4, one launch (start us, length us, event | category | flops | bytes accessed | tf_op | source)
XLA Modules:
  0.0 135.7 jit_solution(1529442351164508579)
XLA Ops:
  7.2 0.7 select_bitcast_fusion.1
  7.9 0.0 copy-start.1
  7.9 1.2 copy-done.1
  9.1 0.9 shard_map.131
  10.0 16.7 %all-to-all-start = ((bf16[32,6,512]{2,1,0:T(8,128)(2,1)}), bf16[32,6,512]{2,1,0:T(8,128)(2,1)S(1)}, u32[]{:S(2)}, u32[]{:S(2)}) async-start(bf16[32,6,512]{2,1,0:T(8,128)(2,1)} %shard_map.131), calls=%async_computation | async-start | bytes 524288 | tf_op jit(solution)/shard_map/all_to_all | solution.py:20
  26.7 1.9 %collective-permute-start = (bf16[512,256]{1,0:T(8,128)(2,1)}, bf16[512,256]{1,0:T(8,128)(2,1)S(1)}, u32[]{:S(2)}, u32[]{:S(2)}) collective-permute-start(bf16[512,256]{1,0:T(8,128)(2,1)} %refs_0_.1), channel_id=1, source_target_pairs={{0,1},{1,0},{2,3},{3,2},{4,5},{5,4},{6,7},{7,6},{8,9},{9,8},{10,11... | collective-permute-start | bytes 786440 | tf_op jit(solution)/shard_map/ppermute | solution.py:24
  28.6 2.4 %collective-permute-start.1 = (bf16[512,256]{1,0:T(8,128)(2,1)}, bf16[512,256]{1,0:T(8,128)(2,1)S(1)}, u32[]{:S(2)}, u32[]{:S(2)}) collective-permute-start(bf16[512,256]{1,0:T(8,128)(2,1)} %refs_2_.1), channel_id=1, source_target_pairs={{0,1},{1,0},{2,3},{3,2},{4,5},{5,4},{6,7},{7,6},{8,9},{9,8},{10,11... | collective-permute-start | bytes 786440 | tf_op jit(solution)/shard_map/ppermute | solution.py:24
  31.1 4.3 %collective-permute-start.2 = (bf16[64,512]{1,0:T(8,128)(2,1)}, bf16[64,512]{1,0:T(8,128)(2,1)S(1)}, u32[]{:S(2)}, u32[]{:S(2)}) collective-permute-start(bf16[64,512]{1,0:T(8,128)(2,1)} %param.23), channel_id=1, source_target_pairs={{0,16},{16,0},{32,48},{48,32},{1,17},{17,1},{33,49},{49,33},{2,18}... | collective-permute-start | bytes 196616 | tf_op jit(solution)/shard_map/ppermute | solution.py:28
  35.4 3.9 %all-to-all-done = bf16[32,6,512]{2,1,0:T(8,128)(2,1)S(1)} async-done(((bf16[32,6,512]{2,1,0:T(8,128)(2,1)}), bf16[32,6,512]{2,1,0:T(8,128)(2,1)S(1)}, u32[]{:S(2)}, u32[]{:S(2)}) %all-to-all-start) | async-done | bytes 196640 | tf_op jit(solution)/shard_map/all_to_all | solution.py:20
  39.3 0.1 reshape.22.rows_ref
  39.4 0.0 copy-start.2
  39.4 0.0 collective-permute-done.refs_1_
  39.4 0.0 collective-permute-done.1.refs_3_
  39.4 0.0 copy-start.3
  39.4 1.0 copy-done.3
  40.5 0.9 copy-done.4
  41.4 1.1 shard_map.132
  42.5 0.0 collective-permute-done.2
  42.5 14.6 %all-to-all-start.1 = ((bf16[8,24,1024]{2,1,0:T(8,128)(2,1)}), bf16[8,24,1024]{2,1,0:T(8,128)(2,1)S(1)}, u32[]{:S(2)}, u32[]{:S(2)}) async-start(bf16[8,24,1024]{2,1,0:T(8,128)(2,1)} %bitcast.2), calls=%async_computation.1 | async-start | bytes 786432 | tf_op jit(solution)/shard_map/all_to_all | solution.py:20
  57.1 0.0 all-gather.2.cloned.1.call-start
  57.2 0.0 copy-done.7
  57.2 2.8 %collective-permute-start.3 = (bf16[128,512]{1,0:T(8,128)(2,1)S(1)}, bf16[128,512]{1,0:T(8,128)(2,1)S(1)}, u32[]{:S(2)}, u32[]{:S(2)}) collective-permute-start(bf16[128,512]{1,0:T(8,128)(2,1)S(1)} %pad_maximum_fusion.1), channel_id=1, source_target_pairs={{0,32},{16,48},{32,0},{48,16},{1,33},{17,49},{33,1},{49,17},{2,34}... | collective-permute-start | bytes 393224 | tf_op jit(solution)/shard_map/ppermute | solution.py:28
  60.0 10.4 %all-to-all-done.1.parts_ref = bf16[8,24,1024]{2,1,0:T(8,128)(2,1)S(1)} async-done(((bf16[8,24,1024]{2,1,0:T(8,128)(2,1)}), bf16[8,24,1024]{2,1,0:T(8,128)(2,1)S(1)}, u32[]{:S(2)}, u32[]{:S(2)}) %all-to-all-start.1) | async-done | bytes 393248 | tf_op jit(solution)/shard_map/all_to_all | solution.py:20
  70.4 0.8 shard_map.133
  71.2 0.0 collective-permute-done.3
  71.3 0.7 pad_maximum_fusion
  72.0 0.0 all-gather.2.cloned.1.call-update
  72.0 5.3 %all-to-all-start.2 = ((bf16[8,24,512]{2,1,0:T(8,128)(2,1)}), bf16[8,24,512]{2,1,0:T(8,128)(2,1)S(1)}, u32[]{:S(2)}, u32[]{:S(2)}) async-start(bf16[8,24,512]{2,1,0:T(8,128)(2,1)} %shard_map.133), calls=%async_computation.2 | async-start | bytes 393216 | tf_op jit(solution)/shard_map/all_to_all | solution.py:20
  77.3 0.0 copy-done.6
  77.4 1.9 %collective-permute-start.4 = (bf16[256,512]{1,0:T(8,128)(2,1)S(1)}, bf16[256,512]{1,0:T(8,128)(2,1)S(1)}, u32[]{:S(2)}, u32[]{:S(2)}) collective-permute-start(bf16[256,512]{1,0:T(8,128)(2,1)S(1)} %copy-done.6), channel_id=1, source_target_pairs={{0,1},{1,0},{2,3},{3,2},{4,5},{5,4},{6,7},{7,6},{8,9},{9,8},{10,11... | collective-permute-start | bytes 786440 | tf_op jit(solution)/shard_map/ppermute | solution.py:24
  79.3 7.8 %all-to-all-done.2 = bf16[8,24,512]{2,1,0:T(8,128)(2,1)S(1)} async-done(((bf16[8,24,512]{2,1,0:T(8,128)(2,1)}), bf16[8,24,512]{2,1,0:T(8,128)(2,1)S(1)}, u32[]{:S(2)}, u32[]{:S(2)}) %all-to-all-start.2) | async-done | bytes 196640 | tf_op jit(solution)/shard_map/all_to_all | solution.py:20
  87.1 0.2 fusion.2
  87.3 0.0 collective-permute-done.4
  87.3 0.2 fusion
  87.6 0.1 reshape.25
  87.6 23.5 %all_to_all.25.parts_ref = bf16[32,6,512]{2,1,0:T(8,128)(2,1)S(1)} all-to-all(bf16[32,6,512]{2,1,0:T(8,128)(2,1)S(1)} %reshape.25), channel_id=1, replica_groups=mesh['y_lo'=2,'z'=8,'y_hi'=4,'x'=8,'core'=2] {'y_hi','x'}, dimensions={0} | all-to-all | bytes 393216 | tf_op jit(solution)/shard_map/all_to_all | solution.py:20
  111.1 0.7 shard_map.134
  111.8 3.5 %all-to-all-start.4 = ((bf16[16,8,512]{2,1,0:T(8,128)(2,1)}), bf16[16,8,512]{2,1,0:T(8,128)(2,1)S(1)}, u32[]{:S(2)}, u32[]{:S(2)}) async-start(bf16[16,8,512]{2,1,0:T(8,128)(2,1)} %shard_map.134), calls=%async_computation.4 | async-start | bytes 262144 | tf_op jit(solution)/shard_map/all_to_all | solution.py:20
  115.4 0.1 copy.18.column_ref
  115.5 0.0 copy-done.8
  115.5 0.0 copy-done.9
  115.5 0.0 copy-done.10
  115.5 0.1 copy.19.gate_ref
  115.6 8.3 %all-to-all-done.4 = bf16[16,8,512]{2,1,0:T(8,128)(2,1)S(1)} async-done(((bf16[16,8,512]{2,1,0:T(8,128)(2,1)}), bf16[16,8,512]{2,1,0:T(8,128)(2,1)S(1)}, u32[]{:S(2)}, u32[]{:S(2)}) %all-to-all-start.4) | async-done | bytes 131104 | tf_op jit(solution)/shard_map/all_to_all | solution.py:20
  123.9 0.0 copy-done.5
  123.9 0.0 copy-done.2
  123.9 2.2 %copy-done = bf16[16,4,64,512]{3,2,1,0:T(8,128)(2,1)S(1)} copy-done((bf16[16,4,64,512]{3,2,1,0:T(8,128)(2,1)S(1)}, bf16[16,4,64,512]{3,2,1,0:T(8,128)(2,1)}, u32[]{:S(2)}) %copy-start) | copy-done | bytes 4194328
  126.1 2.8 %shard_map.135 = (bf16[128,4096]{1,0:T(8,128)(2,1)}, bf16[128,512]{1,0:T(8,128)(2,1)}) custom-call(bf16[128,4096]{1,0:T(8,128)(2,1)S(1)} %copy-done.2, bf16[128,512]{1,0:T(8,128)(2,1)S(1)} %bitcast.17, s32[128,1]{1,0:T(8,128)S(1)} %copy.18.column_ref, f32[128,1]{1,0:T(8,128)S(1)} %copy.19.gate_ref, f32[1,4096]{1,0:T(1,128)S(1)} %bitcast.18, ...), custom_call_target="tpu_custom_call" | custom-call | flops 536870912 | bytes 8388608 | tf_op jit(solution)/shard_map/pallas_call | solution.py:158
  (13 shorter events, 0.1 us)
Async XLA Ops:
  7.9 1.2 copy-start.1
  9.1 48.1 %copy-start.7 = (bf16[64,512]{1,0:T(8,128)(2,1)S(1)}, bf16[64,512]{1,0:T(8,128)(2,1)}, u32[]{:S(2)}) copy-start(bf16[64,512]{1,0:T(8,128)(2,1)} %param.23) | copy-start | bytes 196612
  9.1 68.2 %copy-start.6 = (bf16[256,512]{1,0:T(8,128)(2,1)S(1)}, bf16[256,512]{1,0:T(8,128)(2,1)}, u32[]{:S(2)}) copy-start(bf16[256,512]{1,0:T(8,128)(2,1)} %param.21) | copy-start | bytes 786436
  10.0 29.3 %all-to-all-start = ((bf16[32,6,512]{2,1,0:T(8,128)(2,1)}), bf16[32,6,512]{2,1,0:T(8,128)(2,1)S(1)}, u32[]{:S(2)}, u32[]{:S(2)}) async-start(bf16[32,6,512]{2,1,0:T(8,128)(2,1)} %shard_map.131), calls=%async_computation | async-start | bytes 524288 | tf_op jit(solution)/shard_map/all_to_all | solution.py:20
  26.7 12.7 %collective-permute-start = (bf16[512,256]{1,0:T(8,128)(2,1)}, bf16[512,256]{1,0:T(8,128)(2,1)S(1)}, u32[]{:S(2)}, u32[]{:S(2)}) collective-permute-start(bf16[512,256]{1,0:T(8,128)(2,1)} %refs_0_.1), channel_id=1, source_target_pairs={{0,1},{1,0},{2,3},{3,2},{4,5},{5,4},{6,7},{7,6},{8,9},{9,8},{10,11... | collective-permute-start | bytes 786440 | tf_op jit(solution)/shard_map/ppermute | solution.py:24
  28.6 10.8 %collective-permute-start.1 = (bf16[512,256]{1,0:T(8,128)(2,1)}, bf16[512,256]{1,0:T(8,128)(2,1)S(1)}, u32[]{:S(2)}, u32[]{:S(2)}) collective-permute-start(bf16[512,256]{1,0:T(8,128)(2,1)} %refs_2_.1), channel_id=1, source_target_pairs={{0,1},{1,0},{2,3},{3,2},{4,5},{5,4},{6,7},{7,6},{8,9},{9,8},{10,11... | collective-permute-start | bytes 786440 | tf_op jit(solution)/shard_map/ppermute | solution.py:24
  31.1 11.5 %collective-permute-start.2 = (bf16[64,512]{1,0:T(8,128)(2,1)}, bf16[64,512]{1,0:T(8,128)(2,1)S(1)}, u32[]{:S(2)}, u32[]{:S(2)}) collective-permute-start(bf16[64,512]{1,0:T(8,128)(2,1)} %param.23), channel_id=1, source_target_pairs={{0,16},{16,0},{32,48},{48,32},{1,17},{17,1},{33,49},{49,33},{2,18}... | collective-permute-start | bytes 196616 | tf_op jit(solution)/shard_map/ppermute | solution.py:28
  39.3 76.2 %copy-start.8 = (s32[128]{0:T(128)S(1)}, s32[128]{0:T(128)}, u32[]{:S(2)}) copy-start(s32[128]{0:T(128)} %param.14) | copy-start | bytes 1540
  39.3 76.2 %copy-start.9 = (f32[128]{0:T(128)S(1)}, f32[128]{0:T(128)}, u32[]{:S(2)}) copy-start(f32[128]{0:T(128)} %param.17) | copy-start | bytes 1540
  39.3 76.2 %copy-start.10 = (f32[128]{0:T(128)S(1)}, f32[128]{0:T(128)}, u32[]{:S(2)}) copy-start(f32[128]{0:T(128)} %param.18) | copy-start | bytes 1540
  39.3 84.6 %copy-start.5 = (f32[4096]{0:T(1024)S(1)}, f32[4096]{0:T(1024)}, u32[]{:S(2)}) copy-start(f32[4096]{0:T(1024)} %param.22) | copy-start | bytes 49156
  39.4 84.5 %copy-start.2 = (bf16[128,4096]{1,0:T(8,128)(2,1)S(1)}, bf16[128,4096]{1,0:T(8,128)(2,1)}, u32[]{:S(2)}) copy-start(bf16[128,4096]{1,0:T(8,128)(2,1)} %tokens_ref.1) | copy-start | bytes 3145732
  39.4 1.0 copy-start.3
  40.5 0.9 copy-start.4
  42.5 27.9 %all-to-all-start.1 = ((bf16[8,24,1024]{2,1,0:T(8,128)(2,1)}), bf16[8,24,1024]{2,1,0:T(8,128)(2,1)S(1)}, u32[]{:S(2)}, u32[]{:S(2)}) async-start(bf16[8,24,1024]{2,1,0:T(8,128)(2,1)} %bitcast.2), calls=%async_computation.1 | async-start | bytes 786432 | tf_op jit(solution)/shard_map/all_to_all | solution.py:20
  57.1 66.8 %all-gather.2.cloned.1.call-start = ((), (), s32[]{:S(2)}) async-start(), calls=%async_computation.5 | async-start | bytes 4456448 | tf_op jit(solution)/shard_map/all_gather | solution.py:231
  57.2 14.0 %collective-permute-start.3 = (bf16[128,512]{1,0:T(8,128)(2,1)S(1)}, bf16[128,512]{1,0:T(8,128)(2,1)S(1)}, u32[]{:S(2)}, u32[]{:S(2)}) collective-permute-start(bf16[128,512]{1,0:T(8,128)(2,1)S(1)} %pad_maximum_fusion.1), channel_id=1, source_target_pairs={{0,32},{16,48},{32,0},{48,16},{1,33},{17,49},{33,1},{49,17},{2,34}... | collective-permute-start | bytes 393224 | tf_op jit(solution)/shard_map/ppermute | solution.py:28
  72.0 15.1 %all-to-all-start.2 = ((bf16[8,24,512]{2,1,0:T(8,128)(2,1)}), bf16[8,24,512]{2,1,0:T(8,128)(2,1)S(1)}, u32[]{:S(2)}, u32[]{:S(2)}) async-start(bf16[8,24,512]{2,1,0:T(8,128)(2,1)} %shard_map.133), calls=%async_computation.2 | async-start | bytes 393216 | tf_op jit(solution)/shard_map/all_to_all | solution.py:20
  77.4 10.0 %collective-permute-start.4 = (bf16[256,512]{1,0:T(8,128)(2,1)S(1)}, bf16[256,512]{1,0:T(8,128)(2,1)S(1)}, u32[]{:S(2)}, u32[]{:S(2)}) collective-permute-start(bf16[256,512]{1,0:T(8,128)(2,1)S(1)} %copy-done.6), channel_id=1, source_target_pairs={{0,1},{1,0},{2,3},{3,2},{4,5},{5,4},{6,7},{7,6},{8,9},{9,8},{10,11... | collective-permute-start | bytes 786440 | tf_op jit(solution)/shard_map/ppermute | solution.py:24
  111.8 12.0 %all-to-all-start.4 = ((bf16[16,8,512]{2,1,0:T(8,128)(2,1)}), bf16[16,8,512]{2,1,0:T(8,128)(2,1)S(1)}, u32[]{:S(2)}, u32[]{:S(2)}) async-start(bf16[16,8,512]{2,1,0:T(8,128)(2,1)} %shard_map.134), calls=%async_computation.4 | async-start | bytes 262144 | tf_op jit(solution)/shard_map/all_to_all | solution.py:20
  123.9 2.2 %copy-start = (bf16[16,4,64,512]{3,2,1,0:T(8,128)(2,1)S(1)}, bf16[16,4,64,512]{3,2,1,0:T(8,128)(2,1)}, u32[]{:S(2)}) copy-start(bf16[16,4,64,512]{3,2,1,0:T(8,128)(2,1)} %all-gather.2.cloned.1.call-done) | copy-start | bytes 12582916
Sparse Core Ops, SparseCore 0:
  72.1 45.3 all-gather.1

commit v7 on v6

--- a/solution.py
+++ b/solution.py
@@ -14,6 +14,8 @@
 SIZES = {"y_lo": 2, "z": 8, "y_hi": 4, "x": 8, "core": 2}
 PADDED = 8
 LANES = 128
+VMEM_BYTES = 60 * 1024 * 1024
+FINISH_BYTES = 50 * 1024 * 1024
 
 
 def exchange(blocks, axes):
@@ -49,17 +51,22 @@
         in_specs=[pl.BlockSpec(memory_space=pltpu.HBM)] * outside + [vmem] * vmem_count,
         out_specs=vmem,
         scratch_shapes=list(scratch),
-        compiler_params=pltpu.CompilerParams(vmem_limit_bytes=16 * 1024 * 1024),
+        compiler_params=pltpu.CompilerParams(vmem_limit_bytes=VMEM_BYTES if outside else VMEM_BYTES // 4),
         cost_estimate=pl.CostEstimate(flops=2 * size, bytes_accessed=4 * size, transcendentals=0),
     )(*operands)
 
 
-def slots_kernel(tokens_hbm, expert_ref, slot_ref, out_ref, block_ref, sem):
+def slots_kernel(
+    tokens_hbm, first_expert_ref, first_slot_ref, second_expert_ref, second_slot_ref, out_ref, block_ref, sem
+):
     width = block_ref.shape[1]
     start = pl.multiple_of(lax.axis_index("z") * width, LANES)
     load = pltpu.make_async_copy(tokens_hbm.at[:, pl.ds(start, width)], block_ref, sem)
     load.start()
-    placement = jnp.where(expert_ref[...] == lax.axis_index("y_lo"), slot_ref[...], -1)
+    own = lax.axis_index("y_lo")
+    first, second = first_slot_ref[...], second_slot_ref[...]
+    placement = jnp.where((second_expert_ref[...] == own) & (second >= 0), second + CAP1, -1)
+    placement = jnp.where((first_expert_ref[...] == own) & (first >= 0), first, placement)
     slots = lax.broadcasted_iota(jnp.int32, (PADDED, placement.shape[1]), 0)
     hot = (slots == placement).astype(jnp.bfloat16)
     load.wait()
@@ -168,7 +175,7 @@
             pltpu.VMEM(w_query.shape, jnp.bfloat16),
             pltpu.SemaphoreType.DMA((w_query.shape[0],)),
         ],
-        compiler_params=pltpu.CompilerParams(vmem_limit_bytes=24 * 1024 * 1024),
+        compiler_params=pltpu.CompilerParams(vmem_limit_bytes=FINISH_BYTES),
         cost_estimate=pl.CostEstimate(
             flops=2 * tok_count * width * columns, bytes_accessed=4 * width * columns, transcendentals=0
         ),
@@ -205,10 +212,12 @@
     slot_copies = small_call(
         slots_kernel,
         (chips, SLOTS, block_width),
-        2,
+        4,
         tokens,
-        expert_of[None, :],
-        jnp.where(served, slot_of, -1)[None, :],
+        first_expert[None, :],
+        first_slot[None, :],
+        second_expert[None, :],
+        second_slot[None, :],
         scratch=(pltpu.VMEM((tok_count, block_width), jnp.bfloat16), pltpu.SemaphoreType.DMA(())),
     )
     slot_copies, w_query = tie(slot_copies, w_query)
@@ -227,9 +236,9 @@
     query_rows_other = across(query_rows, 2)
     hidden_copies = small_call(hidden_kernel, (blocks, share, 2 * units), 1, summed)
     hidden_copies, query_rows_other = tie(hidden_copies, query_rows_other)
-    column_rows = in_order(query_rows, query_rows_other, 2).reshape((-1,) + w_query.shape)
-    w_query_full = lax.all_gather(column_rows, ("x", "core"), axis=0)
-    w_query_full = w_query_full.reshape((-1, 2) + column_rows.shape)
+    query_rows = in_order(query_rows, query_rows_other, 2).reshape((-1,) + w_query.shape)
+    w_query_full = lax.all_gather(query_rows, ("x", "core"), axis=0)
+    w_query_full = w_query_full.reshape((-1, 2) + query_rows.shape)
     hidden = exchange(hidden_copies, "z").reshape(chips * SLOTS, 2 * units)
     w_down_other = other_core(w_down)
     out_part = jnp.dot(hidden[:, :units], w_down, preferred_element_type=jnp.float32) + jnp.dot(

time: 136 us -> 135 us (level)
  local copies, waits for them, and re-layouts: 5.78 us -> 2.39 us
  Pallas kernels: 6.27 us -> 8.84 us
    unnamed x22 -> x24, local copies, waits for them, and re-layouts: 5.42 us -> 2.03 us
    pallas_call x4, Pallas kernels: 3.48 us -> 5.11 us  [small_call(): pl.pallas_call(kernel, out_shape=jax.ShapeDtypeStruct(shape, jnp.bfloat16...]
where the time goes in v7:
time: 135 us; the launch traced here: 134 us
  starting transfers between devices  53.5 us (40%)
  waiting for transfers between devices  30.4 us (23%)
  blocking collectives  23.4 us (17%)
  between operations  14.3 us (11%)
  Pallas kernels  8.84 us (7%)
  local copies, waits for them, and re-layouts  2.39 us (2%)
    all_to_all x4, starting transfers between devices, exchange(): return lax.all_to_all(blocks, axes, split_axis=0, concat_axis=0, tiled=True)  40.1 us
    all_to_all x4, waiting for transfers between devices, exchange(): return lax.all_to_all(blocks, axes, split_axis=0, concat_axis=0, tiled=True)  30.4 us
    all_to_all x1, blocking collectives, exchange(): return lax.all_to_all(blocks, axes, split_axis=0, concat_axis=0, tiled=True)  23.4 us
    ppermute x2, starting transfers between devices, across(): lax.ppermute(block, 'y_hi', [(i, i ^ bit) for i in range(lax.axis_size('y...  7.11 us
    ppermute x3, starting transfers between devices, other_core(): return lax.ppermute(block, 'core', [(0, 1), (1, 0)])  6.25 us
    pallas_call x4, Pallas kernels, small_call(): pl.pallas_call(kernel, out_shape=jax.ShapeDtypeStruct(shape, jnp.bfloat16...  5.11 us
    pallas_call x1, Pallas kernels, finish(): pl.pallas_call(finish_kernel, out_shape=(jax.ShapeDtypeStruct((tok_count,...  3.72 us
  transfers between devices with their start and end apart: 10, of which 4 were waited for; matrix products, arithmetic and copies ran while one was open for 1% of the time, Pallas kernels for 2%

profile of v7, /device:TPU:4, one launch (start us, length us, event | category | flops | bytes accessed | tf_op | source)
XLA Modules:
  0.0 134.2 jit_solution(13930860207098922352)
XLA Ops:
  7.2 0.0 copy-start.5
  7.2 0.0 copy-start.4
  7.2 2.5 %shard_map.131 = bf16[32,6,512]{2,1,0:T(8,128)(2,1)} custom-call(bf16[128,4096]{1,0:T(8,128)(2,1)} %tokens_ref.1, s32[1,128]{1,0:T(1,128)} %bitcast.23, s32[1,128]{1,0:T(1,128)} %bitcast.22, s32[1,128]{1,0:T(1,128)} %bitcast.24, s32[1,128]{1,0:T(1,128)} %bitcast.25), custom_call_target="tpu_custom_call" | custom-call | flops 196608 | bytes 393216 | tf_op jit(solution)/shard_map/pallas_call | solution.py:48
  9.7 16.7 %all-to-all-start = ((bf16[32,6,512]{2,1,0:T(8,128)(2,1)}), bf16[32,6,512]{2,1,0:T(8,128)(2,1)S(1)}, u32[]{:S(2)}, u32[]{:S(2)}) async-start(bf16[32,6,512]{2,1,0:T(8,128)(2,1)} %shard_map.131), calls=%async_computation | async-start | bytes 524288 | tf_op jit(solution)/shard_map/all_to_all | solution.py:22
  26.4 1.9 %collective-permute-start = (bf16[512,256]{1,0:T(8,128)(2,1)}, bf16[512,256]{1,0:T(8,128)(2,1)S(1)}, u32[]{:S(2)}, u32[]{:S(2)}) collective-permute-start(bf16[512,256]{1,0:T(8,128)(2,1)} %refs_0_.1), channel_id=1, source_target_pairs={{0,1},{1,0},{2,3},{3,2},{4,5},{5,4},{6,7},{7,6},{8,9},{9,8},{10,11... | collective-permute-start | bytes 786440 | tf_op jit(solution)/shard_map/ppermute | solution.py:26
  28.3 2.4 %collective-permute-start.1 = (bf16[512,256]{1,0:T(8,128)(2,1)}, bf16[512,256]{1,0:T(8,128)(2,1)S(1)}, u32[]{:S(2)}, u32[]{:S(2)}) collective-permute-start(bf16[512,256]{1,0:T(8,128)(2,1)} %refs_2_.1), channel_id=1, source_target_pairs={{0,1},{1,0},{2,3},{3,2},{4,5},{5,4},{6,7},{7,6},{8,9},{9,8},{10,11... | collective-permute-start | bytes 786440 | tf_op jit(solution)/shard_map/ppermute | solution.py:26
  30.8 4.3 %collective-permute-start.2 = (bf16[64,512]{1,0:T(8,128)(2,1)}, bf16[64,512]{1,0:T(8,128)(2,1)S(1)}, u32[]{:S(2)}, u32[]{:S(2)}) collective-permute-start(bf16[64,512]{1,0:T(8,128)(2,1)} %param.23), channel_id=1, source_target_pairs={{0,16},{16,0},{32,48},{48,32},{1,17},{17,1},{33,49},{49,33},{2,18}... | collective-permute-start | bytes 196616 | tf_op jit(solution)/shard_map/ppermute | solution.py:30
  35.1 3.9 %all-to-all-done = bf16[32,6,512]{2,1,0:T(8,128)(2,1)S(1)} async-done(((bf16[32,6,512]{2,1,0:T(8,128)(2,1)}), bf16[32,6,512]{2,1,0:T(8,128)(2,1)S(1)}, u32[]{:S(2)}, u32[]{:S(2)}) %all-to-all-start) | async-done | bytes 196640 | tf_op jit(solution)/shard_map/all_to_all | solution.py:22
  39.0 0.0 copy-start.10
  39.0 0.0 copy-start.11
  39.1 0.0 copy-start.3
  39.1 0.1 reshape.22.rows_ref
  39.1 0.0 copy-start
  39.2 0.0 collective-permute-done.refs_1_
  39.2 0.0 collective-permute-done.1.refs_3_
  39.2 0.0 copy-start.1
  39.2 1.0 copy-done.1
  40.2 0.9 copy-done.2
  41.2 1.1 shard_map.132
  42.3 0.0 collective-permute-done.2
  42.3 14.6 %all-to-all-start.1 = ((bf16[8,24,1024]{2,1,0:T(8,128)(2,1)}), bf16[8,24,1024]{2,1,0:T(8,128)(2,1)S(1)}, u32[]{:S(2)}, u32[]{:S(2)}) async-start(bf16[8,24,1024]{2,1,0:T(8,128)(2,1)} %bitcast.4), calls=%async_computation.1 | async-start | bytes 786432 | tf_op jit(solution)/shard_map/all_to_all | solution.py:22
  56.9 0.0 all-gather.2.cloned.1.call-start
  56.9 0.0 copy-done.5
  57.0 2.8 %collective-permute-start.3 = (bf16[128,512]{1,0:T(8,128)(2,1)S(1)}, bf16[128,512]{1,0:T(8,128)(2,1)S(1)}, u32[]{:S(2)}, u32[]{:S(2)}) collective-permute-start(bf16[128,512]{1,0:T(8,128)(2,1)S(1)} %pad_maximum_fusion.1), channel_id=1, source_target_pairs={{0,32},{16,48},{32,0},{48,16},{1,33},{17,49},{33,1},{49,17},{2,34}... | collective-permute-start | bytes 393224 | tf_op jit(solution)/shard_map/ppermute | solution.py:30
  59.8 10.4 %all-to-all-done.1.parts_ref = bf16[8,24,1024]{2,1,0:T(8,128)(2,1)S(1)} async-done(((bf16[8,24,1024]{2,1,0:T(8,128)(2,1)}), bf16[8,24,1024]{2,1,0:T(8,128)(2,1)S(1)}, u32[]{:S(2)}, u32[]{:S(2)}) %all-to-all-start.1) | async-done | bytes 393248 | tf_op jit(solution)/shard_map/all_to_all | solution.py:22
  70.2 0.8 shard_map.133
  71.0 0.0 collective-permute-done.3
  71.0 0.7 pad_maximum_fusion
  71.7 0.0 all-gather.2.cloned.1.call-update
  71.8 5.3 %all-to-all-start.2 = ((bf16[8,24,512]{2,1,0:T(8,128)(2,1)}), bf16[8,24,512]{2,1,0:T(8,128)(2,1)S(1)}, u32[]{:S(2)}, u32[]{:S(2)}) async-start(bf16[8,24,512]{2,1,0:T(8,128)(2,1)} %shard_map.133), calls=%async_computation.2 | async-start | bytes 393216 | tf_op jit(solution)/shard_map/all_to_all | solution.py:22
  77.1 0.0 copy-done.4
  77.1 1.9 %collective-permute-start.4 = (bf16[256,512]{1,0:T(8,128)(2,1)S(1)}, bf16[256,512]{1,0:T(8,128)(2,1)S(1)}, u32[]{:S(2)}, u32[]{:S(2)}) collective-permute-start(bf16[256,512]{1,0:T(8,128)(2,1)S(1)} %copy-done.4), channel_id=1, source_target_pairs={{0,1},{1,0},{2,3},{3,2},{4,5},{5,4},{6,7},{7,6},{8,9},{9,8},{10,11... | collective-permute-start | bytes 786440 | tf_op jit(solution)/shard_map/ppermute | solution.py:26
  79.0 7.8 %all-to-all-done.2 = bf16[8,24,512]{2,1,0:T(8,128)(2,1)S(1)} async-done(((bf16[8,24,512]{2,1,0:T(8,128)(2,1)}), bf16[8,24,512]{2,1,0:T(8,128)(2,1)S(1)}, u32[]{:S(2)}, u32[]{:S(2)}) %all-to-all-start.2) | async-done | bytes 196640 | tf_op jit(solution)/shard_map/all_to_all | solution.py:22
  86.9 0.2 fusion.2
  87.1 0.0 collective-permute-done.4
  87.1 0.2 fusion
  87.3 0.1 reshape.25
  87.4 23.4 %all_to_all.25.parts_ref = bf16[32,6,512]{2,1,0:T(8,128)(2,1)S(1)} all-to-all(bf16[32,6,512]{2,1,0:T(8,128)(2,1)S(1)} %reshape.25), channel_id=1, replica_groups=mesh['y_lo'=2,'z'=8,'y_hi'=4,'x'=8,'core'=2] {'y_hi','x'}, dimensions={0} | all-to-all | bytes 393216 | tf_op jit(solution)/shard_map/all_to_all | solution.py:22
  110.8 0.7 shard_map.134
  111.5 3.5 %all-to-all-start.4 = ((bf16[16,8,512]{2,1,0:T(8,128)(2,1)}), bf16[16,8,512]{2,1,0:T(8,128)(2,1)S(1)}, u32[]{:S(2)}, u32[]{:S(2)}) async-start(bf16[16,8,512]{2,1,0:T(8,128)(2,1)} %shard_map.134), calls=%async_computation.4 | async-start | bytes 262144 | tf_op jit(solution)/shard_map/all_to_all | solution.py:22
  115.0 0.0 copy-done.6
  115.1 0.0 copy-done.7
  115.1 0.0 copy-done.8
  115.1 0.1 copy.18.column_ref
  115.2 0.0 copy-done.10
  115.2 0.1 copy.19.gate_ref
  115.4 8.2 %all-to-all-done.4 = bf16[16,8,512]{2,1,0:T(8,128)(2,1)S(1)} async-done(((bf16[16,8,512]{2,1,0:T(8,128)(2,1)}), bf16[16,8,512]{2,1,0:T(8,128)(2,1)S(1)}, u32[]{:S(2)}, u32[]{:S(2)}) %all-to-all-start.4) | async-done | bytes 131104 | tf_op jit(solution)/shard_map/all_to_all | solution.py:22
  123.6 3.7 %shard_map.135 = (bf16[128,4096]{1,0:T(8,128)(2,1)}, bf16[128,512]{1,0:T(8,128)(2,1)}) custom-call(bf16[128,4096]{1,0:T(8,128)(2,1)S(1)} %copy-done, bf16[128,512]{1,0:T(8,128)(2,1)S(1)} %bitcast.16, s32[128,1]{1,0:T(8,128)S(1)} %copy.18.column_ref, f32[128,1]{1,0:T(8,128)S(1)} %copy.19.gate_ref, f32[1,4096]{1,0:T(1,128)S(1)} %bitcast.17, ...), custom_call_target="tpu_custom_call" | custom-call | flops 536870912 | bytes 8388608 | tf_op jit(solution)/shard_map/pallas_call | solution.py:165
  (15 shorter events, 0.1 us)
Async XLA Ops:
  7.2 49.8 %copy-start.5 = (bf16[64,512]{1,0:T(8,128)(2,1)S(1)}, bf16[64,512]{1,0:T(8,128)(2,1)}, u32[]{:S(2)}) copy-start(bf16[64,512]{1,0:T(8,128)(2,1)} %param.23) | copy-start | bytes 196612
  7.2 69.9 %copy-start.4 = (bf16[256,512]{1,0:T(8,128)(2,1)S(1)}, bf16[256,512]{1,0:T(8,128)(2,1)}, u32[]{:S(2)}) copy-start(bf16[256,512]{1,0:T(8,128)(2,1)} %param.21) | copy-start | bytes 786436
  9.7 29.3 %all-to-all-start = ((bf16[32,6,512]{2,1,0:T(8,128)(2,1)}), bf16[32,6,512]{2,1,0:T(8,128)(2,1)S(1)}, u32[]{:S(2)}, u32[]{:S(2)}) async-start(bf16[32,6,512]{2,1,0:T(8,128)(2,1)} %shard_map.131), calls=%async_computation | async-start | bytes 524288 | tf_op jit(solution)/shard_map/all_to_all | solution.py:22
  26.4 12.7 %collective-permute-start = (bf16[512,256]{1,0:T(8,128)(2,1)}, bf16[512,256]{1,0:T(8,128)(2,1)S(1)}, u32[]{:S(2)}, u32[]{:S(2)}) collective-permute-start(bf16[512,256]{1,0:T(8,128)(2,1)} %refs_0_.1), channel_id=1, source_target_pairs={{0,1},{1,0},{2,3},{3,2},{4,5},{5,4},{6,7},{7,6},{8,9},{9,8},{10,11... | collective-permute-start | bytes 786440 | tf_op jit(solution)/shard_map/ppermute | solution.py:26
  28.3 10.8 %collective-permute-start.1 = (bf16[512,256]{1,0:T(8,128)(2,1)}, bf16[512,256]{1,0:T(8,128)(2,1)S(1)}, u32[]{:S(2)}, u32[]{:S(2)}) collective-permute-start(bf16[512,256]{1,0:T(8,128)(2,1)} %refs_2_.1), channel_id=1, source_target_pairs={{0,1},{1,0},{2,3},{3,2},{4,5},{5,4},{6,7},{7,6},{8,9},{9,8},{10,11... | collective-permute-start | bytes 786440 | tf_op jit(solution)/shard_map/ppermute | solution.py:26
  30.8 11.5 %collective-permute-start.2 = (bf16[64,512]{1,0:T(8,128)(2,1)}, bf16[64,512]{1,0:T(8,128)(2,1)S(1)}, u32[]{:S(2)}, u32[]{:S(2)}) collective-permute-start(bf16[64,512]{1,0:T(8,128)(2,1)} %param.23), channel_id=1, source_target_pairs={{0,16},{16,0},{32,48},{48,32},{1,17},{17,1},{33,49},{49,33},{2,18}... | collective-permute-start | bytes 196616 | tf_op jit(solution)/shard_map/ppermute | solution.py:30
  39.0 76.0 %copy-start.6 = (s32[128]{0:T(128)S(1)}, s32[128]{0:T(128)}, u32[]{:S(2)}) copy-start(s32[128]{0:T(128)} %param.14) | copy-start | bytes 1540
  39.0 76.0 %copy-start.7 = (s32[128]{0:T(128)S(1)}, s32[128]{0:T(128)}, u32[]{:S(2)}) copy-start(s32[128]{0:T(128)} %param.13) | copy-start | bytes 1540
  39.0 76.0 %copy-start.8 = (s32[128]{0:T(128)S(1)}, s32[128]{0:T(128)}, u32[]{:S(2)}) copy-start(s32[128]{0:T(128)} %param.15) | copy-start | bytes 1540
  39.0 76.1 %copy-start.9 = (s32[128]{0:T(128)S(1)}, s32[128]{0:T(128)}, u32[]{:S(2)}) copy-start(s32[128]{0:T(128)} %param.16) | copy-start | bytes 1540
  39.0 76.2 %copy-start.10 = (f32[128]{0:T(128)S(1)}, f32[128]{0:T(128)}, u32[]{:S(2)}) copy-start(f32[128]{0:T(128)} %param.17) | copy-start | bytes 1540
  39.0 76.2 %copy-start.11 = (f32[128]{0:T(128)S(1)}, f32[128]{0:T(128)}, u32[]{:S(2)}) copy-start(f32[128]{0:T(128)} %param.18) | copy-start | bytes 1540
  39.1 84.5 %copy-start.3 = (f32[4096]{0:T(1024)S(1)}, f32[4096]{0:T(1024)}, u32[]{:S(2)}) copy-start(f32[4096]{0:T(1024)} %param.22) | copy-start | bytes 49156
  39.1 84.4 %copy-start = (bf16[128,4096]{1,0:T(8,128)(2,1)S(1)}, bf16[128,4096]{1,0:T(8,128)(2,1)}, u32[]{:S(2)}) copy-start(bf16[128,4096]{1,0:T(8,128)(2,1)} %tokens_ref.1) | copy-start | bytes 3145732
  39.2 1.0 copy-start.1
  40.2 0.9 copy-start.2
  42.3 27.9 %all-to-all-start.1 = ((bf16[8,24,1024]{2,1,0:T(8,128)(2,1)}), bf16[8,24,1024]{2,1,0:T(8,128)(2,1)S(1)}, u32[]{:S(2)}, u32[]{:S(2)}) async-start(bf16[8,24,1024]{2,1,0:T(8,128)(2,1)} %bitcast.4), calls=%async_computation.1 | async-start | bytes 786432 | tf_op jit(solution)/shard_map/all_to_all | solution.py:22
  56.9 66.7 %all-gather.2.cloned.1.call-start = ((), (), s32[]{:S(2)}) async-start(), calls=%async_computation.5 | async-start | bytes 4456448 | tf_op jit(solution)/shard_map/all_gather | solution.py:240
  57.0 14.0 %collective-permute-start.3 = (bf16[128,512]{1,0:T(8,128)(2,1)S(1)}, bf16[128,512]{1,0:T(8,128)(2,1)S(1)}, u32[]{:S(2)}, u32[]{:S(2)}) collective-permute-start(bf16[128,512]{1,0:T(8,128)(2,1)S(1)} %pad_maximum_fusion.1), channel_id=1, source_target_pairs={{0,32},{16,48},{32,0},{48,16},{1,33},{17,49},{33,1},{49,17},{2,34}... | collective-permute-start | bytes 393224 | tf_op jit(solution)/shard_map/ppermute | solution.py:30
  71.8 15.1 %all-to-all-start.2 = ((bf16[8,24,512]{2,1,0:T(8,128)(2,1)}), bf16[8,24,512]{2,1,0:T(8,128)(2,1)S(1)}, u32[]{:S(2)}, u32[]{:S(2)}) async-start(bf16[8,24,512]{2,1,0:T(8,128)(2,1)} %shard_map.133), calls=%async_computation.2 | async-start | bytes 393216 | tf_op jit(solution)/shard_map/all_to_all | solution.py:22
  77.1 10.0 %collective-permute-start.4 = (bf16[256,512]{1,0:T(8,128)(2,1)S(1)}, bf16[256,512]{1,0:T(8,128)(2,1)S(1)}, u32[]{:S(2)}, u32[]{:S(2)}) collective-permute-start(bf16[256,512]{1,0:T(8,128)(2,1)S(1)} %copy-done.4), channel_id=1, source_target_pairs={{0,1},{1,0},{2,3},{3,2},{4,5},{5,4},{6,7},{7,6},{8,9},{9,8},{10,11... | collective-permute-start | bytes 786440 | tf_op jit(solution)/shard_map/ppermute | solution.py:26
  111.5 12.0 %all-to-all-start.4 = ((bf16[16,8,512]{2,1,0:T(8,128)(2,1)}), bf16[16,8,512]{2,1,0:T(8,128)(2,1)S(1)}, u32[]{:S(2)}, u32[]{:S(2)}) async-start(bf16[16,8,512]{2,1,0:T(8,128)(2,1)} %shard_map.134), calls=%async_computation.4 | async-start | bytes 262144 | tf_op jit(solution)/shard_map/all_to_all | solution.py:22
Sparse Core Ops, SparseCore 0:
  71.9 45.3 all-gather.1

commit v8 on v7

--- a/solution.py
+++ b/solution.py
@@ -75,14 +75,19 @@
         out_ref[i] = rows[:SLOTS]
 
 
-def products_kernel(rows_ref, *refs):
-    out_ref = refs[-1]
+def products_kernel(rows_ref, own_ref, gate_other_ref, up_other_ref, out_ref):
     rows = rows_ref[...]
-    units = refs[0].shape[1]
-    for i, w_ref in enumerate(refs[:-1]):
-        out_ref[:, i * units : (i + 1) * units] = jnp.dot(
-            rows, w_ref[...], preferred_element_type=jnp.float32
+    units = gate_other_ref.shape[1]
+
+    def product(at, w):
+        out_ref[:, at * units : (at + 1) * units] = jnp.dot(
+            rows, w, preferred_element_type=jnp.float32
         ).astype(jnp.bfloat16)
+
+    product(0, own_ref[:, :units])
+    product(1, gate_other_ref[...])
+    product(2, own_ref[:, units:])
+    product(3, up_other_ref[...])
 
 
 def hidden_kernel(parts_ref, out_ref):
@@ -220,22 +225,21 @@
         second_slot[None, :],
         scratch=(pltpu.VMEM((tok_count, block_width), jnp.bfloat16), pltpu.SemaphoreType.DMA(())),
     )
-    slot_copies, w_query = tie(slot_copies, w_query)
+    query_rows = in_order(w_query, across(w_query, 1), 1)
+    slot_copies, query_rows = tie(slot_copies, query_rows)
     rows = exchange(slot_copies, CHIPS).reshape(chips * SLOTS, block_width)
     w_gate_other = other_core(w_gate)
     w_up_other = other_core(w_up)
-    w_query_beside = across(w_query, 1)
-
+    query_rows_other = across(query_rows, 2)
+
+    w_own = jnp.concatenate([w_gate, w_up], axis=1)
     partial = small_call(
-        products_kernel, (chips * SLOTS, 4 * units), 5, rows, w_gate, w_gate_other, w_up, w_up_other
+        products_kernel, (chips * SLOTS, 4 * units), 4, rows, w_own, w_gate_other, w_up_other
     )
     share = chips * SLOTS // blocks
-    partial, w_query, w_query_beside = tie(partial, w_query, w_query_beside)
+    partial, query_rows, query_rows_other = tie(partial, query_rows, query_rows_other)
     summed = exchange(partial.reshape(blocks, share, 4 * units), "z")
-    query_rows = in_order(w_query, w_query_beside, 1)
-    query_rows_other = across(query_rows, 2)
     hidden_copies = small_call(hidden_kernel, (blocks, share, 2 * units), 1, summed)
-    hidden_copies, query_rows_other = tie(hidden_copies, query_rows_other)
     query_rows = in_order(query_rows, query_rows_other, 2).reshape((-1,) + w_query.shape)
     w_query_full = lax.all_gather(query_rows, ("x", "core"), axis=0)
     w_query_full = w_query_full.reshape((-1, 2) + query_rows.shape)

time: 135 us -> 141 us (1.044)
  the two profiles are of different devices: /device:TPU:4 before, /device:TPU:2 now
where the time goes in v8:
time: 141 us
  blocking collectives  54.2 us (38%)
  starting transfers between devices  40.6 us (29%)
  waiting for transfers between devices  19.8 us (14%)
  between operations  14.3 us (10%)
  Pallas kernels  8.09 us (6%)
  other arithmetic  2.69 us (2%)
    all_to_all x2, blocking collectives, exchange(): return lax.all_to_all(blocks, axes, split_axis=0, concat_axis=0, tiled=True)  54.2 us
    all_to_all x3, starting transfers between devices, exchange(): return lax.all_to_all(blocks, axes, split_axis=0, concat_axis=0, tiled=True)  22.2 us
    all_to_all x3, waiting for transfers between devices, exchange(): return lax.all_to_all(blocks, axes, split_axis=0, concat_axis=0, tiled=True)  16.6 us
    ppermute x2, starting transfers between devices, across(): lax.ppermute(block, 'y_hi', [(i, i ^ bit) for i in range(lax.axis_size('y...  12.1 us
    ppermute x3, starting transfers between devices, other_core(): return lax.ppermute(block, 'core', [(0, 1), (1, 0)])  6.25 us
    pallas_call x4, Pallas kernels, small_call(): pl.pallas_call(kernel, out_shape=jax.ShapeDtypeStruct(shape, jnp.bfloat16...  4.37 us
    pallas_call x1, Pallas kernels, finish(): pl.pallas_call(finish_kernel, out_shape=(jax.ShapeDtypeStruct((tok_count,...  3.72 us
    ppermute x2, waiting for transfers between devices, across(): lax.ppermute(block, 'y_hi', [(i, i ^ bit) for i in range(lax.axis_size('y...  3.21 us
  transfers between devices with their start and end apart: 9, of which 5 were waited for; matrix products, arithmetic and copies ran while one was open for 1% of the time, Pallas kernels for 3%

profile of v8, /device:TPU:2, one launch (start us, length us, event | category | flops | bytes accessed | tf_op | source)
XLA Modules:
  0.0 140.6 jit_solution(18363180331070141889)
XLA Ops:
  7.2 4.7 %collective-permute-start = (bf16[64,512]{1,0:T(8,128)(2,1)}, bf16[64,512]{1,0:T(8,128)(2,1)S(1)}, u32[]{:S(2)}, u32[]{:S(2)}) collective-permute-start(bf16[64,512]{1,0:T(8,128)(2,1)} %param.23), channel_id=1, source_target_pairs={{0,16},{16,0},{32,48},{48,32},{1,17},{17,1},{33,49},{49,33},{2,18}... | collective-permute-start | bytes 196616 | tf_op jit(solution)/shard_map/ppermute | solution.py:30
  11.9 0.0 copy-start.2
  11.9 2.5 %shard_map.131 = bf16[32,6,512]{2,1,0:T(8,128)(2,1)} custom-call(bf16[128,4096]{1,0:T(8,128)(2,1)} %tokens_ref.1, s32[1,128]{1,0:T(1,128)} %bitcast.24, s32[1,128]{1,0:T(1,128)} %bitcast.23, s32[1,128]{1,0:T(1,128)} %bitcast.25, s32[1,128]{1,0:T(1,128)} %bitcast.26), custom_call_target="tpu_custom_call" | custom-call | flops 196608 | bytes 393216 | tf_op jit(solution)/shard_map/pallas_call | solution.py:48
  14.4 1.4 collective-permute-done
  15.8 0.9 broadcast_select_fusion.3
  16.7 15.3 %all-to-all-start = ((bf16[32,6,512]{2,1,0:T(8,128)(2,1)}), bf16[32,6,512]{2,1,0:T(8,128)(2,1)S(1)}, u32[]{:S(2)}, u32[]{:S(2)}) async-start(bf16[32,6,512]{2,1,0:T(8,128)(2,1)} %shard_map.131), calls=%async_computation | async-start | bytes 524288 | tf_op jit(solution)/shard_map/all_to_all | solution.py:22
  32.0 0.0 all-gather.2.cloned.1.call-start
  32.1 1.9 %collective-permute-start.1 = (bf16[512,256]{1,0:T(8,128)(2,1)}, bf16[512,256]{1,0:T(8,128)(2,1)S(1)}, u32[]{:S(2)}, u32[]{:S(2)}) collective-permute-start(bf16[512,256]{1,0:T(8,128)(2,1)} %param.19), channel_id=1, source_target_pairs={{0,1},{1,0},{2,3},{3,2},{4,5},{5,4},{6,7},{7,6},{8,9},{9,8},{10,11... | collective-permute-start | bytes 786440 | tf_op jit(solution)/shard_map/ppermute | solution.py:26
  34.0 2.4 %collective-permute-start.2 = (bf16[512,256]{1,0:T(8,128)(2,1)}, bf16[512,256]{1,0:T(8,128)(2,1)S(1)}, u32[]{:S(2)}, u32[]{:S(2)}) collective-permute-start(bf16[512,256]{1,0:T(8,128)(2,1)} %param.20), channel_id=1, source_target_pairs={{0,1},{1,0},{2,3},{3,2},{4,5},{5,4},{6,7},{7,6},{8,9},{9,8},{10,11... | collective-permute-start | bytes 786440 | tf_op jit(solution)/shard_map/ppermute | solution.py:26
  36.4 7.4 %collective-permute-start.3 = (bf16[128,512]{1,0:T(8,128)(2,1)S(1)}, bf16[128,512]{1,0:T(8,128)(2,1)S(1)}, u32[]{:S(2)}, u32[]{:S(2)}) collective-permute-start(bf16[128,512]{1,0:T(8,128)(2,1)S(1)} %pad_maximum_fusion.2), channel_id=1, source_target_pairs={{0,32},{16,48},{32,0},{48,16},{1,33},{17,49},{33,1},{49,17},{2,34}... | collective-permute-start | bytes 393224 | tf_op jit(solution)/shard_map/ppermute | solution.py:30
  43.8 1.1 pad_maximum_fusion.own_ref
  44.9 0.0 copy-start.3
  44.9 0.0 copy-start.4
  44.9 0.0 copy-start.5
  44.9 0.0 copy-start.6
  45.0 0.0 copy-start.7
  45.0 0.0 copy-start.8
  45.0 0.6 all-to-all-done
  45.6 0.1 reshape.22.rows_ref
  45.7 0.0 copy-start
  45.7 0.0 copy-start.1
  45.7 0.0 collective-permute-done.1.gate_other_ref
  45.7 0.0 collective-permute-done.2.up_other_ref
  45.7 0.4 shard_map.132
  46.1 1.8 %collective-permute-done.3 = bf16[128,512]{1,0:T(8,128)(2,1)S(1)} collective-permute-done((bf16[128,512]{1,0:T(8,128)(2,1)S(1)}, bf16[128,512]{1,0:T(8,128)(2,1)S(1)}, u32[]{:S(2)}, u32[]{:S(2)}) %collective-permute-start.3) | collective-permute-done | bytes 131104 | tf_op jit(solution)/shard_map/ppermute | solution.py:30
  47.9 0.7 pad_maximum_fusion.1
  48.7 0.0 all-gather.2.cloned.1.call-update
  48.7 28.5 %all_to_all.25.parts_ref = bf16[8,24,1024]{2,1,0:T(8,128)(2,1)S(1)} all-to-all(bf16[8,24,1024]{2,1,0:T(8,128)(2,1)S(1)} %bitcast.16), channel_id=1, replica_groups=mesh['y_lo'=2,'z'=8,'y_hi'=4,'x'=8,'core'=2] {'z'}, dimensions={0} | all-to-all | bytes 786432 | tf_op jit(solution)/shard_map/all_to_all | solution.py:22
  77.2 0.8 shard_map.133
  78.0 3.4 %all-to-all-start.2 = ((bf16[8,24,512]{2,1,0:T(8,128)(2,1)}), bf16[8,24,512]{2,1,0:T(8,128)(2,1)S(1)}, u32[]{:S(2)}, u32[]{:S(2)}) async-start(bf16[8,24,512]{2,1,0:T(8,128)(2,1)} %shard_map.133), calls=%async_computation.2 | async-start | bytes 393216 | tf_op jit(solution)/shard_map/all_to_all | solution.py:22
  81.4 1.9 %collective-permute-start.4 = (bf16[256,512]{1,0:T(8,128)(2,1)S(1)}, bf16[256,512]{1,0:T(8,128)(2,1)S(1)}, u32[]{:S(2)}, u32[]{:S(2)}) collective-permute-start(bf16[256,512]{1,0:T(8,128)(2,1)S(1)} %copy-done.2), channel_id=1, source_target_pairs={{0,1},{1,0},{2,3},{3,2},{4,5},{5,4},{6,7},{7,6},{8,9},{9,8},{10,11... | collective-permute-start | bytes 786440 | tf_op jit(solution)/shard_map/ppermute | solution.py:26
  83.3 7.7 %all-to-all-done.2 = bf16[8,24,512]{2,1,0:T(8,128)(2,1)S(1)} async-done(((bf16[8,24,512]{2,1,0:T(8,128)(2,1)}), bf16[8,24,512]{2,1,0:T(8,128)(2,1)S(1)}, u32[]{:S(2)}, u32[]{:S(2)}) %all-to-all-start.2) | async-done | bytes 196640 | tf_op jit(solution)/shard_map/all_to_all | solution.py:22
  91.1 0.2 fusion.2
  91.3 0.0 collective-permute-done.4
  91.3 0.2 fusion
  91.5 0.1 reshape.25
  91.6 25.7 %all_to_all.26.parts_ref = bf16[32,6,512]{2,1,0:T(8,128)(2,1)S(1)} all-to-all(bf16[32,6,512]{2,1,0:T(8,128)(2,1)S(1)} %reshape.25), channel_id=1, replica_groups=mesh['y_lo'=2,'z'=8,'y_hi'=4,'x'=8,'core'=2] {'y_hi','x'}, dimensions={0} | all-to-all | bytes 393216 | tf_op jit(solution)/shard_map/all_to_all | solution.py:22
  117.3 0.7 shard_map.134
  118.0 3.5 %all-to-all-start.4 = ((bf16[16,8,512]{2,1,0:T(8,128)(2,1)}), bf16[16,8,512]{2,1,0:T(8,128)(2,1)S(1)}, u32[]{:S(2)}, u32[]{:S(2)}) async-start(bf16[16,8,512]{2,1,0:T(8,128)(2,1)} %shard_map.134), calls=%async_computation.4 | async-start | bytes 262144 | tf_op jit(solution)/shard_map/all_to_all | solution.py:22
  121.5 0.0 copy-done.3
  121.5 0.0 copy-done.4
  121.5 0.0 copy-done.5
  121.5 0.0 copy-done.6
  121.6 0.1 copy.18.column_ref
  121.7 0.1 copy.19.gate_ref
  121.8 8.2 %all-to-all-done.4 = bf16[16,8,512]{2,1,0:T(8,128)(2,1)S(1)} async-done(((bf16[16,8,512]{2,1,0:T(8,128)(2,1)}), bf16[16,8,512]{2,1,0:T(8,128)(2,1)S(1)}, u32[]{:S(2)}, u32[]{:S(2)}) %all-to-all-start.4) | async-done | bytes 131104 | tf_op jit(solution)/shard_map/all_to_all | solution.py:22
  130.0 0.0 copy-done
  130.0 3.7 %shard_map.135 = (bf16[128,4096]{1,0:T(8,128)(2,1)}, bf16[128,512]{1,0:T(8,128)(2,1)}) custom-call(bf16[128,4096]{1,0:T(8,128)(2,1)S(1)} %copy-done, bf16[128,512]{1,0:T(8,128)(2,1)S(1)} %bitcast.17, s32[128,1]{1,0:T(8,128)S(1)} %copy.18.column_ref, f32[128,1]{1,0:T(8,128)S(1)} %copy.19.gate_ref, f32[1,4096]{1,0:T(1,128)S(1)} %bitcast.18, ...), custom_call_target="tpu_custom_call" | custom-call | flops 536870912 | bytes 8388608 | tf_op jit(solution)/shard_map/pallas_call | solution.py:170
  (9 shorter events, 0.1 us)
Async XLA Ops:
  7.2 8.7 %collective-permute-start = (bf16[64,512]{1,0:T(8,128)(2,1)}, bf16[64,512]{1,0:T(8,128)(2,1)S(1)}, u32[]{:S(2)}, u32[]{:S(2)}) collective-permute-start(bf16[64,512]{1,0:T(8,128)(2,1)} %param.23), channel_id=1, source_target_pairs={{0,16},{16,0},{32,48},{48,32},{1,17},{17,1},{33,49},{49,33},{2,18}... | collective-permute-start | bytes 196616 | tf_op jit(solution)/shard_map/ppermute | solution.py:30
  11.9 69.5 %copy-start.2 = (bf16[256,512]{1,0:T(8,128)(2,1)S(1)}, bf16[256,512]{1,0:T(8,128)(2,1)}, u32[]{:S(2)}) copy-start(bf16[256,512]{1,0:T(8,128)(2,1)} %param.21) | copy-start | bytes 786436
  16.7 28.9 %all-to-all-start = ((bf16[32,6,512]{2,1,0:T(8,128)(2,1)}), bf16[32,6,512]{2,1,0:T(8,128)(2,1)S(1)}, u32[]{:S(2)}, u32[]{:S(2)}) async-start(bf16[32,6,512]{2,1,0:T(8,128)(2,1)} %shard_map.131), calls=%async_computation | async-start | bytes 524288 | tf_op jit(solution)/shard_map/all_to_all | solution.py:22
  32.0 98.0 %all-gather.2.cloned.1.call-start = ((), (), s32[]{:S(2)}) async-start(), calls=%async_computation.5 | async-start | bytes 4456448 | tf_op jit(solution)/shard_map/all_gather | solution.py:244
  32.1 13.6 %collective-permute-start.1 = (bf16[512,256]{1,0:T(8,128)(2,1)}, bf16[512,256]{1,0:T(8,128)(2,1)S(1)}, u32[]{:S(2)}, u32[]{:S(2)}) collective-permute-start(bf16[512,256]{1,0:T(8,128)(2,1)} %param.19), channel_id=1, source_target_pairs={{0,1},{1,0},{2,3},{3,2},{4,5},{5,4},{6,7},{7,6},{8,9},{9,8},{10,11... | collective-permute-start | bytes 786440 | tf_op jit(solution)/shard_map/ppermute | solution.py:26
  34.0 11.7 %collective-permute-start.2 = (bf16[512,256]{1,0:T(8,128)(2,1)}, bf16[512,256]{1,0:T(8,128)(2,1)S(1)}, u32[]{:S(2)}, u32[]{:S(2)}) collective-permute-start(bf16[512,256]{1,0:T(8,128)(2,1)} %param.20), channel_id=1, source_target_pairs={{0,1},{1,0},{2,3},{3,2},{4,5},{5,4},{6,7},{7,6},{8,9},{9,8},{10,11... | collective-permute-start | bytes 786440 | tf_op jit(solution)/shard_map/ppermute | solution.py:26
  36.4 11.5 %collective-permute-start.3 = (bf16[128,512]{1,0:T(8,128)(2,1)S(1)}, bf16[128,512]{1,0:T(8,128)(2,1)S(1)}, u32[]{:S(2)}, u32[]{:S(2)}) collective-permute-start(bf16[128,512]{1,0:T(8,128)(2,1)S(1)} %pad_maximum_fusion.2), channel_id=1, source_target_pairs={{0,32},{16,48},{32,0},{48,16},{1,33},{17,49},{33,1},{49,17},{2,34}... | collective-permute-start | bytes 393224 | tf_op jit(solution)/shard_map/ppermute | solution.py:30
  44.9 76.6 %copy-start.3 = (s32[128]{0:T(128)S(1)}, s32[128]{0:T(128)}, u32[]{:S(2)}) copy-start(s32[128]{0:T(128)} %param.14) | copy-start | bytes 1540
  44.9 76.6 %copy-start.4 = (s32[128]{0:T(128)S(1)}, s32[128]{0:T(128)}, u32[]{:S(2)}) copy-start(s32[128]{0:T(128)} %param.13) | copy-start | bytes 1540
  44.9 76.6 %copy-start.5 = (s32[128]{0:T(128)S(1)}, s32[128]{0:T(128)}, u32[]{:S(2)}) copy-start(s32[128]{0:T(128)} %param.15) | copy-start | bytes 1540
  44.9 76.6 %copy-start.6 = (s32[128]{0:T(128)S(1)}, s32[128]{0:T(128)}, u32[]{:S(2)}) copy-start(s32[128]{0:T(128)} %param.16) | copy-start | bytes 1540
  45.0 76.7 %copy-start.7 = (f32[128]{0:T(128)S(1)}, f32[128]{0:T(128)}, u32[]{:S(2)}) copy-start(f32[128]{0:T(128)} %param.17) | copy-start | bytes 1540
  45.0 76.7 %copy-start.8 = (f32[128]{0:T(128)S(1)}, f32[128]{0:T(128)}, u32[]{:S(2)}) copy-start(f32[128]{0:T(128)} %param.18) | copy-start | bytes 1540
  45.7 84.4 %copy-start = (bf16[128,4096]{1,0:T(8,128)(2,1)S(1)}, bf16[128,4096]{1,0:T(8,128)(2,1)}, u32[]{:S(2)}) copy-start(bf16[128,4096]{1,0:T(8,128)(2,1)} %tokens_ref.1) | copy-start | bytes 3145732
  45.7 84.4 %copy-start.1 = (f32[4096]{0:T(1024)S(1)}, f32[4096]{0:T(1024)}, u32[]{:S(2)}) copy-start(f32[4096]{0:T(1024)} %param.22) | copy-start | bytes 49156
  78.0 13.1 %all-to-all-start.2 = ((bf16[8,24,512]{2,1,0:T(8,128)(2,1)}), bf16[8,24,512]{2,1,0:T(8,128)(2,1)S(1)}, u32[]{:S(2)}, u32[]{:S(2)}) async-start(bf16[8,24,512]{2,1,0:T(8,128)(2,1)} %shard_map.133), calls=%async_computation.2 | async-start | bytes 393216 | tf_op jit(solution)/shard_map/all_to_all | solution.py:22
  81.4 9.9 %collective-permute-start.4 = (bf16[256,512]{1,0:T(8,128)(2,1)S(1)}, bf16[256,512]{1,0:T(8,128)(2,1)S(1)}, u32[]{:S(2)}, u32[]{:S(2)}) collective-permute-start(bf16[256,512]{1,0:T(8,128)(2,1)S(1)} %copy-done.2), channel_id=1, source_target_pairs={{0,1},{1,0},{2,3},{3,2},{4,5},{5,4},{6,7},{7,6},{8,9},{9,8},{10,11... | collective-permute-start | bytes 786440 | tf_op jit(solution)/shard_map/ppermute | solution.py:26
  118.0 12.0 %all-to-all-start.4 = ((bf16[16,8,512]{2,1,0:T(8,128)(2,1)}), bf16[16,8,512]{2,1,0:T(8,128)(2,1)S(1)}, u32[]{:S(2)}, u32[]{:S(2)}) async-start(bf16[16,8,512]{2,1,0:T(8,128)(2,1)} %shard_map.134), calls=%async_computation.4 | async-start | bytes 262144 | tf_op jit(solution)/shard_map/all_to_all | solution.py:22
Sparse Core Ops, SparseCore 0:
  48.8 56.8 all-gather.1

commit v9 on v8

--- a/solution.py
+++ b/solution.py
@@ -148,12 +148,12 @@
         cols = pl.ds(z * block_width, block_width)
         values = mixed_ref[:, cols].astype(jnp.float32)
         normed_ref[:, cols] = (values * scale * gain_ref[:, cols]).astype(jnp.bfloat16)
-    for load in loads:
-        load.wait()
     cores, ys, rows = w_ref.shape[1:4]
     pair = 2 * cores * rows
     query = jnp.zeros(query_ref.shape, jnp.float32)
     for x in range(0, parts, 2):
+        loads[x].wait()
+        loads[x + 1].wait()
         for y in range(ys):
             block = jnp.concatenate([w_ref[x + i, c, y] for i in range(2) for c in range(cores)], axis=0)
             start = (y * parts + x) * cores * rows
@@ -225,21 +225,23 @@
         second_slot[None, :],
         scratch=(pltpu.VMEM((tok_count, block_width), jnp.bfloat16), pltpu.SemaphoreType.DMA(())),
     )
-    query_rows = in_order(w_query, across(w_query, 1), 1)
-    slot_copies, query_rows = tie(slot_copies, query_rows)
+    slot_copies, w_query = tie(slot_copies, w_query)
     rows = exchange(slot_copies, CHIPS).reshape(chips * SLOTS, block_width)
     w_gate_other = other_core(w_gate)
     w_up_other = other_core(w_up)
-    query_rows_other = across(query_rows, 2)
+    w_query_beside = across(w_query, 1)
 
     w_own = jnp.concatenate([w_gate, w_up], axis=1)
     partial = small_call(
         products_kernel, (chips * SLOTS, 4 * units), 4, rows, w_own, w_gate_other, w_up_other
     )
     share = chips * SLOTS // blocks
-    partial, query_rows, query_rows_other = tie(partial, query_rows, query_rows_other)
+    partial, w_query, w_query_beside = tie(partial, w_query, w_query_beside)
     summed = exchange(partial.reshape(blocks, share, 4 * units), "z")
+    query_rows = in_order(w_query, w_query_beside, 1)
+    query_rows_other = across(query_rows, 2)
     hidden_copies = small_call(hidden_kernel, (blocks, share, 2 * units), 1, summed)
+    hidden_copies, query_rows_other = tie(hidden_copies, query_rows_other)
     query_rows = in_order(query_rows, query_rows_other, 2).reshape((-1,) + w_query.shape)
     w_query_full = lax.all_gather(query_rows, ("x", "core"), axis=0)
     w_query_full = w_query_full.reshape((-1, 2) + query_rows.shape)

time: 141 us -> 134 us (0.950)
  the two profiles are of different devices: /device:TPU:2 before, /device:TPU:4 now
where the time goes in v9:
time: 134 us
  starting transfers between devices  55.4 us (41%)
  waiting for transfers between devices  27.4 us (20%)
  blocking collectives  25.2 us (19%)
  between operations  14.3 us (11%)
  Pallas kernels  8.49 us (6%)
  other arithmetic  1.87 us (1%)
    all_to_all x4, starting transfers between devices, exchange(): return lax.all_to_all(blocks, axes, split_axis=0, concat_axis=0, tiled=True)  40.1 us
    all_to_all x4, waiting for transfers between devices, exchange(): return lax.all_to_all(blocks, axes, split_axis=0, concat_axis=0, tiled=True)  27.4 us
    all_to_all x1, blocking collectives, exchange(): return lax.all_to_all(blocks, axes, split_axis=0, concat_axis=0, tiled=True)  25.2 us
    ppermute x2, starting transfers between devices, across(): lax.ppermute(block, 'y_hi', [(i, i ^ bit) for i in range(lax.axis_size('y...  9.01 us
    ppermute x3, starting transfers between devices, other_core(): return lax.ppermute(block, 'core', [(0, 1), (1, 0)])  6.25 us
    pallas_call x4, Pallas kernels, small_call(): pl.pallas_call(kernel, out_shape=jax.ShapeDtypeStruct(shape, jnp.bfloat16...  5.12 us
    pallas_call x1, Pallas kernels, finish(): pl.pallas_call(finish_kernel, out_shape=(jax.ShapeDtypeStruct((tok_count,...  3.37 us
  transfers between devices with their start and end apart: 10, of which 4 were waited for; matrix products, arithmetic and copies ran while one was open for 1% of the time, Pallas kernels for 2%

profile of v9, /device:TPU:4, one launch (start us, length us, event | category | flops | bytes accessed | tf_op | source)
XLA Modules:
  0.0 133.7 jit_solution(16205317786645327884)
XLA Ops:
  7.2 0.0 copy-start.3
  7.2 0.0 copy-start.2
  7.2 2.5 %shard_map.131 = bf16[32,6,512]{2,1,0:T(8,128)(2,1)} custom-call(bf16[128,4096]{1,0:T(8,128)(2,1)} %tokens_ref.1, s32[1,128]{1,0:T(1,128)} %bitcast.23, s32[1,128]{1,0:T(1,128)} %bitcast.22, s32[1,128]{1,0:T(1,128)} %bitcast.24, s32[1,128]{1,0:T(1,128)} %bitcast.25), custom_call_target="tpu_custom_call" | custom-call | flops 196608 | bytes 393216 | tf_op jit(solution)/shard_map/pallas_call | solution.py:48
  9.7 16.7 %all-to-all-start = ((bf16[32,6,512]{2,1,0:T(8,128)(2,1)}), bf16[32,6,512]{2,1,0:T(8,128)(2,1)S(1)}, u32[]{:S(2)}, u32[]{:S(2)}) async-start(bf16[32,6,512]{2,1,0:T(8,128)(2,1)} %shard_map.131), calls=%async_computation | async-start | bytes 524288 | tf_op jit(solution)/shard_map/all_to_all | solution.py:22
  26.4 1.9 %collective-permute-start = (bf16[512,256]{1,0:T(8,128)(2,1)}, bf16[512,256]{1,0:T(8,128)(2,1)S(1)}, u32[]{:S(2)}, u32[]{:S(2)}) collective-permute-start(bf16[512,256]{1,0:T(8,128)(2,1)} %param.19), channel_id=1, source_target_pairs={{0,1},{1,0},{2,3},{3,2},{4,5},{5,4},{6,7},{7,6},{8,9},{9,8},{10,11... | collective-permute-start | bytes 786440 | tf_op jit(solution)/shard_map/ppermute | solution.py:26
  28.3 2.4 %collective-permute-start.1 = (bf16[512,256]{1,0:T(8,128)(2,1)}, bf16[512,256]{1,0:T(8,128)(2,1)S(1)}, u32[]{:S(2)}, u32[]{:S(2)}) collective-permute-start(bf16[512,256]{1,0:T(8,128)(2,1)} %param.20), channel_id=1, source_target_pairs={{0,1},{1,0},{2,3},{3,2},{4,5},{5,4},{6,7},{7,6},{8,9},{9,8},{10,11... | collective-permute-start | bytes 786440 | tf_op jit(solution)/shard_map/ppermute | solution.py:26
  30.8 4.3 %collective-permute-start.2 = (bf16[64,512]{1,0:T(8,128)(2,1)}, bf16[64,512]{1,0:T(8,128)(2,1)S(1)}, u32[]{:S(2)}, u32[]{:S(2)}) collective-permute-start(bf16[64,512]{1,0:T(8,128)(2,1)} %param.23), channel_id=1, source_target_pairs={{0,16},{16,0},{32,48},{48,32},{1,17},{17,1},{33,49},{49,33},{2,18}... | collective-permute-start | bytes 196616 | tf_op jit(solution)/shard_map/ppermute | solution.py:30
  35.1 1.1 pad_maximum_fusion.own_ref
  36.2 2.8 %all-to-all-done = bf16[32,6,512]{2,1,0:T(8,128)(2,1)S(1)} async-done(((bf16[32,6,512]{2,1,0:T(8,128)(2,1)}), bf16[32,6,512]{2,1,0:T(8,128)(2,1)S(1)}, u32[]{:S(2)}, u32[]{:S(2)}) %all-to-all-start) | async-done | bytes 196640 | tf_op jit(solution)/shard_map/all_to_all | solution.py:22
  39.0 0.1 reshape.22.rows_ref
  39.1 0.0 copy-start.4
  39.1 0.0 copy-start.5
  39.1 0.0 copy-start.6
  39.1 0.0 copy-start.7
  39.1 0.0 copy-start.8
  39.1 0.0 copy-start.9
  39.2 0.0 copy-start
  39.2 0.0 copy-start.1
  39.2 0.0 collective-permute-done.gate_other_ref
  39.2 0.0 collective-permute-done.1.up_other_ref
  39.2 1.1 shard_map.132
  40.3 0.0 collective-permute-done.2
  40.3 14.6 %all-to-all-start.1 = ((bf16[8,24,1024]{2,1,0:T(8,128)(2,1)}), bf16[8,24,1024]{2,1,0:T(8,128)(2,1)S(1)}, u32[]{:S(2)}, u32[]{:S(2)}) async-start(bf16[8,24,1024]{2,1,0:T(8,128)(2,1)} %bitcast.4), calls=%async_computation.1 | async-start | bytes 786432 | tf_op jit(solution)/shard_map/all_to_all | solution.py:22
  54.9 0.0 all-gather.2.cloned.1.call-start
  55.0 0.0 copy-done.3
  55.0 4.7 %collective-permute-start.3 = (bf16[128,512]{1,0:T(8,128)(2,1)S(1)}, bf16[128,512]{1,0:T(8,128)(2,1)S(1)}, u32[]{:S(2)}, u32[]{:S(2)}) collective-permute-start(bf16[128,512]{1,0:T(8,128)(2,1)S(1)} %pad_maximum_fusion.2), channel_id=1, source_target_pairs={{0,32},{16,48},{32,0},{48,16},{1,33},{17,49},{33,1},{49,17},{2,34}... | collective-permute-start | bytes 393224 | tf_op jit(solution)/shard_map/ppermute | solution.py:30
  59.7 8.5 %all-to-all-done.1.parts_ref = bf16[8,24,1024]{2,1,0:T(8,128)(2,1)S(1)} async-done(((bf16[8,24,1024]{2,1,0:T(8,128)(2,1)}), bf16[8,24,1024]{2,1,0:T(8,128)(2,1)S(1)}, u32[]{:S(2)}, u32[]{:S(2)}) %all-to-all-start.1) | async-done | bytes 393248 | tf_op jit(solution)/shard_map/all_to_all | solution.py:22
  68.2 0.8 shard_map.133
  69.0 0.0 collective-permute-done.3
  69.1 0.7 pad_maximum_fusion.1
  69.8 0.0 all-gather.2.cloned.1.call-update
  69.8 5.3 %all-to-all-start.2 = ((bf16[8,24,512]{2,1,0:T(8,128)(2,1)}), bf16[8,24,512]{2,1,0:T(8,128)(2,1)S(1)}, u32[]{:S(2)}, u32[]{:S(2)}) async-start(bf16[8,24,512]{2,1,0:T(8,128)(2,1)} %shard_map.133), calls=%async_computation.2 | async-start | bytes 393216 | tf_op jit(solution)/shard_map/all_to_all | solution.py:22
  75.1 0.0 copy-done.2
  75.1 1.9 %collective-permute-start.4 = (bf16[256,512]{1,0:T(8,128)(2,1)S(1)}, bf16[256,512]{1,0:T(8,128)(2,1)S(1)}, u32[]{:S(2)}, u32[]{:S(2)}) collective-permute-start(bf16[256,512]{1,0:T(8,128)(2,1)S(1)} %copy-done.2), channel_id=1, source_target_pairs={{0,1},{1,0},{2,3},{3,2},{4,5},{5,4},{6,7},{7,6},{8,9},{9,8},{10,11... | collective-permute-start | bytes 786440 | tf_op jit(solution)/shard_map/ppermute | solution.py:26
  77.1 7.8 %all-to-all-done.2 = bf16[8,24,512]{2,1,0:T(8,128)(2,1)S(1)} async-done(((bf16[8,24,512]{2,1,0:T(8,128)(2,1)}), bf16[8,24,512]{2,1,0:T(8,128)(2,1)S(1)}, u32[]{:S(2)}, u32[]{:S(2)}) %all-to-all-start.2) | async-done | bytes 196640 | tf_op jit(solution)/shard_map/all_to_all | solution.py:22
  84.9 0.2 fusion.2
  85.1 0.0 collective-permute-done.4
  85.1 0.2 fusion
  85.4 0.1 reshape.25
  85.4 25.2 %all_to_all.25.parts_ref = bf16[32,6,512]{2,1,0:T(8,128)(2,1)S(1)} all-to-all(bf16[32,6,512]{2,1,0:T(8,128)(2,1)S(1)} %reshape.25), channel_id=1, replica_groups=mesh['y_lo'=2,'z'=8,'y_hi'=4,'x'=8,'core'=2] {'y_hi','x'}, dimensions={0} | all-to-all | bytes 393216 | tf_op jit(solution)/shard_map/all_to_all | solution.py:22
  110.7 0.7 shard_map.134
  111.4 3.5 %all-to-all-start.4 = ((bf16[16,8,512]{2,1,0:T(8,128)(2,1)}), bf16[16,8,512]{2,1,0:T(8,128)(2,1)S(1)}, u32[]{:S(2)}, u32[]{:S(2)}) async-start(bf16[16,8,512]{2,1,0:T(8,128)(2,1)} %shard_map.134), calls=%async_computation.4 | async-start | bytes 262144 | tf_op jit(solution)/shard_map/all_to_all | solution.py:22
  114.9 0.0 copy-done.4
  115.0 0.1 copy.18.column_ref
  115.1 0.1 copy.19.gate_ref
  115.2 8.2 %all-to-all-done.4 = bf16[16,8,512]{2,1,0:T(8,128)(2,1)S(1)} async-done(((bf16[16,8,512]{2,1,0:T(8,128)(2,1)}), bf16[16,8,512]{2,1,0:T(8,128)(2,1)S(1)}, u32[]{:S(2)}, u32[]{:S(2)}) %all-to-all-start.4) | async-done | bytes 131104 | tf_op jit(solution)/shard_map/all_to_all | solution.py:22
  123.4 0.0 copy-done
  123.4 3.4 %shard_map.135 = (bf16[128,4096]{1,0:T(8,128)(2,1)}, bf16[128,512]{1,0:T(8,128)(2,1)}) custom-call(bf16[128,4096]{1,0:T(8,128)(2,1)S(1)} %copy-done, bf16[128,512]{1,0:T(8,128)(2,1)S(1)} %bitcast.16, s32[128,1]{1,0:T(8,128)S(1)} %copy.18.column_ref, f32[128,1]{1,0:T(8,128)S(1)} %copy.19.gate_ref, f32[1,4096]{1,0:T(1,128)S(1)} %bitcast.17, ...), custom_call_target="tpu_custom_call" | custom-call | flops 536870912 | bytes 8388608 | tf_op jit(solution)/shard_map/pallas_call | solution.py:170
  (12 shorter events, 0.1 us)
Async XLA Ops:
  7.2 47.8 %copy-start.3 = (bf16[64,512]{1,0:T(8,128)(2,1)S(1)}, bf16[64,512]{1,0:T(8,128)(2,1)}, u32[]{:S(2)}) copy-start(bf16[64,512]{1,0:T(8,128)(2,1)} %param.23) | copy-start | bytes 196612
  7.2 68.0 %copy-start.2 = (bf16[256,512]{1,0:T(8,128)(2,1)S(1)}, bf16[256,512]{1,0:T(8,128)(2,1)}, u32[]{:S(2)}) copy-start(bf16[256,512]{1,0:T(8,128)(2,1)} %param.21) | copy-start | bytes 786436
  9.7 29.3 %all-to-all-start = ((bf16[32,6,512]{2,1,0:T(8,128)(2,1)}), bf16[32,6,512]{2,1,0:T(8,128)(2,1)S(1)}, u32[]{:S(2)}, u32[]{:S(2)}) async-start(bf16[32,6,512]{2,1,0:T(8,128)(2,1)} %shard_map.131), calls=%async_computation | async-start | bytes 524288 | tf_op jit(solution)/shard_map/all_to_all | solution.py:22
  26.4 12.8 %collective-permute-start = (bf16[512,256]{1,0:T(8,128)(2,1)}, bf16[512,256]{1,0:T(8,128)(2,1)S(1)}, u32[]{:S(2)}, u32[]{:S(2)}) collective-permute-start(bf16[512,256]{1,0:T(8,128)(2,1)} %param.19), channel_id=1, source_target_pairs={{0,1},{1,0},{2,3},{3,2},{4,5},{5,4},{6,7},{7,6},{8,9},{9,8},{10,11... | collective-permute-start | bytes 786440 | tf_op jit(solution)/shard_map/ppermute | solution.py:26
  28.3 10.9 %collective-permute-start.1 = (bf16[512,256]{1,0:T(8,128)(2,1)}, bf16[512,256]{1,0:T(8,128)(2,1)S(1)}, u32[]{:S(2)}, u32[]{:S(2)}) collective-permute-start(bf16[512,256]{1,0:T(8,128)(2,1)} %param.20), channel_id=1, source_target_pairs={{0,1},{1,0},{2,3},{3,2},{4,5},{5,4},{6,7},{7,6},{8,9},{9,8},{10,11... | collective-permute-start | bytes 786440 | tf_op jit(solution)/shard_map/ppermute | solution.py:26
  30.8 9.6 %collective-permute-start.2 = (bf16[64,512]{1,0:T(8,128)(2,1)}, bf16[64,512]{1,0:T(8,128)(2,1)S(1)}, u32[]{:S(2)}, u32[]{:S(2)}) collective-permute-start(bf16[64,512]{1,0:T(8,128)(2,1)} %param.23), channel_id=1, source_target_pairs={{0,16},{16,0},{32,48},{48,32},{1,17},{17,1},{33,49},{49,33},{2,18}... | collective-permute-start | bytes 196616 | tf_op jit(solution)/shard_map/ppermute | solution.py:30
  39.1 75.8 %copy-start.4 = (s32[128]{0:T(128)S(1)}, s32[128]{0:T(128)}, u32[]{:S(2)}) copy-start(s32[128]{0:T(128)} %param.14) | copy-start | bytes 1540
  39.1 75.8 %copy-start.5 = (s32[128]{0:T(128)S(1)}, s32[128]{0:T(128)}, u32[]{:S(2)}) copy-start(s32[128]{0:T(128)} %param.13) | copy-start | bytes 1540
  39.1 75.8 %copy-start.6 = (s32[128]{0:T(128)S(1)}, s32[128]{0:T(128)}, u32[]{:S(2)}) copy-start(s32[128]{0:T(128)} %param.15) | copy-start | bytes 1540
  39.1 75.8 %copy-start.7 = (s32[128]{0:T(128)S(1)}, s32[128]{0:T(128)}, u32[]{:S(2)}) copy-start(s32[128]{0:T(128)} %param.16) | copy-start | bytes 1540
  39.1 75.9 %copy-start.8 = (f32[128]{0:T(128)S(1)}, f32[128]{0:T(128)}, u32[]{:S(2)}) copy-start(f32[128]{0:T(128)} %param.17) | copy-start | bytes 1540
  39.1 75.9 %copy-start.9 = (f32[128]{0:T(128)S(1)}, f32[128]{0:T(128)}, u32[]{:S(2)}) copy-start(f32[128]{0:T(128)} %param.18) | copy-start | bytes 1540
  39.2 84.3 %copy-start = (bf16[128,4096]{1,0:T(8,128)(2,1)S(1)}, bf16[128,4096]{1,0:T(8,128)(2,1)}, u32[]{:S(2)}) copy-start(bf16[128,4096]{1,0:T(8,128)(2,1)} %tokens_ref.1) | copy-start | bytes 3145732
  39.2 84.3 %copy-start.1 = (f32[4096]{0:T(1024)S(1)}, f32[4096]{0:T(1024)}, u32[]{:S(2)}) copy-start(f32[4096]{0:T(1024)} %param.22) | copy-start | bytes 49156
  40.3 27.9 %all-to-all-start.1 = ((bf16[8,24,1024]{2,1,0:T(8,128)(2,1)}), bf16[8,24,1024]{2,1,0:T(8,128)(2,1)S(1)}, u32[]{:S(2)}, u32[]{:S(2)}) async-start(bf16[8,24,1024]{2,1,0:T(8,128)(2,1)} %bitcast.4), calls=%async_computation.1 | async-start | bytes 786432 | tf_op jit(solution)/shard_map/all_to_all | solution.py:22
  54.9 68.5 %all-gather.2.cloned.1.call-start = ((), (), s32[]{:S(2)}) async-start(), calls=%async_computation.5 | async-start | bytes 4456448 | tf_op jit(solution)/shard_map/all_gather | solution.py:246
  55.0 14.0 %collective-permute-start.3 = (bf16[128,512]{1,0:T(8,128)(2,1)S(1)}, bf16[128,512]{1,0:T(8,128)(2,1)S(1)}, u32[]{:S(2)}, u32[]{:S(2)}) collective-permute-start(bf16[128,512]{1,0:T(8,128)(2,1)S(1)} %pad_maximum_fusion.2), channel_id=1, source_target_pairs={{0,32},{16,48},{32,0},{48,16},{1,33},{17,49},{33,1},{49,17},{2,34}... | collective-permute-start | bytes 393224 | tf_op jit(solution)/shard_map/ppermute | solution.py:30
  69.8 15.1 %all-to-all-start.2 = ((bf16[8,24,512]{2,1,0:T(8,128)(2,1)}), bf16[8,24,512]{2,1,0:T(8,128)(2,1)S(1)}, u32[]{:S(2)}, u32[]{:S(2)}) async-start(bf16[8,24,512]{2,1,0:T(8,128)(2,1)} %shard_map.133), calls=%async_computation.2 | async-start | bytes 393216 | tf_op jit(solution)/shard_map/all_to_all | solution.py:22
  75.1 10.0 %collective-permute-start.4 = (bf16[256,512]{1,0:T(8,128)(2,1)S(1)}, bf16[256,512]{1,0:T(8,128)(2,1)S(1)}, u32[]{:S(2)}, u32[]{:S(2)}) collective-permute-start(bf16[256,512]{1,0:T(8,128)(2,1)S(1)} %copy-done.2), channel_id=1, source_target_pairs={{0,1},{1,0},{2,3},{3,2},{4,5},{5,4},{6,7},{7,6},{8,9},{9,8},{10,11... | collective-permute-start | bytes 786440 | tf_op jit(solution)/shard_map/ppermute | solution.py:26
  111.4 12.0 %all-to-all-start.4 = ((bf16[16,8,512]{2,1,0:T(8,128)(2,1)}), bf16[16,8,512]{2,1,0:T(8,128)(2,1)S(1)}, u32[]{:S(2)}, u32[]{:S(2)}) async-start(bf16[16,8,512]{2,1,0:T(8,128)(2,1)} %shard_map.134), calls=%async_computation.4 | async-start | bytes 262144 | tf_op jit(solution)/shard_map/all_to_all | solution.py:22
Sparse Core Ops, SparseCore 0:
  69.9 46.8 all-gather.1

commit v10 on v9

--- a/solution.py
+++ b/solution.py
@@ -14,6 +14,7 @@
 SIZES = {"y_lo": 2, "z": 8, "y_hi": 4, "x": 8, "core": 2}
 PADDED = 8
 LANES = 128
+PIECES = 4
 VMEM_BYTES = 60 * 1024 * 1024
 FINISH_BYTES = 50 * 1024 * 1024
 
@@ -30,9 +31,9 @@
     return lax.ppermute(block, "y_hi", [(i, i ^ bit) for i in range(lax.axis_size("y_hi"))])
 
 
-def in_order(own, other, bit):
+def in_order(own, other, bit, axis):
     upper = (lax.axis_index("y_hi") & bit) != 0
-    return jnp.concatenate([jnp.where(upper, other, own), jnp.where(upper, own, other)], axis=0)
+    return jnp.stack([jnp.where(upper, other, own), jnp.where(upper, own, other)], axis=axis)
 
 
 def tie(*values):
@@ -57,19 +58,33 @@
 
 
 def slots_kernel(
-    tokens_hbm, first_expert_ref, first_slot_ref, second_expert_ref, second_slot_ref, out_ref, block_ref, sem
+    tokens_hbm, first_expert_hbm, first_slot_hbm, second_expert_hbm, second_slot_hbm, out_ref, block_ref, *refs
 ):
+    ids, sem = refs[:-1], refs[-1]
     width = block_ref.shape[1]
     start = pl.multiple_of(lax.axis_index("z") * width, LANES)
-    load = pltpu.make_async_copy(tokens_hbm.at[:, pl.ds(start, width)], block_ref, sem)
-    load.start()
+    sources = (first_expert_hbm, first_slot_hbm, second_expert_hbm, second_slot_hbm)
+    loads = [pltpu.make_async_copy(s, d, sem.at[i]) for i, (s, d) in enumerate(zip(sources, ids, strict=True))]
+    share = block_ref.shape[0] // PIECES
+    for i in range(PIECES):
+        rows = pl.ds(i * share, share)
+        loads.append(
+            pltpu.make_async_copy(
+                tokens_hbm.at[rows, pl.ds(start, width)], block_ref.at[rows], sem.at[len(ids) + i]
+            )
+        )
+    for load in loads:
+        load.start()
+    for load in loads[: len(ids)]:
+        load.wait()
     own = lax.axis_index("y_lo")
-    first, second = first_slot_ref[...], second_slot_ref[...]
-    placement = jnp.where((second_expert_ref[...] == own) & (second >= 0), second + CAP1, -1)
-    placement = jnp.where((first_expert_ref[...] == own) & (first >= 0), first, placement)
+    first_expert, first, second_expert, second = (ref[...] for ref in ids)
+    placement = jnp.where((second_expert == own) & (second >= 0), second + CAP1, -1)
+    placement = jnp.where((first_expert == own) & (first >= 0), first, placement)
     slots = lax.broadcasted_iota(jnp.int32, (PADDED, placement.shape[1]), 0)
     hot = (slots == placement).astype(jnp.bfloat16)
-    load.wait()
+    for load in loads[len(ids) :]:
+        load.wait()
     rows = jnp.dot(hot, block_ref[...], preferred_element_type=jnp.float32).astype(jnp.bfloat16)
     for i in range(out_ref.shape[0]):
         out_ref[i] = rows[:SLOTS]
@@ -217,19 +232,23 @@
     slot_copies = small_call(
         slots_kernel,
         (chips, SLOTS, block_width),
-        4,
+        0,
         tokens,
         first_expert[None, :],
         first_slot[None, :],
         second_expert[None, :],
         second_slot[None, :],
-        scratch=(pltpu.VMEM((tok_count, block_width), jnp.bfloat16), pltpu.SemaphoreType.DMA(())),
+        scratch=(
+            pltpu.VMEM((tok_count, block_width), jnp.bfloat16),
+            *[pltpu.VMEM((1, tok_count), jnp.int32)] * 4,
+            pltpu.SemaphoreType.DMA((4 + PIECES,)),
+        ),
     )
     slot_copies, w_query = tie(slot_copies, w_query)
     rows = exchange(slot_copies, CHIPS).reshape(chips * SLOTS, block_width)
     w_gate_other = other_core(w_gate)
     w_up_other = other_core(w_up)
-    w_query_beside = across(w_query, 1)
+    w_query_beside = across(w_query, 2)
 
     w_own = jnp.concatenate([w_gate, w_up], axis=1)
     partial = small_call(
@@ -238,11 +257,11 @@
     share = chips * SLOTS // blocks
     partial, w_query, w_query_beside = tie(partial, w_query, w_query_beside)
     summed = exchange(partial.reshape(blocks, share, 4 * units), "z")
-    query_rows = in_order(w_query, w_query_beside, 1)
-    query_rows_other = across(query_rows, 2)
+    query_rows = in_order(w_query, w_query_beside, 2, 0)
+    query_rows_other = across(query_rows, 1)
     hidden_copies = small_call(hidden_kernel, (blocks, share, 2 * units), 1, summed)
     hidden_copies, query_rows_other = tie(hidden_copies, query_rows_other)
-    query_rows = in_order(query_rows, query_rows_other, 2).reshape((-1,) + w_query.shape)
+    query_rows = in_order(query_rows, query_rows_other, 1, 1).reshape((-1,) + w_query.shape)
     w_query_full = lax.all_gather(query_rows, ("x", "core"), axis=0)
     w_query_full = w_query_full.reshape((-1, 2) + query_rows.shape)
     hidden = exchange(hidden_copies, "z").reshape(chips * SLOTS, 2 * units)

time: 134 us -> 134 us (level)
  waiting for transfers between devices: 27.4 us -> 25 us
  blocking collectives: 25.2 us -> 27.4 us
    ppermute x2, starting transfers between devices: 9.01 us -> 12.2 us  [across(): lax.ppermute(block, 'y_hi', [(i, i ^ bit) for i in range(lax.axis_size('y...]
    all_to_all x4, waiting for transfers between devices: 27.4 us -> 24.5 us  [exchange(): return lax.all_to_all(blocks, axes, split_axis=0, concat_axis=0, tiled=True)]
    all_to_all x4, starting transfers between devices: 40.1 us -> 37.6 us  [exchange(): return lax.all_to_all(blocks, axes, split_axis=0, concat_axis=0, tiled=True)]
    all_to_all x1, blocking collectives: 25.2 us -> 27.4 us  [exchange(): return lax.all_to_all(blocks, axes, split_axis=0, concat_axis=0, tiled=True)]
where the time goes in v10:
time: 134 us; the launch traced here: 133 us
  starting transfers between devices  56.1 us (42%)
  blocking collectives  27.4 us (20%)
  waiting for transfers between devices  25 us (19%)
  between operations  14.4 us (11%)
  Pallas kernels  7.81 us (6%)
  other arithmetic  1.86 us (1%)
    all_to_all x4, starting transfers between devices, exchange(): return lax.all_to_all(blocks, axes, split_axis=0, concat_axis=0, tiled=True)  37.6 us
    all_to_all x1, blocking collectives, exchange(): return lax.all_to_all(blocks, axes, split_axis=0, concat_axis=0, tiled=True)  27.4 us
    all_to_all x4, waiting for transfers between devices, exchange(): return lax.all_to_all(blocks, axes, split_axis=0, concat_axis=0, tiled=True)  24.5 us
    ppermute x2, starting transfers between devices, across(): lax.ppermute(block, 'y_hi', [(i, i ^ bit) for i in range(lax.axis_size('y...  12.2 us
    ppermute x3, starting transfers between devices, other_core(): return lax.ppermute(block, 'core', [(0, 1), (1, 0)])  6.25 us
    pallas_call x4, Pallas kernels, small_call(): pl.pallas_call(kernel, out_shape=jax.ShapeDtypeStruct(shape, jnp.bfloat16...  4.44 us
    pallas_call x1, Pallas kernels, finish(): pl.pallas_call(finish_kernel, out_shape=(jax.ShapeDtypeStruct((tok_count,...  3.37 us
  transfers between devices with their start and end apart: 10, of which 4 were waited for; matrix products, arithmetic and copies ran while one was open for 1% of the time, Pallas kernels for 2%

profile of v10, /device:TPU:4, one launch (start us, length us, event | category | flops | bytes accessed | tf_op | source)
XLA Modules:
  0.0 133.3 jit_solution(12461609400411182080)
XLA Ops:
  7.2 0.0 copy-start.3
  7.2 0.0 copy-start.2
  7.2 1.8 %shard_map.131 = bf16[32,6,512]{2,1,0:T(8,128)(2,1)} custom-call(bf16[128,4096]{1,0:T(8,128)(2,1)} %tokens_ref.1, s32[1,128]{1,0:T(1,128)} %bitcast.33, s32[1,128]{1,0:T(1,128)} %bitcast.32, s32[1,128]{1,0:T(1,128)} %bitcast.34, s32[1,128]{1,0:T(1,128)} %bitcast.35), custom_call_target="tpu_custom_call" | custom-call | flops 196608 | bytes 393216 | tf_op jit(solution)/shard_map/pallas_call | solution.py:49
  9.0 16.7 %all-to-all-start = ((bf16[32,6,512]{2,1,0:T(8,128)(2,1)}), bf16[32,6,512]{2,1,0:T(8,128)(2,1)S(1)}, u32[]{:S(2)}, u32[]{:S(2)}) async-start(bf16[32,6,512]{2,1,0:T(8,128)(2,1)} %shard_map.131), calls=%async_computation | async-start | bytes 524288 | tf_op jit(solution)/shard_map/all_to_all | solution.py:23
  25.7 1.9 %collective-permute-start = (bf16[512,256]{1,0:T(8,128)(2,1)}, bf16[512,256]{1,0:T(8,128)(2,1)S(1)}, u32[]{:S(2)}, u32[]{:S(2)}) collective-permute-start(bf16[512,256]{1,0:T(8,128)(2,1)} %param.19), channel_id=1, source_target_pairs={{0,1},{1,0},{2,3},{3,2},{4,5},{5,4},{6,7},{7,6},{8,9},{9,8},{10,11... | collective-permute-start | bytes 786440 | tf_op jit(solution)/shard_map/ppermute | solution.py:27
  27.7 2.4 %collective-permute-start.1 = (bf16[512,256]{1,0:T(8,128)(2,1)}, bf16[512,256]{1,0:T(8,128)(2,1)S(1)}, u32[]{:S(2)}, u32[]{:S(2)}) collective-permute-start(bf16[512,256]{1,0:T(8,128)(2,1)} %param.20), channel_id=1, source_target_pairs={{0,1},{1,0},{2,3},{3,2},{4,5},{5,4},{6,7},{7,6},{8,9},{9,8},{10,11... | collective-permute-start | bytes 786440 | tf_op jit(solution)/shard_map/ppermute | solution.py:27
  30.1 7.4 %collective-permute-start.2 = (bf16[64,512]{1,0:T(8,128)(2,1)}, bf16[64,512]{1,0:T(8,128)(2,1)S(1)}, u32[]{:S(2)}, u32[]{:S(2)}) collective-permute-start(bf16[64,512]{1,0:T(8,128)(2,1)} %param.23), channel_id=1, source_target_pairs={{0,32},{16,48},{32,0},{48,16},{1,33},{17,49},{33,1},{49,17},{2,34}... | collective-permute-start | bytes 196616 | tf_op jit(solution)/shard_map/ppermute | solution.py:31
  37.5 1.1 pad_maximum_fusion.own_ref
  38.6 0.0 all-to-all-done
  38.6 0.1 reshape.22.rows_ref
  38.6 0.0 copy-start.4
  38.7 0.0 copy-start.5
  38.7 0.0 copy-start.6
  38.7 0.0 copy-start.7
  38.7 0.0 copy-start.8
  38.7 0.0 copy-start.9
  38.7 0.0 copy-start
  38.7 0.0 copy-start.1
  38.7 0.0 collective-permute-done.gate_other_ref
  38.7 0.0 collective-permute-done.1.up_other_ref
  38.8 1.1 shard_map.132
  39.9 0.5 collective-permute-done.2
  40.4 13.9 %all-to-all-start.1 = ((bf16[8,24,1024]{2,1,0:T(8,128)(2,1)}), bf16[8,24,1024]{2,1,0:T(8,128)(2,1)S(1)}, u32[]{:S(2)}, u32[]{:S(2)}) async-start(bf16[8,24,1024]{2,1,0:T(8,128)(2,1)} %bitcast.4), calls=%async_computation.1 | async-start | bytes 786432 | tf_op jit(solution)/shard_map/all_to_all | solution.py:23
  54.2 0.0 all-gather.2.cloned.1.call-start
  54.3 0.0 copy-done.3
  54.3 4.8 %collective-permute-start.3 = (bf16[2,64,512]{2,1,0:T(8,128)(2,1)S(1)}, bf16[2,64,512]{2,1,0:T(8,128)(2,1)S(1)}, u32[]{:S(2)}, u32[]{:S(2)}) collective-permute-start(bf16[2,64,512]{2,1,0:T(8,128)(2,1)S(1)} %pad_maximum_fusion.2), channel_id=1, source_target_pairs={{0,16},{16,0},{32,48},{48,32},{1,17},{17,1},{33,49},{49,33},{2,18}... | collective-permute-start | bytes 393224 | tf_op jit(solution)/shard_map/ppermute | solution.py:31
  59.1 8.4 %all-to-all-done.1.parts_ref = bf16[8,24,1024]{2,1,0:T(8,128)(2,1)S(1)} async-done(((bf16[8,24,1024]{2,1,0:T(8,128)(2,1)}), bf16[8,24,1024]{2,1,0:T(8,128)(2,1)S(1)}, u32[]{:S(2)}, u32[]{:S(2)}) %all-to-all-start.1) | async-done | bytes 393248 | tf_op jit(solution)/shard_map/all_to_all | solution.py:23
  67.6 0.8 shard_map.133
  68.4 0.0 collective-permute-done.3
  68.4 0.7 pad_maximum_fusion.1
  69.1 0.0 all-gather.2.cloned.1.call-update
  69.1 3.4 %all-to-all-start.2 = ((bf16[8,24,512]{2,1,0:T(8,128)(2,1)}), bf16[8,24,512]{2,1,0:T(8,128)(2,1)S(1)}, u32[]{:S(2)}, u32[]{:S(2)}) async-start(bf16[8,24,512]{2,1,0:T(8,128)(2,1)} %shard_map.133), calls=%async_computation.2 | async-start | bytes 393216 | tf_op jit(solution)/shard_map/all_to_all | solution.py:23
  72.5 0.0 copy-done.2
  72.6 1.9 %collective-permute-start.4 = (bf16[256,512]{1,0:T(8,128)(2,1)S(1)}, bf16[256,512]{1,0:T(8,128)(2,1)S(1)}, u32[]{:S(2)}, u32[]{:S(2)}) collective-permute-start(bf16[256,512]{1,0:T(8,128)(2,1)S(1)} %copy-done.2), channel_id=1, source_target_pairs={{0,1},{1,0},{2,3},{3,2},{4,5},{5,4},{6,7},{7,6},{8,9},{9,8},{10,11... | collective-permute-start | bytes 786440 | tf_op jit(solution)/shard_map/ppermute | solution.py:27
  74.5 7.7 %all-to-all-done.2 = bf16[8,24,512]{2,1,0:T(8,128)(2,1)S(1)} async-done(((bf16[8,24,512]{2,1,0:T(8,128)(2,1)}), bf16[8,24,512]{2,1,0:T(8,128)(2,1)S(1)}, u32[]{:S(2)}, u32[]{:S(2)}) %all-to-all-start.2) | async-done | bytes 196640 | tf_op jit(solution)/shard_map/all_to_all | solution.py:23
  82.2 0.2 fusion.2
  82.4 0.0 collective-permute-done.4
  82.5 0.2 fusion
  82.7 0.1 reshape.25
  82.7 27.4 %all_to_all.25.parts_ref = bf16[32,6,512]{2,1,0:T(8,128)(2,1)S(1)} all-to-all(bf16[32,6,512]{2,1,0:T(8,128)(2,1)S(1)} %reshape.25), channel_id=1, replica_groups=mesh['y_lo'=2,'z'=8,'y_hi'=4,'x'=8,'core'=2] {'y_hi','x'}, dimensions={0} | all-to-all | bytes 393216 | tf_op jit(solution)/shard_map/all_to_all | solution.py:23
  110.1 0.7 shard_map.134
  110.8 3.7 %all-to-all-start.4 = ((bf16[16,8,512]{2,1,0:T(8,128)(2,1)}), bf16[16,8,512]{2,1,0:T(8,128)(2,1)S(1)}, u32[]{:S(2)}, u32[]{:S(2)}) async-start(bf16[16,8,512]{2,1,0:T(8,128)(2,1)} %shard_map.134), calls=%async_computation.4 | async-start | bytes 262144 | tf_op jit(solution)/shard_map/all_to_all | solution.py:23
  114.5 0.1 copy.20.column_ref
  114.6 0.0 copy-done.9
  114.7 0.1 copy.21.gate_ref
  114.8 8.3 %all-to-all-done.4 = bf16[16,8,512]{2,1,0:T(8,128)(2,1)S(1)} async-done(((bf16[16,8,512]{2,1,0:T(8,128)(2,1)}), bf16[16,8,512]{2,1,0:T(8,128)(2,1)S(1)}, u32[]{:S(2)}, u32[]{:S(2)}) %all-to-all-start.4) | async-done | bytes 131104 | tf_op jit(solution)/shard_map/all_to_all | solution.py:23
  123.0 0.0 copy-done.1
  123.0 3.4 %shard_map.135 = (bf16[128,4096]{1,0:T(8,128)(2,1)}, bf16[128,512]{1,0:T(8,128)(2,1)}) custom-call(bf16[128,4096]{1,0:T(8,128)(2,1)S(1)} %copy-done, bf16[128,512]{1,0:T(8,128)(2,1)S(1)} %bitcast.26, s32[128,1]{1,0:T(8,128)S(1)} %copy.20.column_ref, f32[128,1]{1,0:T(8,128)S(1)} %copy.21.gate_ref, f32[1,4096]{1,0:T(1,128)S(1)} %bitcast.27, ...), custom_call_target="tpu_custom_call" | custom-call | flops 536870912 | bytes 8388608 | tf_op jit(solution)/shard_map/pallas_call | solution.py:185
  (12 shorter events, 0.1 us)
Async XLA Ops:
  7.2 47.1 %copy-start.3 = (bf16[64,512]{1,0:T(8,128)(2,1)S(1)}, bf16[64,512]{1,0:T(8,128)(2,1)}, u32[]{:S(2)}) copy-start(bf16[64,512]{1,0:T(8,128)(2,1)} %param.23) | copy-start | bytes 196612
  7.2 65.4 %copy-start.2 = (bf16[256,512]{1,0:T(8,128)(2,1)S(1)}, bf16[256,512]{1,0:T(8,128)(2,1)}, u32[]{:S(2)}) copy-start(bf16[256,512]{1,0:T(8,128)(2,1)} %param.21) | copy-start | bytes 786436
  9.0 29.5 %all-to-all-start = ((bf16[32,6,512]{2,1,0:T(8,128)(2,1)}), bf16[32,6,512]{2,1,0:T(8,128)(2,1)S(1)}, u32[]{:S(2)}, u32[]{:S(2)}) async-start(bf16[32,6,512]{2,1,0:T(8,128)(2,1)} %shard_map.131), calls=%async_computation | async-start | bytes 524288 | tf_op jit(solution)/shard_map/all_to_all | solution.py:23
  25.7 13.0 %collective-permute-start = (bf16[512,256]{1,0:T(8,128)(2,1)}, bf16[512,256]{1,0:T(8,128)(2,1)S(1)}, u32[]{:S(2)}, u32[]{:S(2)}) collective-permute-start(bf16[512,256]{1,0:T(8,128)(2,1)} %param.19), channel_id=1, source_target_pairs={{0,1},{1,0},{2,3},{3,2},{4,5},{5,4},{6,7},{7,6},{8,9},{9,8},{10,11... | collective-permute-start | bytes 786440 | tf_op jit(solution)/shard_map/ppermute | solution.py:27
  27.7 11.1 %collective-permute-start.1 = (bf16[512,256]{1,0:T(8,128)(2,1)}, bf16[512,256]{1,0:T(8,128)(2,1)S(1)}, u32[]{:S(2)}, u32[]{:S(2)}) collective-permute-start(bf16[512,256]{1,0:T(8,128)(2,1)} %param.20), channel_id=1, source_target_pairs={{0,1},{1,0},{2,3},{3,2},{4,5},{5,4},{6,7},{7,6},{8,9},{9,8},{10,11... | collective-permute-start | bytes 786440 | tf_op jit(solution)/shard_map/ppermute | solution.py:27
  30.1 10.3 %collective-permute-start.2 = (bf16[64,512]{1,0:T(8,128)(2,1)}, bf16[64,512]{1,0:T(8,128)(2,1)S(1)}, u32[]{:S(2)}, u32[]{:S(2)}) collective-permute-start(bf16[64,512]{1,0:T(8,128)(2,1)} %param.23), channel_id=1, source_target_pairs={{0,32},{16,48},{32,0},{48,16},{1,33},{17,49},{33,1},{49,17},{2,34}... | collective-permute-start | bytes 196616 | tf_op jit(solution)/shard_map/ppermute | solution.py:31
  38.6 75.8 %copy-start.4 = (s32[128]{0:T(128)S(1)}, s32[128]{0:T(128)}, u32[]{:S(2)}) copy-start(s32[128]{0:T(128)} %param.14) | copy-start | bytes 1540
  38.7 75.8 %copy-start.5 = (s32[128]{0:T(128)S(1)}, s32[128]{0:T(128)}, u32[]{:S(2)}) copy-start(s32[128]{0:T(128)} %param.13) | copy-start | bytes 1540
  38.7 75.8 %copy-start.6 = (s32[128]{0:T(128)S(1)}, s32[128]{0:T(128)}, u32[]{:S(2)}) copy-start(s32[128]{0:T(128)} %param.15) | copy-start | bytes 1540
  38.7 75.8 %copy-start.7 = (s32[128]{0:T(128)S(1)}, s32[128]{0:T(128)}, u32[]{:S(2)}) copy-start(s32[128]{0:T(128)} %param.16) | copy-start | bytes 1540
  38.7 76.0 %copy-start.8 = (f32[128]{0:T(128)S(1)}, f32[128]{0:T(128)}, u32[]{:S(2)}) copy-start(f32[128]{0:T(128)} %param.17) | copy-start | bytes 1540
  38.7 75.9 %copy-start.9 = (f32[128]{0:T(128)S(1)}, f32[128]{0:T(128)}, u32[]{:S(2)}) copy-start(f32[128]{0:T(128)} %param.18) | copy-start | bytes 1540
  38.7 84.3 %copy-start = (bf16[128,4096]{1,0:T(8,128)(2,1)S(1)}, bf16[128,4096]{1,0:T(8,128)(2,1)}, u32[]{:S(2)}) copy-start(bf16[128,4096]{1,0:T(8,128)(2,1)} %tokens_ref.1) | copy-start | bytes 3145732
  38.7 84.3 %copy-start.1 = (f32[4096]{0:T(1024)S(1)}, f32[4096]{0:T(1024)}, u32[]{:S(2)}) copy-start(f32[4096]{0:T(1024)} %param.22) | copy-start | bytes 49156
  40.4 27.2 %all-to-all-start.1 = ((bf16[8,24,1024]{2,1,0:T(8,128)(2,1)}), bf16[8,24,1024]{2,1,0:T(8,128)(2,1)S(1)}, u32[]{:S(2)}, u32[]{:S(2)}) async-start(bf16[8,24,1024]{2,1,0:T(8,128)(2,1)} %bitcast.4), calls=%async_computation.1 | async-start | bytes 786432 | tf_op jit(solution)/shard_map/all_to_all | solution.py:23
  54.2 68.8 %all-gather.2.cloned.1.call-start = ((), (), s32[]{:S(2)}) async-start(), calls=%async_computation.5 | async-start | bytes 4456448 | tf_op jit(solution)/shard_map/all_gather | solution.py:265
  54.3 14.0 %collective-permute-start.3 = (bf16[2,64,512]{2,1,0:T(8,128)(2,1)S(1)}, bf16[2,64,512]{2,1,0:T(8,128)(2,1)S(1)}, u32[]{:S(2)}, u32[]{:S(2)}) collective-permute-start(bf16[2,64,512]{2,1,0:T(8,128)(2,1)S(1)} %pad_maximum_fusion.2), channel_id=1, source_target_pairs={{0,16},{16,0},{32,48},{48,32},{1,17},{17,1},{33,49},{49,33},{2,18}... | collective-permute-start | bytes 393224 | tf_op jit(solution)/shard_map/ppermute | solution.py:31
  69.1 13.1 %all-to-all-start.2 = ((bf16[8,24,512]{2,1,0:T(8,128)(2,1)}), bf16[8,24,512]{2,1,0:T(8,128)(2,1)S(1)}, u32[]{:S(2)}, u32[]{:S(2)}) async-start(bf16[8,24,512]{2,1,0:T(8,128)(2,1)} %shard_map.133), calls=%async_computation.2 | async-start | bytes 393216 | tf_op jit(solution)/shard_map/all_to_all | solution.py:23
  72.6 9.9 %collective-permute-start.4 = (bf16[256,512]{1,0:T(8,128)(2,1)S(1)}, bf16[256,512]{1,0:T(8,128)(2,1)S(1)}, u32[]{:S(2)}, u32[]{:S(2)}) collective-permute-start(bf16[256,512]{1,0:T(8,128)(2,1)S(1)} %copy-done.2), channel_id=1, source_target_pairs={{0,1},{1,0},{2,3},{3,2},{4,5},{5,4},{6,7},{7,6},{8,9},{9,8},{10,11... | collective-permute-start | bytes 786440 | tf_op jit(solution)/shard_map/ppermute | solution.py:27
  110.8 12.2 %all-to-all-start.4 = ((bf16[16,8,512]{2,1,0:T(8,128)(2,1)}), bf16[16,8,512]{2,1,0:T(8,128)(2,1)S(1)}, u32[]{:S(2)}, u32[]{:S(2)}) async-start(bf16[16,8,512]{2,1,0:T(8,128)(2,1)} %shard_map.134), calls=%async_computation.4 | async-start | bytes 262144 | tf_op jit(solution)/shard_map/all_to_all | solution.py:23
Sparse Core Ops, SparseCore 0:
  69.3 45.9 all-gather.1

commit v11 on v10

--- a/solution.py
+++ b/solution.py
@@ -255,7 +255,7 @@
         products_kernel, (chips * SLOTS, 4 * units), 4, rows, w_own, w_gate_other, w_up_other
     )
     share = chips * SLOTS // blocks
-    partial, w_query, w_query_beside = tie(partial, w_query, w_query_beside)
+    _, w_query, w_query_beside = tie(partial, w_query, w_query_beside)
     summed = exchange(partial.reshape(blocks, share, 4 * units), "z")
     query_rows = in_order(w_query, w_query_beside, 2, 0)
     query_rows_other = across(query_rows, 1)

time: 134 us -> 136 us (1.015)
  waiting for transfers between devices: 25 us -> 37.3 us
  blocking collectives: 27.4 us -> 19.7 us
  starting transfers between devices: 56.1 us -> 53.6 us
    ppermute x2, waiting for transfers between devices: 0.48 us -> 13.6 us  [across(): lax.ppermute(block, 'y_hi', [(i, i ^ bit) for i in range(lax.axis_size('y...]
    all_to_all x1, blocking collectives: 27.4 us -> 19.7 us  [exchange(): return lax.all_to_all(blocks, axes, split_axis=0, concat_axis=0, tiled=True)]
    ppermute x2, starting transfers between devices: 12.2 us -> 4.86 us  [across(): lax.ppermute(block, 'y_hi', [(i, i ^ bit) for i in range(lax.axis_size('y...]
    all_to_all x4, starting transfers between devices: 37.6 us -> 42.5 us  [exchange(): return lax.all_to_all(blocks, axes, split_axis=0, concat_axis=0, tiled=True)]
  transfers between devices with their start and end apart: 10 -> 10, of which waited for: 4 -> 6; matrix products, arithmetic and copies ran while one was open for 1% -> 1% of each run, Pallas kernels for 2% -> 1%
where the time goes in v11:
time: 136 us; the launch traced here: 135 us
  starting transfers between devices  53.6 us (39%)
  waiting for transfers between devices  37.3 us (27%)
  blocking collectives  19.7 us (14%)
  between operations  14.3 us (11%)
  Pallas kernels  7.81 us (6%)
  other arithmetic  1.86 us (1%)
    all_to_all x4, starting transfers between devices, exchange(): return lax.all_to_all(blocks, axes, split_axis=0, concat_axis=0, tiled=True)  42.5 us
    all_to_all x4, waiting for transfers between devices, exchange(): return lax.all_to_all(blocks, axes, split_axis=0, concat_axis=0, tiled=True)  23.7 us
    all_to_all x1, blocking collectives, exchange(): return lax.all_to_all(blocks, axes, split_axis=0, concat_axis=0, tiled=True)  19.7 us
    ppermute x2, waiting for transfers between devices, across(): lax.ppermute(block, 'y_hi', [(i, i ^ bit) for i in range(lax.axis_size('y...  13.6 us
    ppermute x3, starting transfers between devices, other_core(): return lax.ppermute(block, 'core', [(0, 1), (1, 0)])  6.25 us
    ppermute x2, starting transfers between devices, across(): lax.ppermute(block, 'y_hi', [(i, i ^ bit) for i in range(lax.axis_size('y...  4.86 us
    pallas_call x4, Pallas kernels, small_call(): pl.pallas_call(kernel, out_shape=jax.ShapeDtypeStruct(shape, jnp.bfloat16...  4.44 us
    pallas_call x1, Pallas kernels, finish(): pl.pallas_call(finish_kernel, out_shape=(jax.ShapeDtypeStruct((tok_count,...  3.37 us
  transfers between devices with their start and end apart: 10, of which 6 were waited for; matrix products, arithmetic and copies ran while one was open for 1% of the time, Pallas kernels for 1%

profile of v11, /device:TPU:4, one launch (start us, length us, event | category | flops | bytes accessed | tf_op | source)
XLA Modules:
  0.0 135.5 jit_solution(2062905247523547450)
XLA Ops:
  7.2 0.0 copy-start.3
  7.2 0.0 copy-start.2
  7.2 1.8 %shard_map.131 = bf16[32,6,512]{2,1,0:T(8,128)(2,1)} custom-call(bf16[128,4096]{1,0:T(8,128)(2,1)} %tokens_ref.1, s32[1,128]{1,0:T(1,128)} %bitcast.33, s32[1,128]{1,0:T(1,128)} %bitcast.32, s32[1,128]{1,0:T(1,128)} %bitcast.34, s32[1,128]{1,0:T(1,128)} %bitcast.35), custom_call_target="tpu_custom_call" | custom-call | flops 196608 | bytes 393216 | tf_op jit(solution)/shard_map/pallas_call | solution.py:49
  9.0 16.7 %all-to-all-start = ((bf16[32,6,512]{2,1,0:T(8,128)(2,1)}), bf16[32,6,512]{2,1,0:T(8,128)(2,1)S(1)}, u32[]{:S(2)}, u32[]{:S(2)}) async-start(bf16[32,6,512]{2,1,0:T(8,128)(2,1)} %shard_map.131), calls=%async_computation | async-start | bytes 524288 | tf_op jit(solution)/shard_map/all_to_all | solution.py:23
  25.7 1.9 %collective-permute-start = (bf16[512,256]{1,0:T(8,128)(2,1)}, bf16[512,256]{1,0:T(8,128)(2,1)S(1)}, u32[]{:S(2)}, u32[]{:S(2)}) collective-permute-start(bf16[512,256]{1,0:T(8,128)(2,1)} %param.19), channel_id=1, source_target_pairs={{0,1},{1,0},{2,3},{3,2},{4,5},{5,4},{6,7},{7,6},{8,9},{9,8},{10,11... | collective-permute-start | bytes 786440 | tf_op jit(solution)/shard_map/ppermute | solution.py:27
  27.7 2.4 %collective-permute-start.1 = (bf16[512,256]{1,0:T(8,128)(2,1)}, bf16[512,256]{1,0:T(8,128)(2,1)S(1)}, u32[]{:S(2)}, u32[]{:S(2)}) collective-permute-start(bf16[512,256]{1,0:T(8,128)(2,1)} %param.20), channel_id=1, source_target_pairs={{0,1},{1,0},{2,3},{3,2},{4,5},{5,4},{6,7},{7,6},{8,9},{9,8},{10,11... | collective-permute-start | bytes 786440 | tf_op jit(solution)/shard_map/ppermute | solution.py:27
  30.1 1.1 pad_maximum_fusion.own_ref
  31.2 7.2 %all-to-all-done = bf16[32,6,512]{2,1,0:T(8,128)(2,1)S(1)} async-done(((bf16[32,6,512]{2,1,0:T(8,128)(2,1)}), bf16[32,6,512]{2,1,0:T(8,128)(2,1)S(1)}, u32[]{:S(2)}, u32[]{:S(2)}) %all-to-all-start) | async-done | bytes 196640 | tf_op jit(solution)/shard_map/all_to_all | solution.py:23
  38.3 0.1 reshape.22.rows_ref
  38.4 0.0 copy-start.4
  38.4 0.0 copy-start.5
  38.4 0.0 copy-start.6
  38.4 0.0 copy-start.7
  38.5 0.0 copy-start.8
  38.5 0.0 copy-start.9
  38.5 0.0 copy-start
  38.5 0.0 copy-start.1
  38.5 0.0 collective-permute-done.gate_other_ref
  38.5 0.0 collective-permute-done.1.up_other_ref
  38.5 1.1 shard_map.132
  39.7 14.6 %all-to-all-start.1 = ((bf16[8,24,1024]{2,1,0:T(8,128)(2,1)}), bf16[8,24,1024]{2,1,0:T(8,128)(2,1)S(1)}, u32[]{:S(2)}, u32[]{:S(2)}) async-start(bf16[8,24,1024]{2,1,0:T(8,128)(2,1)} %bitcast.4), calls=%async_computation.1 | async-start | bytes 786432 | tf_op jit(solution)/shard_map/all_to_all | solution.py:23
  54.2 0.0 all-gather.2.cloned.1.call-start
  54.3 0.0 copy-done.3
  54.3 2.8 %collective-permute-start.2 = (bf16[64,512]{1,0:T(8,128)(2,1)S(1)}, bf16[64,512]{1,0:T(8,128)(2,1)S(1)}, u32[]{:S(2)}, u32[]{:S(2)}) collective-permute-start(bf16[64,512]{1,0:T(8,128)(2,1)S(1)} %copy-done.3), channel_id=1, source_target_pairs={{0,32},{16,48},{32,0},{48,16},{1,33},{17,49},{33,1},{49,17},{2,34}... | collective-permute-start | bytes 196616 | tf_op jit(solution)/shard_map/ppermute | solution.py:31
  57.1 7.9 %collective-permute-done.2 = bf16[64,512]{1,0:T(8,128)(2,1)S(1)} collective-permute-done((bf16[64,512]{1,0:T(8,128)(2,1)S(1)}, bf16[64,512]{1,0:T(8,128)(2,1)S(1)}, u32[]{:S(2)}, u32[]{:S(2)}) %collective-permute-start.2) | collective-permute-done | bytes 65568 | tf_op jit(solution)/shard_map/ppermute | solution.py:31
  65.1 2.1 %collective-permute-start.3 = (bf16[2,64,512]{2,1,0:T(8,128)(2,1)S(1)}, bf16[2,64,512]{2,1,0:T(8,128)(2,1)S(1)}, u32[]{:S(2)}, u32[]{:S(2)}) collective-permute-start(bf16[2,64,512]{2,1,0:T(8,128)(2,1)S(1)} %pad_maximum_fusion.2), channel_id=1, source_target_pairs={{0,16},{16,0},{32,48},{48,32},{1,17},{17,1},{33,49},{49,33},{2,18}... | collective-permute-start | bytes 393224 | tf_op jit(solution)/shard_map/ppermute | solution.py:31
  67.2 0.4 all-to-all-done.1.parts_ref
  67.6 0.8 shard_map.133
  68.3 5.7 %collective-permute-done.3 = bf16[2,64,512]{2,1,0:T(8,128)(2,1)S(1)} collective-permute-done((bf16[2,64,512]{2,1,0:T(8,128)(2,1)S(1)}, bf16[2,64,512]{2,1,0:T(8,128)(2,1)S(1)}, u32[]{:S(2)}, u32[]{:S(2)}) %collective-permute-start.3) | collective-permute-done | bytes 131104 | tf_op jit(solution)/shard_map/ppermute | solution.py:31
  74.0 0.7 pad_maximum_fusion.1
  74.8 0.0 all-gather.2.cloned.1.call-update
  74.8 7.2 %all-to-all-start.2 = ((bf16[8,24,512]{2,1,0:T(8,128)(2,1)}), bf16[8,24,512]{2,1,0:T(8,128)(2,1)S(1)}, u32[]{:S(2)}, u32[]{:S(2)}) async-start(bf16[8,24,512]{2,1,0:T(8,128)(2,1)} %shard_map.133), calls=%async_computation.2 | async-start | bytes 393216 | tf_op jit(solution)/shard_map/all_to_all | solution.py:23
  82.0 0.0 copy-done.2
  82.0 1.9 %collective-permute-start.4 = (bf16[256,512]{1,0:T(8,128)(2,1)S(1)}, bf16[256,512]{1,0:T(8,128)(2,1)S(1)}, u32[]{:S(2)}, u32[]{:S(2)}) collective-permute-start(bf16[256,512]{1,0:T(8,128)(2,1)S(1)} %copy-done.2), channel_id=1, source_target_pairs={{0,1},{1,0},{2,3},{3,2},{4,5},{5,4},{6,7},{7,6},{8,9},{9,8},{10,11... | collective-permute-start | bytes 786440 | tf_op jit(solution)/shard_map/ppermute | solution.py:27
  83.9 7.8 %all-to-all-done.2 = bf16[8,24,512]{2,1,0:T(8,128)(2,1)S(1)} async-done(((bf16[8,24,512]{2,1,0:T(8,128)(2,1)}), bf16[8,24,512]{2,1,0:T(8,128)(2,1)S(1)}, u32[]{:S(2)}, u32[]{:S(2)}) %all-to-all-start.2) | async-done | bytes 196640 | tf_op jit(solution)/shard_map/all_to_all | solution.py:23
  91.7 0.2 fusion.2
  91.9 0.0 collective-permute-done.4
  91.9 0.2 fusion
  92.2 0.1 reshape.25
  92.2 19.7 %all_to_all.25.parts_ref = bf16[32,6,512]{2,1,0:T(8,128)(2,1)S(1)} all-to-all(bf16[32,6,512]{2,1,0:T(8,128)(2,1)S(1)} %reshape.25), channel_id=1, replica_groups=mesh['y_lo'=2,'z'=8,'y_hi'=4,'x'=8,'core'=2] {'y_hi','x'}, dimensions={0} | all-to-all | bytes 393216 | tf_op jit(solution)/shard_map/all_to_all | solution.py:23
  111.9 0.7 shard_map.134
  112.6 4.0 %all-to-all-start.4 = ((bf16[16,8,512]{2,1,0:T(8,128)(2,1)}), bf16[16,8,512]{2,1,0:T(8,128)(2,1)S(1)}, u32[]{:S(2)}, u32[]{:S(2)}) async-start(bf16[16,8,512]{2,1,0:T(8,128)(2,1)} %shard_map.134), calls=%async_computation.4 | async-start | bytes 262144 | tf_op jit(solution)/shard_map/all_to_all | solution.py:23
  116.7 0.1 copy.20.column_ref
  116.8 0.0 copy-done.9
  116.9 0.1 copy.21.gate_ref
  117.0 8.3 %all-to-all-done.4 = bf16[16,8,512]{2,1,0:T(8,128)(2,1)S(1)} async-done(((bf16[16,8,512]{2,1,0:T(8,128)(2,1)}), bf16[16,8,512]{2,1,0:T(8,128)(2,1)S(1)}, u32[]{:S(2)}, u32[]{:S(2)}) %all-to-all-start.4) | async-done | bytes 131104 | tf_op jit(solution)/shard_map/all_to_all | solution.py:23
  125.2 0.0 copy-done.1
  125.2 3.4 %shard_map.135 = (bf16[128,4096]{1,0:T(8,128)(2,1)}, bf16[128,512]{1,0:T(8,128)(2,1)}) custom-call(bf16[128,4096]{1,0:T(8,128)(2,1)S(1)} %copy-done, bf16[128,512]{1,0:T(8,128)(2,1)S(1)} %bitcast.26, s32[128,1]{1,0:T(8,128)S(1)} %copy.20.column_ref, f32[128,1]{1,0:T(8,128)S(1)} %copy.21.gate_ref, f32[1,4096]{1,0:T(1,128)S(1)} %bitcast.27, ...), custom_call_target="tpu_custom_call" | custom-call | flops 536870912 | bytes 8388608 | tf_op jit(solution)/shard_map/pallas_call | solution.py:185
  (12 shorter events, 0.1 us)
Async XLA Ops:
  7.2 47.1 %copy-start.3 = (bf16[64,512]{1,0:T(8,128)(2,1)S(1)}, bf16[64,512]{1,0:T(8,128)(2,1)}, u32[]{:S(2)}) copy-start(bf16[64,512]{1,0:T(8,128)(2,1)} %param.23) | copy-start | bytes 196612
  7.2 74.8 %copy-start.2 = (bf16[256,512]{1,0:T(8,128)(2,1)S(1)}, bf16[256,512]{1,0:T(8,128)(2,1)}, u32[]{:S(2)}) copy-start(bf16[256,512]{1,0:T(8,128)(2,1)} %param.21) | copy-start | bytes 786436
  9.0 29.3 %all-to-all-start = ((bf16[32,6,512]{2,1,0:T(8,128)(2,1)}), bf16[32,6,512]{2,1,0:T(8,128)(2,1)S(1)}, u32[]{:S(2)}, u32[]{:S(2)}) async-start(bf16[32,6,512]{2,1,0:T(8,128)(2,1)} %shard_map.131), calls=%async_computation | async-start | bytes 524288 | tf_op jit(solution)/shard_map/all_to_all | solution.py:23
  25.7 12.8 %collective-permute-start = (bf16[512,256]{1,0:T(8,128)(2,1)}, bf16[512,256]{1,0:T(8,128)(2,1)S(1)}, u32[]{:S(2)}, u32[]{:S(2)}) collective-permute-start(bf16[512,256]{1,0:T(8,128)(2,1)} %param.19), channel_id=1, source_target_pairs={{0,1},{1,0},{2,3},{3,2},{4,5},{5,4},{6,7},{7,6},{8,9},{9,8},{10,11... | collective-permute-start | bytes 786440 | tf_op jit(solution)/shard_map/ppermute | solution.py:27
  27.7 10.9 %collective-permute-start.1 = (bf16[512,256]{1,0:T(8,128)(2,1)}, bf16[512,256]{1,0:T(8,128)(2,1)S(1)}, u32[]{:S(2)}, u32[]{:S(2)}) collective-permute-start(bf16[512,256]{1,0:T(8,128)(2,1)} %param.20), channel_id=1, source_target_pairs={{0,1},{1,0},{2,3},{3,2},{4,5},{5,4},{6,7},{7,6},{8,9},{9,8},{10,11... | collective-permute-start | bytes 786440 | tf_op jit(solution)/shard_map/ppermute | solution.py:27
  38.4 78.3 %copy-start.4 = (s32[128]{0:T(128)S(1)}, s32[128]{0:T(128)}, u32[]{:S(2)}) copy-start(s32[128]{0:T(128)} %param.14) | copy-start | bytes 1540
  38.4 78.3 %copy-start.5 = (s32[128]{0:T(128)S(1)}, s32[128]{0:T(128)}, u32[]{:S(2)}) copy-start(s32[128]{0:T(128)} %param.13) | copy-start | bytes 1540
  38.4 78.3 %copy-start.6 = (s32[128]{0:T(128)S(1)}, s32[128]{0:T(128)}, u32[]{:S(2)}) copy-start(s32[128]{0:T(128)} %param.15) | copy-start | bytes 1540
  38.4 78.2 %copy-start.7 = (s32[128]{0:T(128)S(1)}, s32[128]{0:T(128)}, u32[]{:S(2)}) copy-start(s32[128]{0:T(128)} %param.16) | copy-start | bytes 1540
  38.5 78.4 %copy-start.8 = (f32[128]{0:T(128)S(1)}, f32[128]{0:T(128)}, u32[]{:S(2)}) copy-start(f32[128]{0:T(128)} %param.17) | copy-start | bytes 1540
  38.5 78.4 %copy-start.9 = (f32[128]{0:T(128)S(1)}, f32[128]{0:T(128)}, u32[]{:S(2)}) copy-start(f32[128]{0:T(128)} %param.18) | copy-start | bytes 1540
  38.5 86.8 %copy-start = (bf16[128,4096]{1,0:T(8,128)(2,1)S(1)}, bf16[128,4096]{1,0:T(8,128)(2,1)}, u32[]{:S(2)}) copy-start(bf16[128,4096]{1,0:T(8,128)(2,1)} %tokens_ref.1) | copy-start | bytes 3145732
  38.5 86.7 %copy-start.1 = (f32[4096]{0:T(1024)S(1)}, f32[4096]{0:T(1024)}, u32[]{:S(2)}) copy-start(f32[4096]{0:T(1024)} %param.22) | copy-start | bytes 49156
  39.7 27.9 %all-to-all-start.1 = ((bf16[8,24,1024]{2,1,0:T(8,128)(2,1)}), bf16[8,24,1024]{2,1,0:T(8,128)(2,1)S(1)}, u32[]{:S(2)}, u32[]{:S(2)}) async-start(bf16[8,24,1024]{2,1,0:T(8,128)(2,1)} %bitcast.4), calls=%async_computation.1 | async-start | bytes 786432 | tf_op jit(solution)/shard_map/all_to_all | solution.py:23
  54.2 71.0 %all-gather.2.cloned.1.call-start = ((), (), s32[]{:S(2)}) async-start(), calls=%async_computation.5 | async-start | bytes 4456448 | tf_op jit(solution)/shard_map/all_gather | solution.py:265
  54.3 10.8 %collective-permute-start.2 = (bf16[64,512]{1,0:T(8,128)(2,1)S(1)}, bf16[64,512]{1,0:T(8,128)(2,1)S(1)}, u32[]{:S(2)}, u32[]{:S(2)}) collective-permute-start(bf16[64,512]{1,0:T(8,128)(2,1)S(1)} %copy-done.3), channel_id=1, source_target_pairs={{0,32},{16,48},{32,0},{48,16},{1,33},{17,49},{33,1},{49,17},{2,34}... | collective-permute-start | bytes 196616 | tf_op jit(solution)/shard_map/ppermute | solution.py:31
  65.1 8.9 %collective-permute-start.3 = (bf16[2,64,512]{2,1,0:T(8,128)(2,1)S(1)}, bf16[2,64,512]{2,1,0:T(8,128)(2,1)S(1)}, u32[]{:S(2)}, u32[]{:S(2)}) collective-permute-start(bf16[2,64,512]{2,1,0:T(8,128)(2,1)S(1)} %pad_maximum_fusion.2), channel_id=1, source_target_pairs={{0,16},{16,0},{32,48},{48,32},{1,17},{17,1},{33,49},{49,33},{2,18}... | collective-permute-start | bytes 393224 | tf_op jit(solution)/shard_map/ppermute | solution.py:31
  74.8 17.0 %all-to-all-start.2 = ((bf16[8,24,512]{2,1,0:T(8,128)(2,1)}), bf16[8,24,512]{2,1,0:T(8,128)(2,1)S(1)}, u32[]{:S(2)}, u32[]{:S(2)}) async-start(bf16[8,24,512]{2,1,0:T(8,128)(2,1)} %shard_map.133), calls=%async_computation.2 | async-start | bytes 393216 | tf_op jit(solution)/shard_map/all_to_all | solution.py:23
  82.0 10.0 %collective-permute-start.4 = (bf16[256,512]{1,0:T(8,128)(2,1)S(1)}, bf16[256,512]{1,0:T(8,128)(2,1)S(1)}, u32[]{:S(2)}, u32[]{:S(2)}) collective-permute-start(bf16[256,512]{1,0:T(8,128)(2,1)S(1)} %copy-done.2), channel_id=1, source_target_pairs={{0,1},{1,0},{2,3},{3,2},{4,5},{5,4},{6,7},{7,6},{8,9},{9,8},{10,11... | collective-permute-start | bytes 786440 | tf_op jit(solution)/shard_map/ppermute | solution.py:27
  112.6 12.6 %all-to-all-start.4 = ((bf16[16,8,512]{2,1,0:T(8,128)(2,1)}), bf16[16,8,512]{2,1,0:T(8,128)(2,1)S(1)}, u32[]{:S(2)}, u32[]{:S(2)}) async-start(bf16[16,8,512]{2,1,0:T(8,128)(2,1)} %shard_map.134), calls=%async_computation.4 | async-start | bytes 262144 | tf_op jit(solution)/shard_map/all_to_all | solution.py:23
Sparse Core Ops, SparseCore 0:
  74.9 44.6 all-gather.1

commit v12 on v10

--- a/solution.py
+++ b/solution.py
@@ -248,7 +248,7 @@
     rows = exchange(slot_copies, CHIPS).reshape(chips * SLOTS, block_width)
     w_gate_other = other_core(w_gate)
     w_up_other = other_core(w_up)
-    w_query_beside = across(w_query, 2)
+    w_query_beside = across(w_query, 1)
 
     w_own = jnp.concatenate([w_gate, w_up], axis=1)
     partial = small_call(
@@ -257,11 +257,11 @@
     share = chips * SLOTS // blocks
     partial, w_query, w_query_beside = tie(partial, w_query, w_query_beside)
     summed = exchange(partial.reshape(blocks, share, 4 * units), "z")
-    query_rows = in_order(w_query, w_query_beside, 2, 0)
-    query_rows_other = across(query_rows, 1)
+    query_rows = in_order(w_query, w_query_beside, 1, 0)
+    query_rows_other = across(query_rows, 2)
     hidden_copies = small_call(hidden_kernel, (blocks, share, 2 * units), 1, summed)
     hidden_copies, query_rows_other = tie(hidden_copies, query_rows_other)
-    query_rows = in_order(query_rows, query_rows_other, 1, 1).reshape((-1,) + w_query.shape)
+    query_rows = in_order(query_rows, query_rows_other, 2, 0).reshape((-1,) + w_query.shape)
     w_query_full = lax.all_gather(query_rows, ("x", "core"), axis=0)
     w_query_full = w_query_full.reshape((-1, 2) + query_rows.shape)
     hidden = exchange(hidden_copies, "z").reshape(chips * SLOTS, 2 * units)

time: 134 us -> 134 us (level)
  waiting for transfers between devices: 25 us -> 27.4 us
  blocking collectives: 27.4 us -> 25.4 us
    ppermute x2, starting transfers between devices: 12.2 us -> 9.01 us  [across(): lax.ppermute(block, 'y_hi', [(i, i ^ bit) for i in range(lax.axis_size('y...]
    all_to_all x4, waiting for transfers between devices: 24.5 us -> 27.4 us  [exchange(): return lax.all_to_all(blocks, axes, split_axis=0, concat_axis=0, tiled=True)]
    all_to_all x4, starting transfers between devices: 37.6 us -> 40.1 us  [exchange(): return lax.all_to_all(blocks, axes, split_axis=0, concat_axis=0, tiled=True)]
    all_to_all x1, blocking collectives: 27.4 us -> 25.4 us  [exchange(): return lax.all_to_all(blocks, axes, split_axis=0, concat_axis=0, tiled=True)]
where the time goes in v12:
time: 134 us; the launch traced here: 133 us
  starting transfers between devices  55.4 us (41%)
  waiting for transfers between devices  27.4 us (20%)
  blocking collectives  25.4 us (19%)
  between operations  14.3 us (11%)
  Pallas kernels  7.81 us (6%)
  other arithmetic  1.86 us (1%)
    all_to_all x4, starting transfers between devices, exchange(): return lax.all_to_all(blocks, axes, split_axis=0, concat_axis=0, tiled=True)  40.1 us
    all_to_all x4, waiting for transfers between devices, exchange(): return lax.all_to_all(blocks, axes, split_axis=0, concat_axis=0, tiled=True)  27.4 us
    all_to_all x1, blocking collectives, exchange(): return lax.all_to_all(blocks, axes, split_axis=0, concat_axis=0, tiled=True)  25.4 us
    ppermute x2, starting transfers between devices, across(): lax.ppermute(block, 'y_hi', [(i, i ^ bit) for i in range(lax.axis_size('y...  9.01 us
    ppermute x3, starting transfers between devices, other_core(): return lax.ppermute(block, 'core', [(0, 1), (1, 0)])  6.25 us
    pallas_call x4, Pallas kernels, small_call(): pl.pallas_call(kernel, out_shape=jax.ShapeDtypeStruct(shape, jnp.bfloat16...  4.44 us
    pallas_call x1, Pallas kernels, finish(): pl.pallas_call(finish_kernel, out_shape=(jax.ShapeDtypeStruct((tok_count,...  3.37 us
  transfers between devices with their start and end apart: 10, of which 4 were waited for; matrix products, arithmetic and copies ran while one was open for 1% of the time, Pallas kernels for 2%

profile of v12, /device:TPU:4, one launch (start us, length us, event | category | flops | bytes accessed | tf_op | source)
XLA Modules:
  0.0 133.1 jit_solution(654976539592613057)
XLA Ops:
  7.2 0.0 copy-start.3
  7.2 0.0 copy-start.2
  7.2 1.8 %shard_map.131 = bf16[32,6,512]{2,1,0:T(8,128)(2,1)} custom-call(bf16[128,4096]{1,0:T(8,128)(2,1)} %tokens_ref.1, s32[1,128]{1,0:T(1,128)} %bitcast.31, s32[1,128]{1,0:T(1,128)} %bitcast.30, s32[1,128]{1,0:T(1,128)} %bitcast.32, s32[1,128]{1,0:T(1,128)} %bitcast.33), custom_call_target="tpu_custom_call" | custom-call | flops 196608 | bytes 393216 | tf_op jit(solution)/shard_map/pallas_call | solution.py:49
  9.0 16.7 %all-to-all-start = ((bf16[32,6,512]{2,1,0:T(8,128)(2,1)}), bf16[32,6,512]{2,1,0:T(8,128)(2,1)S(1)}, u32[]{:S(2)}, u32[]{:S(2)}) async-start(bf16[32,6,512]{2,1,0:T(8,128)(2,1)} %shard_map.131), calls=%async_computation | async-start | bytes 524288 | tf_op jit(solution)/shard_map/all_to_all | solution.py:23
  25.7 1.9 %collective-permute-start = (bf16[512,256]{1,0:T(8,128)(2,1)}, bf16[512,256]{1,0:T(8,128)(2,1)S(1)}, u32[]{:S(2)}, u32[]{:S(2)}) collective-permute-start(bf16[512,256]{1,0:T(8,128)(2,1)} %param.19), channel_id=1, source_target_pairs={{0,1},{1,0},{2,3},{3,2},{4,5},{5,4},{6,7},{7,6},{8,9},{9,8},{10,11... | collective-permute-start | bytes 786440 | tf_op jit(solution)/shard_map/ppermute | solution.py:27
  27.7 2.4 %collective-permute-start.1 = (bf16[512,256]{1,0:T(8,128)(2,1)}, bf16[512,256]{1,0:T(8,128)(2,1)S(1)}, u32[]{:S(2)}, u32[]{:S(2)}) collective-permute-start(bf16[512,256]{1,0:T(8,128)(2,1)} %param.20), channel_id=1, source_target_pairs={{0,1},{1,0},{2,3},{3,2},{4,5},{5,4},{6,7},{7,6},{8,9},{9,8},{10,11... | collective-permute-start | bytes 786440 | tf_op jit(solution)/shard_map/ppermute | solution.py:27
  30.1 4.3 %collective-permute-start.2 = (bf16[64,512]{1,0:T(8,128)(2,1)}, bf16[64,512]{1,0:T(8,128)(2,1)S(1)}, u32[]{:S(2)}, u32[]{:S(2)}) collective-permute-start(bf16[64,512]{1,0:T(8,128)(2,1)} %param.23), channel_id=1, source_target_pairs={{0,16},{16,0},{32,48},{48,32},{1,17},{17,1},{33,49},{49,33},{2,18}... | collective-permute-start | bytes 196616 | tf_op jit(solution)/shard_map/ppermute | solution.py:31
  34.4 1.1 pad_maximum_fusion.own_ref
  35.5 2.8 %all-to-all-done = bf16[32,6,512]{2,1,0:T(8,128)(2,1)S(1)} async-done(((bf16[32,6,512]{2,1,0:T(8,128)(2,1)}), bf16[32,6,512]{2,1,0:T(8,128)(2,1)S(1)}, u32[]{:S(2)}, u32[]{:S(2)}) %all-to-all-start) | async-done | bytes 196640 | tf_op jit(solution)/shard_map/all_to_all | solution.py:23
  38.3 0.1 reshape.22.rows_ref
  38.4 0.0 copy-start.4
  38.4 0.0 copy-start.5
  38.4 0.0 copy-start.6
  38.4 0.0 copy-start.7
  38.5 0.0 copy-start.8
  38.5 0.0 copy-start.9
  38.5 0.0 copy-start
  38.5 0.0 copy-start.1
  38.5 0.0 collective-permute-done.gate_other_ref
  38.5 0.0 collective-permute-done.1.up_other_ref
  38.5 1.1 shard_map.132
  39.7 0.0 collective-permute-done.2
  39.7 14.6 %all-to-all-start.1 = ((bf16[8,24,1024]{2,1,0:T(8,128)(2,1)}), bf16[8,24,1024]{2,1,0:T(8,128)(2,1)S(1)}, u32[]{:S(2)}, u32[]{:S(2)}) async-start(bf16[8,24,1024]{2,1,0:T(8,128)(2,1)} %bitcast.4), calls=%async_computation.1 | async-start | bytes 786432 | tf_op jit(solution)/shard_map/all_to_all | solution.py:23
  54.2 0.0 all-gather.2.cloned.1.call-start
  54.3 0.0 copy-done.3
  54.3 4.7 %collective-permute-start.3 = (bf16[2,64,512]{2,1,0:T(8,128)(2,1)S(1)}, bf16[2,64,512]{2,1,0:T(8,128)(2,1)S(1)}, u32[]{:S(2)}, u32[]{:S(2)}) collective-permute-start(bf16[2,64,512]{2,1,0:T(8,128)(2,1)S(1)} %pad_maximum_fusion.2), channel_id=1, source_target_pairs={{0,32},{16,48},{32,0},{48,16},{1,33},{17,49},{33,1},{49,17},{2,34}... | collective-permute-start | bytes 393224 | tf_op jit(solution)/shard_map/ppermute | solution.py:31
  59.0 8.5 %all-to-all-done.1.parts_ref = bf16[8,24,1024]{2,1,0:T(8,128)(2,1)S(1)} async-done(((bf16[8,24,1024]{2,1,0:T(8,128)(2,1)}), bf16[8,24,1024]{2,1,0:T(8,128)(2,1)S(1)}, u32[]{:S(2)}, u32[]{:S(2)}) %all-to-all-start.1) | async-done | bytes 393248 | tf_op jit(solution)/shard_map/all_to_all | solution.py:23
  67.6 0.8 shard_map.133
  68.3 0.0 collective-permute-done.3
  68.4 0.7 pad_maximum_fusion.1
  69.1 0.0 all-gather.2.cloned.1.call-update
  69.1 5.3 %all-to-all-start.2 = ((bf16[8,24,512]{2,1,0:T(8,128)(2,1)}), bf16[8,24,512]{2,1,0:T(8,128)(2,1)S(1)}, u32[]{:S(2)}, u32[]{:S(2)}) async-start(bf16[8,24,512]{2,1,0:T(8,128)(2,1)} %shard_map.133), calls=%async_computation.2 | async-start | bytes 393216 | tf_op jit(solution)/shard_map/all_to_all | solution.py:23
  74.5 0.0 copy-done.2
  74.5 1.9 %collective-permute-start.4 = (bf16[256,512]{1,0:T(8,128)(2,1)S(1)}, bf16[256,512]{1,0:T(8,128)(2,1)S(1)}, u32[]{:S(2)}, u32[]{:S(2)}) collective-permute-start(bf16[256,512]{1,0:T(8,128)(2,1)S(1)} %copy-done.2), channel_id=1, source_target_pairs={{0,1},{1,0},{2,3},{3,2},{4,5},{5,4},{6,7},{7,6},{8,9},{9,8},{10,11... | collective-permute-start | bytes 786440 | tf_op jit(solution)/shard_map/ppermute | solution.py:27
  76.4 7.8 %all-to-all-done.2 = bf16[8,24,512]{2,1,0:T(8,128)(2,1)S(1)} async-done(((bf16[8,24,512]{2,1,0:T(8,128)(2,1)}), bf16[8,24,512]{2,1,0:T(8,128)(2,1)S(1)}, u32[]{:S(2)}, u32[]{:S(2)}) %all-to-all-start.2) | async-done | bytes 196640 | tf_op jit(solution)/shard_map/all_to_all | solution.py:23
  84.2 0.2 fusion.2
  84.4 0.0 collective-permute-done.4
  84.4 0.2 fusion
  84.7 0.1 reshape.25
  84.7 25.4 %all_to_all.25.parts_ref = bf16[32,6,512]{2,1,0:T(8,128)(2,1)S(1)} all-to-all(bf16[32,6,512]{2,1,0:T(8,128)(2,1)S(1)} %reshape.25), channel_id=1, replica_groups=mesh['y_lo'=2,'z'=8,'y_hi'=4,'x'=8,'core'=2] {'y_hi','x'}, dimensions={0} | all-to-all | bytes 393216 | tf_op jit(solution)/shard_map/all_to_all | solution.py:23
  110.1 0.7 shard_map.134
  110.8 3.5 %all-to-all-start.4 = ((bf16[16,8,512]{2,1,0:T(8,128)(2,1)}), bf16[16,8,512]{2,1,0:T(8,128)(2,1)S(1)}, u32[]{:S(2)}, u32[]{:S(2)}) async-start(bf16[16,8,512]{2,1,0:T(8,128)(2,1)} %shard_map.134), calls=%async_computation.4 | async-start | bytes 262144 | tf_op jit(solution)/shard_map/all_to_all | solution.py:23
  114.3 0.0 copy-done.4
  114.4 0.1 copy.18.column_ref
  114.5 0.0 copy-done.8
  114.5 0.1 copy.19.gate_ref
  114.6 8.2 %all-to-all-done.4 = bf16[16,8,512]{2,1,0:T(8,128)(2,1)S(1)} async-done(((bf16[16,8,512]{2,1,0:T(8,128)(2,1)}), bf16[16,8,512]{2,1,0:T(8,128)(2,1)S(1)}, u32[]{:S(2)}, u32[]{:S(2)}) %all-to-all-start.4) | async-done | bytes 131104 | tf_op jit(solution)/shard_map/all_to_all | solution.py:23
  122.9 3.4 %shard_map.135 = (bf16[128,4096]{1,0:T(8,128)(2,1)}, bf16[128,512]{1,0:T(8,128)(2,1)}) custom-call(bf16[128,4096]{1,0:T(8,128)(2,1)S(1)} %copy-done, bf16[128,512]{1,0:T(8,128)(2,1)S(1)} %bitcast.24, s32[128,1]{1,0:T(8,128)S(1)} %copy.18.column_ref, f32[128,1]{1,0:T(8,128)S(1)} %copy.19.gate_ref, f32[1,4096]{1,0:T(1,128)S(1)} %bitcast.25, ...), custom_call_target="tpu_custom_call" | custom-call | flops 536870912 | bytes 8388608 | tf_op jit(solution)/shard_map/pallas_call | solution.py:185
  (12 shorter events, 0.1 us)
Async XLA Ops:
  7.2 47.1 %copy-start.3 = (bf16[64,512]{1,0:T(8,128)(2,1)S(1)}, bf16[64,512]{1,0:T(8,128)(2,1)}, u32[]{:S(2)}) copy-start(bf16[64,512]{1,0:T(8,128)(2,1)} %param.23) | copy-start | bytes 196612
  7.2 67.3 %copy-start.2 = (bf16[256,512]{1,0:T(8,128)(2,1)S(1)}, bf16[256,512]{1,0:T(8,128)(2,1)}, u32[]{:S(2)}) copy-start(bf16[256,512]{1,0:T(8,128)(2,1)} %param.21) | copy-start | bytes 786436
  9.0 29.3 %all-to-all-start = ((bf16[32,6,512]{2,1,0:T(8,128)(2,1)}), bf16[32,6,512]{2,1,0:T(8,128)(2,1)S(1)}, u32[]{:S(2)}, u32[]{:S(2)}) async-start(bf16[32,6,512]{2,1,0:T(8,128)(2,1)} %shard_map.131), calls=%async_computation | async-start | bytes 524288 | tf_op jit(solution)/shard_map/all_to_all | solution.py:23
  25.7 12.8 %collective-permute-start = (bf16[512,256]{1,0:T(8,128)(2,1)}, bf16[512,256]{1,0:T(8,128)(2,1)S(1)}, u32[]{:S(2)}, u32[]{:S(2)}) collective-permute-start(bf16[512,256]{1,0:T(8,128)(2,1)} %param.19), channel_id=1, source_target_pairs={{0,1},{1,0},{2,3},{3,2},{4,5},{5,4},{6,7},{7,6},{8,9},{9,8},{10,11... | collective-permute-start | bytes 786440 | tf_op jit(solution)/shard_map/ppermute | solution.py:27
  27.7 10.9 %collective-permute-start.1 = (bf16[512,256]{1,0:T(8,128)(2,1)}, bf16[512,256]{1,0:T(8,128)(2,1)S(1)}, u32[]{:S(2)}, u32[]{:S(2)}) collective-permute-start(bf16[512,256]{1,0:T(8,128)(2,1)} %param.20), channel_id=1, source_target_pairs={{0,1},{1,0},{2,3},{3,2},{4,5},{5,4},{6,7},{7,6},{8,9},{9,8},{10,11... | collective-permute-start | bytes 786440 | tf_op jit(solution)/shard_map/ppermute | solution.py:27
  30.1 9.6 %collective-permute-start.2 = (bf16[64,512]{1,0:T(8,128)(2,1)}, bf16[64,512]{1,0:T(8,128)(2,1)S(1)}, u32[]{:S(2)}, u32[]{:S(2)}) collective-permute-start(bf16[64,512]{1,0:T(8,128)(2,1)} %param.23), channel_id=1, source_target_pairs={{0,16},{16,0},{32,48},{48,32},{1,17},{17,1},{33,49},{49,33},{2,18}... | collective-permute-start | bytes 196616 | tf_op jit(solution)/shard_map/ppermute | solution.py:31
  38.4 75.9 %copy-start.4 = (s32[128]{0:T(128)S(1)}, s32[128]{0:T(128)}, u32[]{:S(2)}) copy-start(s32[128]{0:T(128)} %param.14) | copy-start | bytes 1540
  38.4 75.9 %copy-start.5 = (s32[128]{0:T(128)S(1)}, s32[128]{0:T(128)}, u32[]{:S(2)}) copy-start(s32[128]{0:T(128)} %param.13) | copy-start | bytes 1540
  38.4 75.9 %copy-start.6 = (s32[128]{0:T(128)S(1)}, s32[128]{0:T(128)}, u32[]{:S(2)}) copy-start(s32[128]{0:T(128)} %param.15) | copy-start | bytes 1540
  38.4 75.9 %copy-start.7 = (s32[128]{0:T(128)S(1)}, s32[128]{0:T(128)}, u32[]{:S(2)}) copy-start(s32[128]{0:T(128)} %param.16) | copy-start | bytes 1540
  38.5 76.1 %copy-start.8 = (f32[128]{0:T(128)S(1)}, f32[128]{0:T(128)}, u32[]{:S(2)}) copy-start(f32[128]{0:T(128)} %param.17) | copy-start | bytes 1540
  38.5 76.0 %copy-start.9 = (f32[128]{0:T(128)S(1)}, f32[128]{0:T(128)}, u32[]{:S(2)}) copy-start(f32[128]{0:T(128)} %param.18) | copy-start | bytes 1540
  38.5 84.4 %copy-start = (bf16[128,4096]{1,0:T(8,128)(2,1)S(1)}, bf16[128,4096]{1,0:T(8,128)(2,1)}, u32[]{:S(2)}) copy-start(bf16[128,4096]{1,0:T(8,128)(2,1)} %tokens_ref.1) | copy-start | bytes 3145732
  38.5 84.4 %copy-start.1 = (f32[4096]{0:T(1024)S(1)}, f32[4096]{0:T(1024)}, u32[]{:S(2)}) copy-start(f32[4096]{0:T(1024)} %param.22) | copy-start | bytes 49156
  39.7 27.9 %all-to-all-start.1 = ((bf16[8,24,1024]{2,1,0:T(8,128)(2,1)}), bf16[8,24,1024]{2,1,0:T(8,128)(2,1)S(1)}, u32[]{:S(2)}, u32[]{:S(2)}) async-start(bf16[8,24,1024]{2,1,0:T(8,128)(2,1)} %bitcast.4), calls=%async_computation.1 | async-start | bytes 786432 | tf_op jit(solution)/shard_map/all_to_all | solution.py:23
  54.2 68.6 %all-gather.2.cloned.1.call-start = ((), (), s32[]{:S(2)}) async-start(), calls=%async_computation.5 | async-start | bytes 4456448 | tf_op jit(solution)/shard_map/all_gather | solution.py:265
  54.3 14.0 %collective-permute-start.3 = (bf16[2,64,512]{2,1,0:T(8,128)(2,1)S(1)}, bf16[2,64,512]{2,1,0:T(8,128)(2,1)S(1)}, u32[]{:S(2)}, u32[]{:S(2)}) collective-permute-start(bf16[2,64,512]{2,1,0:T(8,128)(2,1)S(1)} %pad_maximum_fusion.2), channel_id=1, source_target_pairs={{0,32},{16,48},{32,0},{48,16},{1,33},{17,49},{33,1},{49,17},{2,34}... | collective-permute-start | bytes 393224 | tf_op jit(solution)/shard_map/ppermute | solution.py:31
  69.1 15.1 %all-to-all-start.2 = ((bf16[8,24,512]{2,1,0:T(8,128)(2,1)}), bf16[8,24,512]{2,1,0:T(8,128)(2,1)S(1)}, u32[]{:S(2)}, u32[]{:S(2)}) async-start(bf16[8,24,512]{2,1,0:T(8,128)(2,1)} %shard_map.133), calls=%async_computation.2 | async-start | bytes 393216 | tf_op jit(solution)/shard_map/all_to_all | solution.py:23
  74.5 10.0 %collective-permute-start.4 = (bf16[256,512]{1,0:T(8,128)(2,1)S(1)}, bf16[256,512]{1,0:T(8,128)(2,1)S(1)}, u32[]{:S(2)}, u32[]{:S(2)}) collective-permute-start(bf16[256,512]{1,0:T(8,128)(2,1)S(1)} %copy-done.2), channel_id=1, source_target_pairs={{0,1},{1,0},{2,3},{3,2},{4,5},{5,4},{6,7},{7,6},{8,9},{9,8},{10,11... | collective-permute-start | bytes 786440 | tf_op jit(solution)/shard_map/ppermute | solution.py:27
  110.8 12.0 %all-to-all-start.4 = ((bf16[16,8,512]{2,1,0:T(8,128)(2,1)}), bf16[16,8,512]{2,1,0:T(8,128)(2,1)S(1)}, u32[]{:S(2)}, u32[]{:S(2)}) async-start(bf16[16,8,512]{2,1,0:T(8,128)(2,1)} %shard_map.134), calls=%async_computation.4 | async-start | bytes 262144 | tf_op jit(solution)/shard_map/all_to_all | solution.py:23
Sparse Core Ops, SparseCore 0:
  69.2 47.1 all-gather.1

commit v13 on v12

--- a/solution.py
+++ b/solution.py
@@ -14,7 +14,7 @@
 SIZES = {"y_lo": 2, "z": 8, "y_hi": 4, "x": 8, "core": 2}
 PADDED = 8
 LANES = 128
-PIECES = 4
+PIECES = 8
 VMEM_BYTES = 60 * 1024 * 1024
 FINISH_BYTES = 50 * 1024 * 1024
 

time: 134 us -> 134 us (level)
  no operation moved by 1% of the time
where the time goes in v13:
time: 134 us; the launch traced here: 133 us
  starting transfers between devices  55.4 us (41%)
  waiting for transfers between devices  27.4 us (20%)
  blocking collectives  25.2 us (19%)
  between operations  14.3 us (11%)
  Pallas kernels  7.83 us (6%)
  other arithmetic  1.86 us (1%)
    all_to_all x4, starting transfers between devices, exchange(): return lax.all_to_all(blocks, axes, split_axis=0, concat_axis=0, tiled=True)  40.1 us
    all_to_all x4, waiting for transfers between devices, exchange(): return lax.all_to_all(blocks, axes, split_axis=0, concat_axis=0, tiled=True)  27.4 us
    all_to_all x1, blocking collectives, exchange(): return lax.all_to_all(blocks, axes, split_axis=0, concat_axis=0, tiled=True)  25.2 us
    ppermute x2, starting transfers between devices, across(): lax.ppermute(block, 'y_hi', [(i, i ^ bit) for i in range(lax.axis_size('y...  9.01 us
    ppermute x3, starting transfers between devices, other_core(): return lax.ppermute(block, 'core', [(0, 1), (1, 0)])  6.25 us
    pallas_call x4, Pallas kernels, small_call(): pl.pallas_call(kernel, out_shape=jax.ShapeDtypeStruct(shape, jnp.bfloat16...  4.46 us
    pallas_call x1, Pallas kernels, finish(): pl.pallas_call(finish_kernel, out_shape=(jax.ShapeDtypeStruct((tok_count,...  3.37 us
  transfers between devices with their start and end apart: 10, of which 4 were waited for; matrix products, arithmetic and copies ran while one was open for 1% of the time, Pallas kernels for 2%

profile of v13, /device:TPU:4, one launch (start us, length us, event | category | flops | bytes accessed | tf_op | source)
XLA Modules:
  0.0 133.0 jit_solution(3071151957607228012)
XLA Ops:
  7.2 0.0 copy-start.3
  7.2 0.0 copy-start.2
  7.2 1.9 %shard_map.131 = bf16[32,6,512]{2,1,0:T(8,128)(2,1)} custom-call(bf16[128,4096]{1,0:T(8,128)(2,1)} %tokens_ref.1, s32[1,128]{1,0:T(1,128)} %bitcast.31, s32[1,128]{1,0:T(1,128)} %bitcast.30, s32[1,128]{1,0:T(1,128)} %bitcast.32, s32[1,128]{1,0:T(1,128)} %bitcast.33), custom_call_target="tpu_custom_call" | custom-call | flops 196608 | bytes 393216 | tf_op jit(solution)/shard_map/pallas_call | solution.py:49
  9.1 16.7 %all-to-all-start = ((bf16[32,6,512]{2,1,0:T(8,128)(2,1)}), bf16[32,6,512]{2,1,0:T(8,128)(2,1)S(1)}, u32[]{:S(2)}, u32[]{:S(2)}) async-start(bf16[32,6,512]{2,1,0:T(8,128)(2,1)} %shard_map.131), calls=%async_computation | async-start | bytes 524288 | tf_op jit(solution)/shard_map/all_to_all | solution.py:23
  25.8 1.9 %collective-permute-start = (bf16[512,256]{1,0:T(8,128)(2,1)}, bf16[512,256]{1,0:T(8,128)(2,1)S(1)}, u32[]{:S(2)}, u32[]{:S(2)}) collective-permute-start(bf16[512,256]{1,0:T(8,128)(2,1)} %param.19), channel_id=1, source_target_pairs={{0,1},{1,0},{2,3},{3,2},{4,5},{5,4},{6,7},{7,6},{8,9},{9,8},{10,11... | collective-permute-start | bytes 786440 | tf_op jit(solution)/shard_map/ppermute | solution.py:27
  27.7 2.4 %collective-permute-start.1 = (bf16[512,256]{1,0:T(8,128)(2,1)}, bf16[512,256]{1,0:T(8,128)(2,1)S(1)}, u32[]{:S(2)}, u32[]{:S(2)}) collective-permute-start(bf16[512,256]{1,0:T(8,128)(2,1)} %param.20), channel_id=1, source_target_pairs={{0,1},{1,0},{2,3},{3,2},{4,5},{5,4},{6,7},{7,6},{8,9},{9,8},{10,11... | collective-permute-start | bytes 786440 | tf_op jit(solution)/shard_map/ppermute | solution.py:27
  30.1 4.3 %collective-permute-start.2 = (bf16[64,512]{1,0:T(8,128)(2,1)}, bf16[64,512]{1,0:T(8,128)(2,1)S(1)}, u32[]{:S(2)}, u32[]{:S(2)}) collective-permute-start(bf16[64,512]{1,0:T(8,128)(2,1)} %param.23), channel_id=1, source_target_pairs={{0,16},{16,0},{32,48},{48,32},{1,17},{17,1},{33,49},{49,33},{2,18}... | collective-permute-start | bytes 196616 | tf_op jit(solution)/shard_map/ppermute | solution.py:31
  34.4 1.1 pad_maximum_fusion.own_ref
  35.5 2.8 %all-to-all-done = bf16[32,6,512]{2,1,0:T(8,128)(2,1)S(1)} async-done(((bf16[32,6,512]{2,1,0:T(8,128)(2,1)}), bf16[32,6,512]{2,1,0:T(8,128)(2,1)S(1)}, u32[]{:S(2)}, u32[]{:S(2)}) %all-to-all-start) | async-done | bytes 196640 | tf_op jit(solution)/shard_map/all_to_all | solution.py:23
  38.4 0.1 reshape.22.rows_ref
  38.4 0.0 copy-start.4
  38.4 0.0 copy-start.5
  38.5 0.0 copy-start.6
  38.5 0.0 copy-start.7
  38.5 0.0 copy-start.8
  38.5 0.0 copy-start.9
  38.5 0.0 copy-start
  38.5 0.0 copy-start.1
  38.5 0.0 collective-permute-done.gate_other_ref
  38.5 0.0 collective-permute-done.1.up_other_ref
  38.5 1.1 shard_map.132
  39.7 0.0 collective-permute-done.2
  39.7 14.6 %all-to-all-start.1 = ((bf16[8,24,1024]{2,1,0:T(8,128)(2,1)}), bf16[8,24,1024]{2,1,0:T(8,128)(2,1)S(1)}, u32[]{:S(2)}, u32[]{:S(2)}) async-start(bf16[8,24,1024]{2,1,0:T(8,128)(2,1)} %bitcast.4), calls=%async_computation.1 | async-start | bytes 786432 | tf_op jit(solution)/shard_map/all_to_all | solution.py:23
  54.3 0.0 all-gather.2.cloned.1.call-start
  54.3 0.0 copy-done.3
  54.4 4.7 %collective-permute-start.3 = (bf16[2,64,512]{2,1,0:T(8,128)(2,1)S(1)}, bf16[2,64,512]{2,1,0:T(8,128)(2,1)S(1)}, u32[]{:S(2)}, u32[]{:S(2)}) collective-permute-start(bf16[2,64,512]{2,1,0:T(8,128)(2,1)S(1)} %pad_maximum_fusion.2), channel_id=1, source_target_pairs={{0,32},{16,48},{32,0},{48,16},{1,33},{17,49},{33,1},{49,17},{2,34}... | collective-permute-start | bytes 393224 | tf_op jit(solution)/shard_map/ppermute | solution.py:31
  59.1 8.5 %all-to-all-done.1.parts_ref = bf16[8,24,1024]{2,1,0:T(8,128)(2,1)S(1)} async-done(((bf16[8,24,1024]{2,1,0:T(8,128)(2,1)}), bf16[8,24,1024]{2,1,0:T(8,128)(2,1)S(1)}, u32[]{:S(2)}, u32[]{:S(2)}) %all-to-all-start.1) | async-done | bytes 393248 | tf_op jit(solution)/shard_map/all_to_all | solution.py:23
  67.6 0.8 shard_map.133
  68.3 0.0 collective-permute-done.3
  68.4 0.7 pad_maximum_fusion.1
  69.1 0.0 all-gather.2.cloned.1.call-update
  69.1 5.3 %all-to-all-start.2 = ((bf16[8,24,512]{2,1,0:T(8,128)(2,1)}), bf16[8,24,512]{2,1,0:T(8,128)(2,1)S(1)}, u32[]{:S(2)}, u32[]{:S(2)}) async-start(bf16[8,24,512]{2,1,0:T(8,128)(2,1)} %shard_map.133), calls=%async_computation.2 | async-start | bytes 393216 | tf_op jit(solution)/shard_map/all_to_all | solution.py:23
  74.5 0.0 copy-done.2
  74.5 1.9 %collective-permute-start.4 = (bf16[256,512]{1,0:T(8,128)(2,1)S(1)}, bf16[256,512]{1,0:T(8,128)(2,1)S(1)}, u32[]{:S(2)}, u32[]{:S(2)}) collective-permute-start(bf16[256,512]{1,0:T(8,128)(2,1)S(1)} %copy-done.2), channel_id=1, source_target_pairs={{0,1},{1,0},{2,3},{3,2},{4,5},{5,4},{6,7},{7,6},{8,9},{9,8},{10,11... | collective-permute-start | bytes 786440 | tf_op jit(solution)/shard_map/ppermute | solution.py:27
  76.4 7.8 %all-to-all-done.2 = bf16[8,24,512]{2,1,0:T(8,128)(2,1)S(1)} async-done(((bf16[8,24,512]{2,1,0:T(8,128)(2,1)}), bf16[8,24,512]{2,1,0:T(8,128)(2,1)S(1)}, u32[]{:S(2)}, u32[]{:S(2)}) %all-to-all-start.2) | async-done | bytes 196640 | tf_op jit(solution)/shard_map/all_to_all | solution.py:23
  84.3 0.2 fusion.2
  84.5 0.0 collective-permute-done.4
  84.5 0.2 fusion
  84.7 0.1 reshape.25
  84.8 25.2 %all_to_all.25.parts_ref = bf16[32,6,512]{2,1,0:T(8,128)(2,1)S(1)} all-to-all(bf16[32,6,512]{2,1,0:T(8,128)(2,1)S(1)} %reshape.25), channel_id=1, replica_groups=mesh['y_lo'=2,'z'=8,'y_hi'=4,'x'=8,'core'=2] {'y_hi','x'}, dimensions={0} | all-to-all | bytes 393216 | tf_op jit(solution)/shard_map/all_to_all | solution.py:23
  110.0 0.7 shard_map.134
  110.7 3.5 %all-to-all-start.4 = ((bf16[16,8,512]{2,1,0:T(8,128)(2,1)}), bf16[16,8,512]{2,1,0:T(8,128)(2,1)S(1)}, u32[]{:S(2)}, u32[]{:S(2)}) async-start(bf16[16,8,512]{2,1,0:T(8,128)(2,1)} %shard_map.134), calls=%async_computation.4 | async-start | bytes 262144 | tf_op jit(solution)/shard_map/all_to_all | solution.py:23
  114.2 0.0 copy-done.4
  114.3 0.1 copy.18.column_ref
  114.4 0.0 copy-done.8
  114.4 0.1 copy.19.gate_ref
  114.5 8.2 %all-to-all-done.4 = bf16[16,8,512]{2,1,0:T(8,128)(2,1)S(1)} async-done(((bf16[16,8,512]{2,1,0:T(8,128)(2,1)}), bf16[16,8,512]{2,1,0:T(8,128)(2,1)S(1)}, u32[]{:S(2)}, u32[]{:S(2)}) %all-to-all-start.4) | async-done | bytes 131104 | tf_op jit(solution)/shard_map/all_to_all | solution.py:23
  122.8 3.4 %shard_map.135 = (bf16[128,4096]{1,0:T(8,128)(2,1)}, bf16[128,512]{1,0:T(8,128)(2,1)}) custom-call(bf16[128,4096]{1,0:T(8,128)(2,1)S(1)} %copy-done, bf16[128,512]{1,0:T(8,128)(2,1)S(1)} %bitcast.24, s32[128,1]{1,0:T(8,128)S(1)} %copy.18.column_ref, f32[128,1]{1,0:T(8,128)S(1)} %copy.19.gate_ref, f32[1,4096]{1,0:T(1,128)S(1)} %bitcast.25, ...), custom_call_target="tpu_custom_call" | custom-call | flops 536870912 | bytes 8388608 | tf_op jit(solution)/shard_map/pallas_call | solution.py:185
  (12 shorter events, 0.1 us)
Async XLA Ops:
  7.2 47.1 %copy-start.3 = (bf16[64,512]{1,0:T(8,128)(2,1)S(1)}, bf16[64,512]{1,0:T(8,128)(2,1)}, u32[]{:S(2)}) copy-start(bf16[64,512]{1,0:T(8,128)(2,1)} %param.23) | copy-start | bytes 196612
  7.2 67.3 %copy-start.2 = (bf16[256,512]{1,0:T(8,128)(2,1)S(1)}, bf16[256,512]{1,0:T(8,128)(2,1)}, u32[]{:S(2)}) copy-start(bf16[256,512]{1,0:T(8,128)(2,1)} %param.21) | copy-start | bytes 786436
  9.1 29.3 %all-to-all-start = ((bf16[32,6,512]{2,1,0:T(8,128)(2,1)}), bf16[32,6,512]{2,1,0:T(8,128)(2,1)S(1)}, u32[]{:S(2)}, u32[]{:S(2)}) async-start(bf16[32,6,512]{2,1,0:T(8,128)(2,1)} %shard_map.131), calls=%async_computation | async-start | bytes 524288 | tf_op jit(solution)/shard_map/all_to_all | solution.py:23
  25.8 12.8 %collective-permute-start = (bf16[512,256]{1,0:T(8,128)(2,1)}, bf16[512,256]{1,0:T(8,128)(2,1)S(1)}, u32[]{:S(2)}, u32[]{:S(2)}) collective-permute-start(bf16[512,256]{1,0:T(8,128)(2,1)} %param.19), channel_id=1, source_target_pairs={{0,1},{1,0},{2,3},{3,2},{4,5},{5,4},{6,7},{7,6},{8,9},{9,8},{10,11... | collective-permute-start | bytes 786440 | tf_op jit(solution)/shard_map/ppermute | solution.py:27
  27.7 10.9 %collective-permute-start.1 = (bf16[512,256]{1,0:T(8,128)(2,1)}, bf16[512,256]{1,0:T(8,128)(2,1)S(1)}, u32[]{:S(2)}, u32[]{:S(2)}) collective-permute-start(bf16[512,256]{1,0:T(8,128)(2,1)} %param.20), channel_id=1, source_target_pairs={{0,1},{1,0},{2,3},{3,2},{4,5},{5,4},{6,7},{7,6},{8,9},{9,8},{10,11... | collective-permute-start | bytes 786440 | tf_op jit(solution)/shard_map/ppermute | solution.py:27
  30.1 9.6 %collective-permute-start.2 = (bf16[64,512]{1,0:T(8,128)(2,1)}, bf16[64,512]{1,0:T(8,128)(2,1)S(1)}, u32[]{:S(2)}, u32[]{:S(2)}) collective-permute-start(bf16[64,512]{1,0:T(8,128)(2,1)} %param.23), channel_id=1, source_target_pairs={{0,16},{16,0},{32,48},{48,32},{1,17},{17,1},{33,49},{49,33},{2,18}... | collective-permute-start | bytes 196616 | tf_op jit(solution)/shard_map/ppermute | solution.py:31
  38.4 75.8 %copy-start.4 = (s32[128]{0:T(128)S(1)}, s32[128]{0:T(128)}, u32[]{:S(2)}) copy-start(s32[128]{0:T(128)} %param.14) | copy-start | bytes 1540
  38.4 75.8 %copy-start.5 = (s32[128]{0:T(128)S(1)}, s32[128]{0:T(128)}, u32[]{:S(2)}) copy-start(s32[128]{0:T(128)} %param.13) | copy-start | bytes 1540
  38.5 75.8 %copy-start.6 = (s32[128]{0:T(128)S(1)}, s32[128]{0:T(128)}, u32[]{:S(2)}) copy-start(s32[128]{0:T(128)} %param.15) | copy-start | bytes 1540
  38.5 75.8 %copy-start.7 = (s32[128]{0:T(128)S(1)}, s32[128]{0:T(128)}, u32[]{:S(2)}) copy-start(s32[128]{0:T(128)} %param.16) | copy-start | bytes 1540
  38.5 75.9 %copy-start.8 = (f32[128]{0:T(128)S(1)}, f32[128]{0:T(128)}, u32[]{:S(2)}) copy-start(f32[128]{0:T(128)} %param.17) | copy-start | bytes 1540
  38.5 75.9 %copy-start.9 = (f32[128]{0:T(128)S(1)}, f32[128]{0:T(128)}, u32[]{:S(2)}) copy-start(f32[128]{0:T(128)} %param.18) | copy-start | bytes 1540
  38.5 84.3 %copy-start = (bf16[128,4096]{1,0:T(8,128)(2,1)S(1)}, bf16[128,4096]{1,0:T(8,128)(2,1)}, u32[]{:S(2)}) copy-start(bf16[128,4096]{1,0:T(8,128)(2,1)} %tokens_ref.1) | copy-start | bytes 3145732
  38.5 84.3 %copy-start.1 = (f32[4096]{0:T(1024)S(1)}, f32[4096]{0:T(1024)}, u32[]{:S(2)}) copy-start(f32[4096]{0:T(1024)} %param.22) | copy-start | bytes 49156
  39.7 27.9 %all-to-all-start.1 = ((bf16[8,24,1024]{2,1,0:T(8,128)(2,1)}), bf16[8,24,1024]{2,1,0:T(8,128)(2,1)S(1)}, u32[]{:S(2)}, u32[]{:S(2)}) async-start(bf16[8,24,1024]{2,1,0:T(8,128)(2,1)} %bitcast.4), calls=%async_computation.1 | async-start | bytes 786432 | tf_op jit(solution)/shard_map/all_to_all | solution.py:23
  54.3 68.5 %all-gather.2.cloned.1.call-start = ((), (), s32[]{:S(2)}) async-start(), calls=%async_computation.5 | async-start | bytes 4456448 | tf_op jit(solution)/shard_map/all_gather | solution.py:265
  54.4 14.0 %collective-permute-start.3 = (bf16[2,64,512]{2,1,0:T(8,128)(2,1)S(1)}, bf16[2,64,512]{2,1,0:T(8,128)(2,1)S(1)}, u32[]{:S(2)}, u32[]{:S(2)}) collective-permute-start(bf16[2,64,512]{2,1,0:T(8,128)(2,1)S(1)} %pad_maximum_fusion.2), channel_id=1, source_target_pairs={{0,32},{16,48},{32,0},{48,16},{1,33},{17,49},{33,1},{49,17},{2,34}... | collective-permute-start | bytes 393224 | tf_op jit(solution)/shard_map/ppermute | solution.py:31
  69.1 15.1 %all-to-all-start.2 = ((bf16[8,24,512]{2,1,0:T(8,128)(2,1)}), bf16[8,24,512]{2,1,0:T(8,128)(2,1)S(1)}, u32[]{:S(2)}, u32[]{:S(2)}) async-start(bf16[8,24,512]{2,1,0:T(8,128)(2,1)} %shard_map.133), calls=%async_computation.2 | async-start | bytes 393216 | tf_op jit(solution)/shard_map/all_to_all | solution.py:23
  74.5 10.0 %collective-permute-start.4 = (bf16[256,512]{1,0:T(8,128)(2,1)S(1)}, bf16[256,512]{1,0:T(8,128)(2,1)S(1)}, u32[]{:S(2)}, u32[]{:S(2)}) collective-permute-start(bf16[256,512]{1,0:T(8,128)(2,1)S(1)} %copy-done.2), channel_id=1, source_target_pairs={{0,1},{1,0},{2,3},{3,2},{4,5},{5,4},{6,7},{7,6},{8,9},{9,8},{10,11... | collective-permute-start | bytes 786440 | tf_op jit(solution)/shard_map/ppermute | solution.py:27
  110.7 12.0 %all-to-all-start.4 = ((bf16[16,8,512]{2,1,0:T(8,128)(2,1)}), bf16[16,8,512]{2,1,0:T(8,128)(2,1)S(1)}, u32[]{:S(2)}, u32[]{:S(2)}) async-start(bf16[16,8,512]{2,1,0:T(8,128)(2,1)} %shard_map.134), calls=%async_computation.4 | async-start | bytes 262144 | tf_op jit(solution)/shard_map/all_to_all | solution.py:23
Sparse Core Ops, SparseCore 0:
  69.2 46.8 all-gather.1
